TPU v7x, 32 devices: a whole 2x2x4 slice. The times are simulated.
32 devices in a mesh: dp: 8 (over z, x), tensor: 4 (over y, core).
Axes of the slice: x: 2, y: 2, z: 4, core: 2. Of those that a mesh axis runs over, the one named last changes fastest.
Arguments:
- resid_in: bfloat16 [4, 1024, 1024], P(None, ('dp', 'tensor')), may hold values from -6 to 6
- segment_ids: int32 [4, 1024], replicated, may hold values from 0 to 64, as said below
- out_grad: bfloat16 [4, 1024, 1024], P(None, ('dp', 'tensor')), may hold values from -6 to 6
- input_gain: float32 [1024], replicated, may hold values from 0.5 to 1.5
- ffn_gain: float32 [1024], replicated, may hold values from 0.5 to 1.5
- query_weight: bfloat16 [1024, 512], P('dp', 'tensor'), may hold values from -0.1875 to 0.1875
- keyvalue_weight: bfloat16 [1024, 2, 128], P('dp'), may hold values from -0.1875 to 0.1875
- attention_output_weight: bfloat16 [512, 1024], P('tensor', 'dp'), may hold values from -1 to 1
- mixer_input_weight: bfloat16 [1024, 2, 1536], P('dp', None, 'tensor'), may hold values from -0.1875 to 0.1875
- state_input_weight: bfloat16 [1024, 256], P('dp'), may hold values from -0.1875 to 0.1875
- step_weight: bfloat16 [1024, 24], P('dp', 'tensor'), may hold values from -0.1875 to 0.1875
- conv_mixer: float32 [4, 1536], P(None, 'tensor'), may hold values from -3 to 3
- conv_mixer_bias: float32 [1536], P('tensor'), may hold values from -2 to 2
- conv_state: float32 [4, 256], replicated, may hold values from -3 to 3
- conv_state_bias: float32 [256], replicated, may hold values from -2 to 2
- step_bias: float32 [24], P('tensor'), may hold values from -1.5 to 0.5
- decay_log: float32 [24], P('tensor'), may hold values from -12 to -2
- skip_gain: float32 [24], P('tensor'), may hold values from 0.5 to 1.5
- mixer_gain: float32 [1536], P('tensor'), may hold values from 0.5 to 1.5
- mixer_output_weight: bfloat16 [1536, 1024], P('tensor', 'dp'), may hold values from -0.15625 to 0.15625
- gate_up_weight: bfloat16 [1024, 2, 2048], P('dp', None, 'tensor'), may hold values from -0.1875 to 0.1875
- down_weight: bfloat16 [2048, 1024], P('tensor', 'dp'), may hold values from -0.125 to 0.125
Outputs:
- block_out: bfloat16 [4, 1024, 1024], P(None, ('dp', 'tensor'))
- resid_grad: float32 [4, 1024, 1024], P(None, ('dp', 'tensor'))
- input_gain_grad: float32 [1024], replicated
- ffn_gain_grad: float32 [1024], replicated
- w_query_grad: float32 [1024, 512], P('dp', 'tensor')
- w_keyval_grad: float32 [1024, 2, 128], P('dp')
- w_attn_out_grad: float32 [512, 1024], P('tensor', 'dp')
- w_mixer_in_grad: float32 [1024, 2, 1536], P('dp', None, 'tensor')
- w_state_in_grad: float32 [1024, 256], P('dp')
- w_step_grad: float32 [1024, 24], P('dp', 'tensor')
- conv_mixer_grad: float32 [4, 1536], P(None, 'tensor')
- conv_mixer_bias_grad: float32 [1536], P('tensor')
- conv_state_grad: float32 [4, 256], replicated
- conv_state_bias_grad: float32 [256], replicated
- step_bias_grad: float32 [24], P('tensor')
- decay_log_grad: float32 [24], P('tensor')
- skip_gain_grad: float32 [24], P('tensor')
- mixer_gain_grad: float32 [1536], P('tensor')
- w_mixer_out_grad: float32 [1536, 1024], P('tensor', 'dp')
- w_gate_up_grad: float32 [1024, 2, 2048], P('dp', None, 'tensor')
- w_down_grad: float32 [2048, 1024], P('tensor', 'dp')
Inputs may be any that keep to these rules, and one draw needn't show every extreme that they name: `segment_ids`: in each sequence the numbers start at 0 and rise by 0 or 1 from one token to the next; equal numbers mark one document. Some sequence is one document from its first token into its last 128 tokens, where 128 // 2 of those tokens each start a new document.
All inputs are finite; a program needn't handle non-finite values.
Results may differ from a plain program's by a relative error of at most 0.035.
Values may be sent and summed in bfloat16 or wider, within the bound.
A program may use at most 320 MiB of HBM per device.

v0:
```python
from functools import partial
import math

import jax
import jax.numpy as jnp
from jax import lax
from jax.sharding import PartitionSpec as P

KVH = 2


EPSILON = 1e-05
ROTARY_BASE = 100000000000.0
MASKED = -1e30
MATMUL_EXACTNESS = lax.Precision.HIGHEST


def as_sent(array):

    def short(part):
        return part.astype(jnp.bfloat16) if part.dtype == jnp.float32 else part

    return jax.tree.map(short, array)


def from_behind(array, axis, by):
    devices = lax.axis_size(axis)
    pairs = [(i, i + by) for i in range(devices) if 0 <= i + by < devices]
    return lax.ppermute(array, axis, pairs)


def prefix(array, axis, combine, identity):
    devices, mine = (lax.axis_size(axis), lax.axis_index(axis))
    everything = jax.tree.map(
        lambda part, kind: lax.all_gather(part.astype(kind), axis),
        array,
        (jnp.bfloat16, jnp.bfloat16),
    )
    start = jax.tree.map(
        lambda part, zero: jnp.broadcast_to(jnp.asarray(zero, part.dtype), part.shape),
        array,
        identity,
    )

    def turn(k, before):
        reached = k < mine
        new = combine(
            before, jax.tree.map(lambda part, own: part[k].astype(own.dtype), everything, array)
        )
        return jax.tree.map(lambda a, b: jnp.where(reached, a, b), new, before)

    return lax.fori_loop(0, devices, turn, start)


def carried_in(array, axis, join, neutral):
    count = lax.axis_size(axis)
    place = lax.axis_index(axis)
    ahead = count - 1 - place
    gathered = jax.tree.map(
        lambda a, kind: lax.all_gather(a.astype(kind), axis),
        array,
        jax.tree.map(lambda a: jnp.bfloat16 if a.dtype == jnp.float32 else a.dtype, array),
    )
    state = jax.tree.map(lambda a, e: jnp.zeros_like(a) + jnp.asarray(e, a.dtype), array, neutral)

    def one(turn, state):
        source = count - 1 - turn
        return join(
            state,
            jax.tree.map(
                lambda a, own: lax.dynamic_index_in_dim(a, source, 0, False).astype(own.dtype),
                gathered,
                array,
            ),
        )

    return lax.fori_loop(0, ahead, one, state)


def rotate(tensor, positions, sign):
    half_dim = tensor.shape[-1] // 2
    frequency = jnp.exp(
        -math.log(ROTARY_BASE) * 2.0 * jnp.arange(half_dim, dtype=jnp.float32) / tensor.shape[-1]
    )
    angle = positions[:, None] * frequency[None, :]
    cosine = jnp.cos(angle)[None, :, None, :]
    sine = sign * jnp.sin(angle)[None, :, None, :]
    first_half = tensor[..., :half_dim]
    second_half = tensor[..., half_dim:]
    return jnp.concatenate(
        [first_half * cosine - second_half * sine, second_half * cosine + first_half * sine], -1
    )


def rms_norm(values, gain):
    return values * lax.rsqrt(jnp.mean(values * values, -1, keepdims=True) + EPSILON) * gain


def conv_apply(extended, weight, bias, seg_ext, seg_span):
    length = seg_span.shape[1]
    summed = bias
    for tap_index in range(weight.shape[0]):
        same_doc = (seg_ext[:, tap_index : tap_index + length] == seg_span).astype(extended.dtype)
        summed = (
            summed
            + weight[tap_index] * extended[:, tap_index : tap_index + length] * same_doc[..., None]
        )
    return jax.nn.silu(summed)


def state_inner(x_heads, step_size, input_heads, output_heads, decay_rate, seg_span, seg_prev):
    cumulative = jnp.cumsum(step_size * decay_rate, axis=1)
    position = jnp.arange(seg_span.shape[1])
    same_doc = (seg_span[:, :, None] == seg_span[:, None, :]) & (
        position[:, None] >= position[None, :]
    )[None]
    allowed = same_doc[..., None]
    gap_log = cumulative[:, :, None, :] - cumulative[:, None, :, :]
    decay_weight = jnp.where(allowed, jnp.exp(jnp.where(allowed, gap_log, 0.0)), 0.0)
    intersection = jnp.einsum(
        "sthn,sjhn->stjh", output_heads, input_heads, precision=MATMUL_EXACTNESS
    )
    inner_y = jnp.einsum(
        "stjh,sjh,sjhe->sthe",
        intersection * decay_weight,
        step_size,
        x_heads,
        precision=MATMUL_EXACTNESS,
    )
    last_seg = seg_span[:, -1]
    tail_weight = jnp.where(
        (seg_span == last_seg[:, None])[..., None], jnp.exp(cumulative[:, -1:, :] - cumulative), 0.0
    )
    state_local = jnp.einsum(
        "sjh,sjhe,sjhn->shen",
        tail_weight * step_size,
        x_heads,
        input_heads,
        precision=MATMUL_EXACTNESS,
    )
    carried = (
        jnp.exp(cumulative[:, -1, :]) * (last_seg == seg_prev).astype(cumulative.dtype)[:, None]
    )
    return (inner_y, carried, state_local)


def state_cross(output_heads, step_size, decay_rate, seg_span, seg_prev, state_in):
    cumulative = jnp.cumsum(step_size * decay_rate, axis=1)
    keep_prior = (seg_span == seg_prev[:, None]).astype(cumulative.dtype)[..., None]
    return (
        jnp.einsum("sthn,shen->sthe", output_heads, state_in, precision=MATMUL_EXACTNESS)
        * (jnp.exp(cumulative) * keep_prior)[..., None]
    )


def combine_states(earlier, later):
    return (earlier[0] * later[0], later[0][:, :, None, None] * earlier[1] + later[1])


def body(
    resid_in,
    segment_ids,
    out_grad,
    input_gain,
    ffn_gain,
    query_weight,
    keyvalue_weight,
    attention_output_weight,
    mixer_input_weight,
    state_input_weight,
    step_weight,
    conv_mixer,
    conv_mixer_bias,
    conv_state,
    conv_state_bias,
    step_bias,
    decay_log,
    skip_gain,
    mixer_gain,
    mixer_output_weight,
    gate_up_weight,
    down_weight,
):
    tensor_count = lax.axis_size("tensor")
    shard_count = lax.axis_size("dp")
    tensor_rank = lax.axis_index("tensor")
    shard_rank = lax.axis_index("dp")
    sequences, sub_rows, model_width = resid_in.shape
    span_rows = sub_rows * tensor_count
    head_dim = keyvalue_weight.shape[2] // 2
    query_width = query_weight.shape[1]
    local_heads = query_width // head_dim
    mixer_local = step_weight.shape[1]
    mixer_width = conv_mixer.shape[1]
    mixer_total = mixer_width * tensor_count
    mixer_dim = mixer_width // mixer_local
    state_dim = state_input_weight.shape[1] // 2
    edge_rows = conv_mixer.shape[0] - 1
    scale = 1.0 / math.sqrt(head_dim)
    gathered = (
        lax.all_gather(query_weight, "dp", axis=0, tiled=True),
        lax.all_gather(keyvalue_weight, "dp", axis=0, tiled=True),
        lax.all_gather(attention_output_weight, "dp", axis=1, tiled=True),
        lax.all_gather(mixer_input_weight, "dp", axis=0, tiled=True),
        lax.all_gather(state_input_weight, "dp", axis=0, tiled=True),
        lax.all_gather(step_weight, "dp", axis=0, tiled=True),
        lax.all_gather(mixer_output_weight, "dp", axis=1, tiled=True),
        lax.all_gather(gate_up_weight, "dp", axis=0, tiled=True),
        lax.all_gather(down_weight, "dp", axis=1, tiled=True),
    )
    (
        gathered_query_weight,
        full_keyval,
        gathered_attention_weight,
        gathered_mixer_input_weight,
        gathered_state_input_weight,
        gathered_step_weight,
        gathered_mixer_output_weight,
        gathered_gate_up_weight,
        gathered_down_weight,
    ) = gathered
    keyval_index = tensor_rank * KVH // tensor_count
    keyvalue_local = lax.dynamic_index_in_dim(full_keyval, keyval_index, 1, keepdims=False)
    first_row = shard_rank * span_rows
    query_pos = first_row + jnp.arange(span_rows, dtype=jnp.int32)
    positions = query_pos.astype(jnp.float32)
    seg_span = lax.dynamic_slice_in_dim(segment_ids, first_row, span_rows, 1)
    seg_padded = jnp.pad(segment_ids, ((0, 0), (edge_rows, 0)), constant_values=-1)
    seg_ext = lax.dynamic_slice_in_dim(seg_padded, first_row, span_rows + edge_rows, 1)
    seg_prev = seg_ext[:, edge_rows - 1]

    def gather_rows(shard_rows):
        return lax.all_gather(shard_rows, "tensor", axis=1, tiled=True)

    def sum_rows(partial_rows):
        return lax.psum_scatter(
            partial_rows.astype(jnp.bfloat16), "tensor", scatter_dimension=1, tiled=True
        ).astype(jnp.float32)

    def tensor_total(partial_value):
        return jax.tree.map(
            lambda part: part.astype(jnp.float32), lax.psum(as_sent(partial_value), "tensor")
        )

    def over_keys(packed_keys, fold_step, initial):
        return fold_step(
            initial, lax.all_gather(packed_keys, "dp", axis=1, tiled=True), jnp.int32(0)
        )

    def key_allowed(key_count):
        key_pos = jnp.arange(key_count, dtype=jnp.int32)
        causal = (key_pos[None, :] <= query_pos[:, None])[None, None]
        return causal & (seg_span[:, None, :, None] == segment_ids[:, None, None, :])

    x_float = resid_in.astype(jnp.float32)
    normed_input = rms_norm(x_float, input_gain).astype(jnp.bfloat16)
    span_normed_input = gather_rows(normed_input)
    query_projected = jnp.einsum(
        "mbn,nf->mbf", span_normed_input, gathered_query_weight, preferred_element_type=jnp.float32
    )
    keyvalue_projected = jnp.einsum(
        "mbn,nf->mbf", span_normed_input, keyvalue_local, preferred_element_type=jnp.float32
    )
    queries = rotate(
        query_projected.reshape(sequences, span_rows, local_heads, head_dim), positions, 1.0
    ).astype(jnp.bfloat16)
    keys_own = rotate(keyvalue_projected[:, :, None, :head_dim], positions, 1.0)[:, :, 0].astype(
        jnp.bfloat16
    )
    values_own = keyvalue_projected[:, :, head_dim:].astype(jnp.bfloat16)
    packed = jnp.concatenate([keys_own, values_own], -1)

    def forward_fold(state_carry, shard_piece, key_first):
        running_max, running_sum, accumulated = state_carry
        key_count = shard_piece.shape[1]
        scores = (
            jnp.einsum(
                "sqhe,ske->shqk",
                queries,
                shard_piece[:, :, :head_dim],
                preferred_element_type=jnp.float32,
            )
            * scale
        )
        allowed = key_allowed(key_count)
        new_max = jnp.maximum(running_max, jnp.max(jnp.where(allowed, scores, MASKED), -1))
        exp_scores = jnp.where(allowed, jnp.exp(scores - new_max[..., None]), 0.0)
        running_sum = jnp.sum(exp_scores, -1)
        accumulated = jnp.einsum(
            "shqk,ske->shqe",
            exp_scores.astype(jnp.bfloat16),
            shard_piece[:, :, head_dim:],
            preferred_element_type=jnp.float32,
        )
        return (new_max, running_sum, accumulated)

    start_fold = (
        jnp.full((sequences, local_heads, span_rows), MASKED, jnp.float32),
        jnp.zeros((sequences, local_heads, span_rows), jnp.float32),
        jnp.zeros((sequences, local_heads, span_rows, head_dim), jnp.float32),
    )
    final_max, final_sum, final_acc = over_keys(packed, forward_fold, start_fold)
    log_total = final_max + jnp.log(final_sum)
    attention_out = final_acc / final_sum[..., None]
    attention_rows = jnp.transpose(attention_out, (0, 2, 1, 3))
    attention_reduced = attention_rows.reshape(sequences, span_rows, query_width).astype(
        jnp.bfloat16
    )
    attn_part = jnp.einsum(
        "uqn,nh->uqh",
        attention_reduced,
        gathered_attention_weight,
        preferred_element_type=jnp.float32,
    )
    mixed_rows = jnp.einsum(
        "uxo,ofw->uxfw",
        span_normed_input,
        gathered_mixer_input_weight,
        preferred_element_type=jnp.float32,
    ).astype(jnp.bfloat16)
    gate_z = mixed_rows[:, :, 0]
    mixer_x = mixed_rows[:, :, 1]
    state_projected = jnp.einsum(
        "mbn,nf->mbf",
        span_normed_input,
        gathered_state_input_weight,
        preferred_element_type=jnp.float32,
    ).astype(jnp.bfloat16)
    step_unactivated = jnp.einsum(
        "qji,ig->qjg", span_normed_input, gathered_step_weight, preferred_element_type=jnp.float32
    )
    edge_x, edge_state = from_behind(
        (mixer_x[:, span_rows - edge_rows :], state_projected[:, span_rows - edge_rows :]), "dp", 1
    )
    ext_x = jnp.concatenate([edge_x, mixer_x], 1).astype(jnp.float32)
    ext_state = jnp.concatenate([edge_state, state_projected], 1).astype(jnp.float32)
    conv_x_fn = partial(conv_apply, seg_ext=seg_ext, seg_span=seg_span)
    conv_x = conv_x_fn(ext_x, conv_mixer, conv_mixer_bias)
    conv_bc = conv_x_fn(ext_state, conv_state, conv_state_bias)
    step_pre = step_unactivated + step_bias
    step_size = jax.nn.softplus(step_pre)
    decay_rate = -jnp.exp(decay_log)
    x_heads = conv_x.reshape(sequences, span_rows, mixer_local, mixer_dim)
    head_shape = (sequences, span_rows, mixer_local, state_dim)

    def intra_fn(x_value, step_value, bc_value, decay_value):
        input_heads = jnp.broadcast_to(bc_value[:, :, None, :state_dim], head_shape)
        output_heads = jnp.broadcast_to(bc_value[:, :, None, state_dim:], head_shape)
        return state_inner(
            x_value, step_value, input_heads, output_heads, decay_value, seg_span, seg_prev
        )

    def cross_fn(bc_value, step_value, decay_value, prior_value):
        output_heads = jnp.broadcast_to(bc_value[:, :, None, state_dim:], head_shape)
        return state_cross(output_heads, step_value, decay_value, seg_span, seg_prev, prior_value)

    inner_y, carry_local, state_local = intra_fn(x_heads, step_size, conv_bc, decay_rate)
    scan_identity = (jnp.ones_like(carry_local), jnp.zeros_like(state_local))
    prior_carry, state_prior = prefix(
        (carry_local, state_local), "dp", combine_states, scan_identity
    )
    cross_y = cross_fn(conv_bc, step_size, decay_rate, state_prior)
    mixer_y = (inner_y + cross_y + skip_gain[:, None] * x_heads).reshape(
        sequences, span_rows, mixer_width
    )
    gate_float = gate_z.astype(jnp.float32)
    gate_sigmoid = jax.nn.sigmoid(gate_float)
    gated = mixer_y * (gate_float * gate_sigmoid)
    square_total = tensor_total(jnp.sum(gated * gated, -1, keepdims=True))
    norm_scale = lax.rsqrt(square_total / mixer_total + EPSILON)
    mixer_normed_input = (gated * norm_scale * mixer_gain).astype(jnp.bfloat16)
    mixer_part = jnp.einsum(
        "uqn,nh->uqh",
        mixer_normed_input,
        gathered_mixer_output_weight,
        preferred_element_type=jnp.float32,
    )
    branch_output = sum_rows(attn_part + mixer_part)
    hidden_rows = x_float + branch_output
    normed_feedforward = rms_norm(hidden_rows, ffn_gain).astype(jnp.bfloat16)
    span_feedforward = gather_rows(normed_feedforward)
    gate_up_rows = jnp.einsum(
        "pjn,nrt->pjrt",
        span_feedforward,
        gathered_gate_up_weight,
        preferred_element_type=jnp.float32,
    )
    gate_value = gate_up_rows[:, :, 0]
    up_value = gate_up_rows[:, :, 1]
    sigmoid_gate = jax.nn.sigmoid(gate_value)
    swiglu_activated = (gate_value * sigmoid_gate * up_value).astype(jnp.bfloat16)
    ffn_out = sum_rows(
        jnp.einsum(
            "axt,tz->axz",
            swiglu_activated,
            gathered_down_weight,
            preferred_element_type=jnp.float32,
        )
    )
    block_out = (hidden_rows + ffn_out).astype(jnp.bfloat16)
    grad_out = out_grad.astype(jnp.float32)
    span_gradient = gather_rows(out_grad)
    activation_gradient = jnp.einsum(
        "ikm,nm->ikn", span_gradient, gathered_down_weight, preferred_element_type=jnp.float32
    )
    down_gradient = jnp.einsum(
        "ukz,ukt->zt", swiglu_activated, span_gradient, preferred_element_type=jnp.float32
    )
    grad_gate = (
        activation_gradient * up_value * sigmoid_gate * (1.0 + gate_value * (1.0 - sigmoid_gate))
    )
    grad_up = activation_gradient * gate_value * sigmoid_gate
    gate_up_gradient = jnp.stack([grad_gate, grad_up], 2).astype(jnp.bfloat16)
    grad_gate_up_w = jnp.einsum(
        "wbm,wbpe->mpe", span_feedforward, gate_up_gradient, preferred_element_type=jnp.float32
    )
    grad_normed_ffn = sum_rows(
        jnp.einsum(
            "xirp,zrp->xiz",
            gate_up_gradient,
            gathered_gate_up_weight,
            preferred_element_type=jnp.float32,
        )
    )
    _, ffn_pull = jax.vjp(rms_norm, hidden_rows, ffn_gain)
    grad_hidden_norm, grad_ffn_gain = ffn_pull(grad_normed_ffn)
    grad_hidden = grad_out + grad_hidden_norm
    span_branch_output = gather_rows(grad_hidden.astype(jnp.bfloat16))
    grad_attention = jnp.einsum(
        "irh,yh->iry",
        span_branch_output,
        gathered_attention_weight,
        preferred_element_type=jnp.float32,
    )
    grad_attn_out = jnp.einsum(
        "nyu,nyb->ub", attention_reduced, span_branch_output, preferred_element_type=jnp.float32
    )
    grad_mixer_norm = jnp.einsum(
        "irh,yh->iry",
        span_branch_output,
        gathered_mixer_output_weight,
        preferred_element_type=jnp.float32,
    )
    grad_mixer_out = jnp.einsum(
        "nyu,nyb->ub", mixer_normed_input, span_branch_output, preferred_element_type=jnp.float32
    )
    grad_attn_low = grad_attention.reshape(sequences, span_rows, local_heads, head_dim).astype(
        jnp.bfloat16
    )
    delta = jnp.transpose(
        jnp.sum(grad_attn_low.astype(jnp.float32) * attention_rows, -1), (0, 2, 1)
    )
    query_zero = jnp.zeros((sequences, local_heads, span_rows, head_dim), jnp.float32)

    def backward_fold(state_carry, shard_piece, key_first):
        key_count = shard_piece.shape[1]
        keys_piece = shard_piece[:, :, :head_dim]
        scores = (
            jnp.einsum("sqhe,ske->shqk", queries, keys_piece, preferred_element_type=jnp.float32)
            * scale
        )
        allowed = key_allowed(key_count)
        exp_scores = jnp.where(allowed, jnp.exp(scores - log_total[..., None]), 0.0)
        grad_probs = jnp.einsum(
            "sqhe,ske->shqk",
            grad_attn_low,
            shard_piece[:, :, head_dim:],
            preferred_element_type=jnp.float32,
        )
        grad_scores = (exp_scores * (grad_probs - delta[..., None])).astype(jnp.bfloat16)
        grad_query = (
            jnp.einsum(
                "shqk,ske->shqe", grad_scores, keys_piece, preferred_element_type=jnp.float32
            )
            * scale
        )
        grad_key_piece = (
            jnp.einsum("shqk,sqhe->ske", grad_scores, queries, preferred_element_type=jnp.float32)
            * scale
        )
        grad_value_piece = jnp.einsum(
            "shqk,sqhe->ske",
            exp_scores.astype(jnp.bfloat16),
            grad_attn_low,
            preferred_element_type=jnp.float32,
        )
        updated = jnp.concatenate([grad_key_piece, grad_value_piece], -1)
        return (grad_query, updated)

    keys_zero = jnp.zeros((sequences, span_rows * shard_count, 2 * head_dim), jnp.float32)
    grad_query, grad_keys_all = over_keys(packed, backward_fold, (query_zero, keys_zero))
    grad_keyval = lax.psum_scatter(grad_keys_all, "dp", scatter_dimension=1, tiled=True)
    query_projected_gradient = (
        rotate(jnp.transpose(grad_query, (0, 2, 1, 3)), positions, -1.0)
        .reshape(sequences, span_rows, query_width)
        .astype(jnp.bfloat16)
    )
    grad_key_pre = rotate(grad_keyval[:, :, None, :head_dim], positions, -1.0)[:, :, 0]
    keyvalue_reduced_gradient = jnp.concatenate(
        [grad_key_pre, grad_keyval[:, :, head_dim:]], -1
    ).astype(jnp.bfloat16)
    gain_term = grad_mixer_norm * mixer_gain
    grad_mixer_gain = jnp.sum(grad_mixer_norm * gated * norm_scale, (0, 1))
    inner_total = tensor_total(jnp.sum(gated * gain_term, -1, keepdims=True))
    grad_gated = norm_scale * (
        gain_term - gated * norm_scale * norm_scale * inner_total / mixer_total
    )
    grad_mixer_y = grad_gated * (gate_float * gate_sigmoid)
    grad_gate_z = grad_gated * mixer_y * gate_sigmoid * (1.0 + gate_float * (1.0 - gate_sigmoid))
    grad_y_heads = grad_mixer_y.reshape(sequences, span_rows, mixer_local, mixer_dim)
    grad_skip = jnp.sum(grad_y_heads * x_heads, (0, 1, 3))
    _, cross_pull = jax.vjp(cross_fn, conv_bc, step_size, decay_rate, state_prior)
    grad_bc_cross, grad_step_cross, grad_decay_cross, grad_prior = cross_pull(grad_y_heads)
    later_carry, grad_after = carried_in(
        (carry_local, grad_prior), "dp", combine_states, scan_identity
    )
    grad_carry = jnp.sum(grad_after * state_prior, (2, 3))
    _, intra_pull = jax.vjp(intra_fn, x_heads, step_size, conv_bc, decay_rate)
    grad_x_intra, grad_step_intra, grad_bc_intra, grad_decay_intra = intra_pull(
        (grad_y_heads, grad_carry, grad_after)
    )
    grad_conv_x = (grad_x_intra + skip_gain[:, None] * grad_y_heads).reshape(
        sequences, span_rows, mixer_width
    )
    grad_conv_bc = grad_bc_intra + grad_bc_cross
    grad_step_pre = (grad_step_intra + grad_step_cross) * jax.nn.sigmoid(step_pre)
    grad_step_bias = jnp.sum(grad_step_pre, (0, 1))
    grad_decay_log = (grad_decay_intra + grad_decay_cross) * decay_rate
    step_reduced_gradient = grad_step_pre.astype(jnp.bfloat16)
    _, conv_x_pull = jax.vjp(conv_x_fn, ext_x, conv_mixer, conv_mixer_bias)
    grad_ext_x, grad_conv_w, grad_conv_b = conv_x_pull(grad_conv_x)
    _, conv_bc_pull = jax.vjp(conv_x_fn, ext_state, conv_state, conv_state_bias)
    grad_ext_state, grad_state_w, grad_state_b = conv_bc_pull(grad_conv_bc)
    back_x, back_state = (
        from_behind(grad_ext_x[:, :edge_rows].astype(jnp.bfloat16), "dp", -1).astype(jnp.float32),
        from_behind(grad_ext_state[:, :edge_rows].astype(jnp.bfloat16), "dp", -1).astype(
            jnp.float32
        ),
    )
    tail_pad = ((0, 0), (span_rows - edge_rows, 0), (0, 0))
    grad_mixer_x = grad_ext_x[:, edge_rows:] + jnp.pad(back_x, tail_pad)
    grad_state_pre = grad_ext_state[:, edge_rows:] + jnp.pad(back_state, tail_pad)
    mixed_gradient = jnp.stack([grad_gate_z, grad_mixer_x], 2).astype(jnp.bfloat16)
    state_reduced_gradient = grad_state_pre.astype(jnp.bfloat16)
    grad_rows_part = jnp.einsum(
        "fvp,jp->fvj",
        query_projected_gradient,
        gathered_query_weight,
        preferred_element_type=jnp.float32,
    )
    grad_rows_part = grad_rows_part + jnp.einsum(
        "fvp,jp->fvj", keyvalue_reduced_gradient, keyvalue_local, preferred_element_type=jnp.float32
    )
    grad_rows_part = grad_rows_part + jnp.einsum(
        "ofgk,ugk->ofu",
        mixed_gradient,
        gathered_mixer_input_weight,
        preferred_element_type=jnp.float32,
    )
    grad_rows_part = grad_rows_part + jnp.einsum(
        "fvp,jp->fvj",
        state_reduced_gradient,
        gathered_state_input_weight,
        preferred_element_type=jnp.float32,
    )
    grad_rows_part = grad_rows_part + jnp.einsum(
        "bmo,eo->bme",
        step_reduced_gradient,
        gathered_step_weight,
        preferred_element_type=jnp.float32,
    )
    grad_normed = sum_rows(grad_rows_part)
    _, input_pull = jax.vjp(rms_norm, x_float, input_gain)
    grad_x_norm, grad_input_gain = input_pull(grad_normed)
    resid_grad = grad_hidden + grad_x_norm
    grad_query_w = jnp.einsum(
        "frh,frp->hp",
        span_normed_input,
        query_projected_gradient,
        preferred_element_type=jnp.float32,
    )
    grad_keyval_own = jnp.einsum(
        "frh,frp->hp",
        span_normed_input,
        keyvalue_reduced_gradient,
        preferred_element_type=jnp.float32,
    )
    grad_mixer_in = jnp.einsum(
        "iqf,iqyj->fyj", span_normed_input, mixed_gradient, preferred_element_type=jnp.float32
    )
    grad_state_in = jnp.einsum(
        "frh,frp->hp", span_normed_input, state_reduced_gradient, preferred_element_type=jnp.float32
    )
    grad_step_w = jnp.einsum(
        "njq,njb->qb", span_normed_input, step_reduced_gradient, preferred_element_type=jnp.float32
    )
    keyval_full = lax.dynamic_update_index_in_dim(
        jnp.zeros(full_keyval.shape, jnp.float32), grad_keyval_own, keyval_index, 1
    )
    shard_grads = (
        lax.psum_scatter(grad_query_w, "dp", scatter_dimension=0, tiled=True),
        lax.psum_scatter(grad_attn_out, "dp", scatter_dimension=1, tiled=True),
        lax.psum_scatter(grad_mixer_in, "dp", scatter_dimension=0, tiled=True),
        lax.psum_scatter(grad_step_w, "dp", scatter_dimension=0, tiled=True),
        lax.psum_scatter(grad_mixer_out, "dp", scatter_dimension=1, tiled=True),
        lax.psum_scatter(grad_gate_up_w, "dp", scatter_dimension=0, tiled=True),
        lax.psum_scatter(down_gradient, "dp", scatter_dimension=1, tiled=True),
        lax.psum_scatter(keyval_full, "dp", scatter_dimension=0, tiled=True),
        lax.psum_scatter(grad_state_in, "dp", scatter_dimension=0, tiled=True),
    )
    keyval_rows, state_rows = tensor_total((shard_grads[7], shard_grads[8]))

    def placed(local_value, axis_number):
        full_shape = list(local_value.shape)
        full_shape[axis_number] = full_shape[axis_number] * tensor_count
        start_index = tensor_rank * local_value.shape[axis_number]
        return lax.dynamic_update_slice_in_dim(
            jnp.zeros(full_shape, jnp.float32), local_value, start_index, axis_number
        )

    def take_slot(full_value, axis_number, piece_size):
        return lax.dynamic_slice_in_dim(
            full_value, tensor_rank * piece_size, piece_size, axis_number
        )

    summed = lax.psum(
        (
            grad_input_gain,
            grad_ffn_gain,
            placed(grad_conv_w, 1),
            placed(grad_conv_b, 0),
            placed(grad_step_bias, 0),
            placed(grad_decay_log, 0),
            placed(grad_skip, 0),
            placed(grad_mixer_gain, 0),
            grad_state_w,
            grad_state_b,
        ),
        ("dp", "tensor"),
    )
    return (
        block_out,
        resid_grad,
        summed[0],
        summed[1],
        shard_grads[0],
        keyval_rows,
        shard_grads[1],
        shard_grads[2],
        state_rows,
        shard_grads[3],
        take_slot(summed[2], 1, mixer_width),
        take_slot(summed[3], 0, mixer_width),
        summed[8],
        summed[9],
        take_slot(summed[4], 0, mixer_local),
        take_slot(summed[5], 0, mixer_local),
        take_slot(summed[6], 0, mixer_local),
        take_slot(summed[7], 0, mixer_width),
        shard_grads[4],
        shard_grads[5],
        shard_grads[6],
    )


def solution(mesh):
    placed = (
        P(None, ("dp", "tensor"), None),
        P(),
        P(None, ("dp", "tensor"), None),
        P(),
        P(),
        P("dp", "tensor"),
        P("dp", None, None),
        P("tensor", "dp"),
        P("dp", None, "tensor"),
        P("dp", None),
        P("dp", "tensor"),
        P(None, "tensor"),
        P("tensor"),
        P(),
        P(),
        P("tensor"),
        P("tensor"),
        P("tensor"),
        P("tensor"),
        P("tensor", "dp"),
        P("dp", None, "tensor"),
        P("tensor", "dp"),
    )
    return jax.shard_map(
        body,
        mesh=mesh,
        in_specs=placed,
        out_specs=(
            P(None, ("dp", "tensor"), None),
            P(None, ("dp", "tensor"), None),
            P(),
            P(),
            P("dp", "tensor"),
            P("dp", None, None),
            P("tensor", "dp"),
            P("dp", None, "tensor"),
            P("dp", None),
            P("dp", "tensor"),
            P(None, "tensor"),
            P("tensor"),
            P(),
            P(),
            P("tensor"),
            P("tensor"),
            P("tensor"),
            P("tensor"),
            P("tensor", "dp"),
            P("dp", None, "tensor"),
            P("tensor", "dp"),
        ),
        check_vma=False,
    )
```

profile of v0, /device:TPU:0, one launch (start us, length us, event | category | flops | bytes accessed | tf_op | source)
XLA Modules:
  0.0 1336.7 jit_solution(5573336877972915375)
XLA Ops:
  17.0 34.0 %all_gather.62 = bf16[1024,2,128]{2,1,0:T(2,128)(2,1)S(1)} all-gather(bf16[128,2,128]{2,1,0:T(2,128)(2,1)} %param.32), channel_id=1, replica_groups=mesh['dp'=8,'tensor'=4] {'dp'}, dimensions={0}, use_global_device_ids=true | all-gather | bytes 589824 | tf_op jit(solution)/shard_map/all_gather | solution.py:202
  52.0 26.1 %all_gather.66 = bf16[1024,6]{0,1:T(8,128)(2,1)S(1)} all-gather(bf16[128,6]{0,1:T(8,128)(2,1)S(1)} %copy-done.141), channel_id=1, replica_groups=mesh['dp'=8,'tensor'=4] {'dp'}, dimensions={0}, use_global_device_ids=true | all-gather | bytes 13824 | tf_op jit(solution)/shard_map/all_gather | solution.py:206
  79.1 31.4 %all_gather.68 = bf16[1024,256]{1,0:T(8,128)(2,1)S(1)} all-gather(bf16[128,256]{1,0:T(8,128)(2,1)S(1)} %copy-done.85), channel_id=1, replica_groups=mesh['dp'=8,'tensor'=4] {'dp'}, dimensions={0}, use_global_device_ids=true | all-gather | bytes 589824 | tf_op jit(solution)/shard_map/all_gather | solution.py:205
  135.5 30.9 %all_gather.64 = bf16[1024,128]{0,1:T(8,128)(2,1)} all-gather(bf16[128,128]{0,1:T(8,128)(2,1)} %copy.202), channel_id=1, replica_groups=mesh['dp'=8,'tensor'=4] {'dp'}, dimensions={0}, use_global_device_ids=true | all-gather | bytes 294912 | tf_op jit(solution)/shard_map/all_gather | solution.py:201
  166.5 29.0 %all_gather.65 = bf16[128,1024]{1,0:T(8,128)(2,1)} all-gather(bf16[128,128]{1,0:T(8,128)(2,1)} %param.33), channel_id=1, replica_groups=mesh['dp'=8,'tensor'=4] {'dp'}, dimensions={1}, use_global_device_ids=true | all-gather | bytes 294912 | tf_op jit(solution)/shard_map/all_gather | solution.py:203
  200.3 35.0 %all_gather.72 = bf16[384,1024]{1,0:T(8,128)(2,1)} all-gather(bf16[384,128]{1,0:T(8,128)(2,1)} %param.45), channel_id=1, replica_groups=mesh['dp'=8,'tensor'=4] {'dp'}, dimensions={1}, use_global_device_ids=true | all-gather | bytes 884736 | tf_op jit(solution)/shard_map/all_gather | solution.py:207
  238.0 19.6 %all_gather.69 = bf16[8,4,6]{2,1,0:T(4,128)(2,1)} all-gather(bf16[1,4,6]{2,1,0:T(4,128)(2,1)S(1)} %fusion.165), channel_id=1, replica_groups=mesh['dp'=8,'tensor'=4] {'dp'}, dimensions={0}, use_global_device_ids=true | all-gather | bytes 432 | tf_op jit(solution)/shard_map/all_gather | solution.py:35
  260.7 5.5 fusion.86
  276.2 14.9 %while.29 = (s32[]{:T(128)}, f32[4,6,64,128]{3,2,1,0:T(8,128)S(1)}, s32[]{:T(128)}, bf16[8,4,6]{2,1,0:T(4,128)(2,1)}, bf16[8,4,6,64,128]{4,3,2,1,0:T(8,128)(2,1)}, /*index=5*/s32[]{:T(128)}, s32[]{:T(128)}) while((s32[]{:T(128)}, f32[4,6,64,128]{3,2,1,0:T(8,128)S(1)}, s32[]{:T(128)}, bf16[8,4,6]{2,1,0:T(4,128)(2,1)}, ...), condition=%wide.region_5.6_spmd.clone, body=%wide.region_4.5_spmd.clone.sunk | while | flops 983068 | bytes 1966433 | solution.py:52
  294.3 4.8 multiply_reduce_fusion.11
  299.1 5.6 psum.98
  306.2 4.1 add_convert_fusion
  312.1 20.3 %reduce-scatter.14.cloned.1.call-done = bf16[4,32,1024]{2,1,0:T(8,128)(2,1)} async-done(((bf16[4,128,1024]{2,1,0:T(8,128)(2,1)}), bf16[4,32,1024]{2,1,0:T(8,128)(2,1)}) %reduce-scatter.14.cloned.1.call-update) | async-done | bytes 262160 | tf_op jit(solution)/shard_map/reduce_scatter | solution.py:236
  337.3 47.3 %all-gather.21.cloned.1.call-done = bf16[1024,2,512]{2,0,1:T(8,128)(2,1)} async-done(((bf16[128,2,512]{2,0,1:T(8,128)(2,1)}), bf16[1024,2,512]{2,0,1:T(8,128)(2,1)}) %all-gather.21.cloned.1.call-update) | async-done | bytes 2097168 | tf_op jit(solution)/shard_map/all_gather | solution.py:208
  384.5 17.5 %all-gather.19.cloned.1.call-done = bf16[4,128,1024]{2,1,0:T(8,128)(2,1)} async-done(((bf16[4,32,1024]{2,1,0:T(8,128)(2,1)}), bf16[4,128,1024]{2,1,0:T(8,128)(2,1)}) %all-gather.19.cloned.1.call-update) | async-done | bytes 1048592 | tf_op jit(solution)/shard_map/all_gather | solution.py:233
  402.0 4.6 fusion.16
  406.6 13.8 %all-gather.25.cloned.1.call-done = bf16[4,128,1024]{2,1,0:T(8,128)(2,1)} async-done(((bf16[4,32,1024]{2,1,0:T(8,128)(2,1)}), bf16[4,128,1024]{2,1,0:T(8,128)(2,1)}) %all-gather.25.cloned.1.call-update) | async-done | bytes 1048592 | tf_op jit(solution)/shard_map/all_gather | solution.py:233
  420.4 41.8 %all-gather.23.cloned.1.call-done = bf16[512,1024]{1,0:T(8,128)(2,1)} async-done(((bf16[512,128]{1,0:T(8,128)(2,1)}), bf16[512,1024]{1,0:T(8,128)(2,1)}) %all-gather.23.cloned.1.call-update) | async-done | bytes 1048592 | tf_op jit(solution)/shard_map/all_gather | solution.py:209
  462.2 4.3 fusion.124
  469.8 23.9 %reduce-scatter.18.cloned.1.call-done = bf16[4,32,1024]{2,1,0:T(8,128)(2,1)} async-done(((bf16[4,128,1024]{2,1,0:T(8,128)(2,1)}), bf16[4,32,1024]{2,1,0:T(8,128)(2,1)}) %reduce-scatter.18.cloned.1.call-update) | async-done | bytes 262160 | tf_op jit(solution)/shard_map/reduce_scatter | solution.py:236
  497.4 16.8 %all-gather.27.cloned.1.call-done = bf16[4,128,1024]{2,1,0:T(8,128)(2,1)} async-done(((bf16[4,32,1024]{2,1,0:T(8,128)(2,1)}), bf16[4,128,1024]{2,1,0:T(8,128)(2,1)}) %all-gather.27.cloned.1.call-update) | async-done | bytes 1048592 | tf_op jit(solution)/shard_map/all_gather | solution.py:233
  514.3 4.1 multiply_reduce_fusion.2
  518.4 5.9 psum.99
  524.3 3.8 multiply_reduce_fusion.3
  534.7 5.5 fusion.2
  555.1 39.3 %all-gather.31.cloned.1.call-done = bf16[32,6,64,128]{3,2,1,0:T(8,128)(2,1)} async-done(((bf16[4,6,64,128]{3,2,1,0:T(8,128)(2,1)}), bf16[32,6,64,128]{3,2,1,0:T(8,128)(2,1)}) %all-gather.31.cloned.1.call-update) | async-done | bytes 3145744 | tf_op jit(solution)/shard_map/all_gather | solution.py:60
  594.5 13.4 %while.28 = (s32[]{:T(128)}, f32[4,6,64,128]{3,2,1,0:T(8,128)S(1)}, s32[]{:T(128)}, bf16[8,4,6]{2,1,0:T(4,128)(2,1)}, bf16[8,4,6,64,128]{4,3,2,1,0:T(8,128)(2,1)...) while((s32[]{:T(128)}, f32[4,6,64,128]{3,2,1,0:T(8,128)S(1)}, s32[]{:T(128)}, ...), condition=%wide.region_18.19_spmd, body=%wide.region_17.18_spmd.sunk | while | flops 589854 | bytes 1966475 | solution.py:77
  607.9 3.9 fusion.99
  611.9 3.8 fusion.31
  621.9 4.2 collective-permute-done.3
  627.7 4.8 convolution_bitcast_fusion
  642.0 6.1 reduce_window_sum.34
  656.2 8.3 reduce-scatter.20.cloned.1.call-done
  670.3 4.1 convolution_bitcast_fusion.7
  674.4 6.2 multiply_reduce_fusion
  684.8 4.6 reduce_window_sum.33
  706.1 11.4 dynamic_update_slice.22
  717.5 85.6 %all-reduce.31 = bf16[1024,2,128]{2,1,0:T(2,128)(2,1)S(1)} all-reduce(f32[1024,2,128]{2,1,0:T(2,128)S(1)} %dynamic_update_slice.22), channel_id=10, replica_groups=mesh['dp'=8,'tensor'=4] {'dp'}, use_global_device_ids=true, to_apply=%region_34.35.clone | all-reduce | flops 262144 | bytes 1572864
  821.2 14.1 %reduce-scatter.36.cloned.1.call-done = f32[128,2,512]{2,0,1:T(8,128)} async-done(((f32[1024,2,512]{2,0,1:T(8,128)}), f32[128,2,512]{2,0,1:T(8,128)}) %reduce-scatter.36.cloned.1.call-update) | async-done | bytes 524304 | tf_op jit(solution)/shard_map/reduce_scatter | solution.py:606
  839.2 23.2 %reduce-scatter.22.cloned.1.call-done = bf16[4,32,1024]{2,1,0:T(8,128)(2,1)} async-done(((bf16[4,128,1024]{2,1,0:T(8,128)(2,1)}), bf16[4,32,1024]{2,1,0:T(8,128)(2,1)}) %reduce-scatter.22.cloned.1.call-update) | async-done | bytes 262160 | tf_op jit(solution)/shard_map/reduce_scatter | solution.py:236
  863.6 40.9 %all-reduce.25 = (f32[1024]{0:T(1024)}, f32[1024]{0:T(1024)}, f32[4,1536]{1,0:T(4,128)S(1)}, f32[1536]{0:T(1024)S(1)}, f32[4,256]{1,0:T(4,128)}, /*index=5*/f32[...) all-reduce(f32[1024]{0:T(1024)S(1)} %get-tuple-element.321, ...), channel_id=1, replica_groups=mesh['dp'=8,'tensor'=4] {'dp','tensor'}, use_global_device_ids=true, to_apply=%region_30.31 | all-reduce | flops 12616 | bytes 100928 | tf_op jit(solution)/shard_map/psum | solution.py:626
  910.5 13.2 all-reduce.30.cloned.1.call-done
  926.7 75.3 %reduce-scatter.28.cloned.1.call-done = f32[128,2,384]{2,0,1:T(8,128)} async-done(((f32[1024,2,384]{2,0,1:T(8,128)}), f32[128,2,384]{2,0,1:T(8,128)}) %reduce-scatter.28.cloned.1.call-update) | async-done | bytes 393232 | tf_op jit(solution)/shard_map/reduce_scatter | solution.py:603
  1004.1 69.8 %reduce-scatter.38.cloned.1.call-done = f32[512,128]{1,0:T(8,128)} async-done(((f32[512,1024]{1,0:T(8,128)}), f32[512,128]{1,0:T(8,128)}) %reduce-scatter.38.cloned.1.call-update) | async-done | bytes 262160 | tf_op jit(solution)/shard_map/reduce_scatter | solution.py:607
  1073.9 65.7 %reduce-scatter.26.cloned.1.call-done = f32[128,128]{1,0:T(8,128)} async-done(((f32[128,1024]{1,0:T(8,128)}), f32[128,128]{1,0:T(8,128)}) %reduce-scatter.26.cloned.1.call-update) | async-done | bytes 65552 | tf_op jit(solution)/shard_map/reduce_scatter | solution.py:602
  1139.6 64.9 %reduce-scatter.24.cloned.1.call-done = f32[128,128]{1,0:T(8,128)} async-done(((f32[1024,128]{1,0:T(8,128)}), f32[128,128]{1,0:T(8,128)}) %reduce-scatter.24.cloned.1.call-update) | async-done | bytes 65552 | tf_op jit(solution)/shard_map/reduce_scatter | solution.py:601
  1204.5 69.1 %reduce-scatter.34.cloned.1.call-done = f32[384,128]{1,0:T(8,128)} async-done(((f32[384,1024]{1,0:T(8,128)}), f32[384,128]{1,0:T(8,128)}) %reduce-scatter.34.cloned.1.call-update) | async-done | bytes 196624 | tf_op jit(solution)/shard_map/reduce_scatter | solution.py:605
  1273.6 56.0 %reduce-scatter.32.cloned.1.call-done = f32[128,6]{0,1:T(8,128)} async-done(((f32[1024,6]{0,1:T(8,128)}), f32[128,6]{0,1:T(8,128)}) %reduce-scatter.32.cloned.1.call-update) | async-done | bytes 3088 | tf_op jit(solution)/shard_map/reduce_scatter | solution.py:604
  (564 shorter events, 208.4 us)
Async XLA Ops:
  7.2 103.4 %all-gather.13.cloned.1.call-start = ((), (), s32[]{:S(2)}) async-start(), calls=%async_computation.13 | async-start | bytes 1310720 | tf_op jit(solution)/shard_map/all_gather | solution.py:233
  7.2 70.9 %copy-start.135 = (f32[4,256]{1,0:T(4,128)S(1)}, f32[4,256]{1,0:T(4,128)}, u32[]{:S(2)}) copy-start(f32[4,256]{1,0:T(4,128)} %param.39) | copy-start | bytes 12292
  7.3 70.9 %copy-start.55 = (s32[4,1024]{1,0:T(4,128)S(1)}, s32[4,1024]{1,0:T(4,128)}, u32[]{:S(2)}) copy-start(s32[4,1024]{1,0:T(4,128)} %param.27) | copy-start | bytes 49156
  7.3 71.9 %copy-start.85 = (bf16[128,256]{1,0:T(8,128)(2,1)S(1)}, bf16[128,256]{1,0:T(8,128)(2,1)}, u32[]{:S(2)}) copy-start(bf16[128,256]{1,0:T(8,128)(2,1)} %param.35) | copy-start | bytes 196612
  8.4 102.2 %copy-start.107 = (f32[4,32]{1,0:T(4,128)}, f32[4,32]{1,0:T(4,128)S(1)}, u32[]{:S(2)}) copy-start(f32[4,32]{1,0:T(4,128)S(1)} %fusion.117) | copy-start | bytes 1540
  8.4 102.1 %copy-start.92 = (f32[4,32]{1,0:T(4,128)}, f32[4,32]{1,0:T(4,128)S(1)}, u32[]{:S(2)}) copy-start(f32[4,32]{1,0:T(4,128)S(1)} %fusion.170) | copy-start | bytes 1540
  10.2 100.4 %copy-start.144 = (f32[6]{0:T(128)S(1)}, f32[6]{0:T(128)}, u32[]{:S(2)}) copy-start(f32[6]{0:T(128)} %param.41) | copy-start | bytes 76
  10.2 109.8 %all-gather.17.cloned.1.call-start = ((), (), s32[]{:S(2)}) async-start(), calls=%async_computation.15 | async-start | bytes 1769472 | tf_op jit(solution)/shard_map/all_gather | solution.py:204
  11.9 256.5 %all-gather.15.cloned.1.call-start = ((), (), s32[]{:S(2)}) async-start(), calls=%async_computation.14 | async-start | bytes 1179648 | tf_op jit(solution)/shard_map/all_gather | solution.py:247
  13.2 99.2 %copy-start.139 = (f32[6]{0:T(128)}, f32[6]{0:T(128)S(1)}, u32[]{:S(2)}) copy-start(f32[6]{0:T(128)S(1)} %exponential_negate_fusion) | copy-start | bytes 76
  15.4 97.0 %copy-start.80 = (s32[4,128]{1,0:T(4,128)}, s32[4,128]{1,0:T(4,128)S(1)}, u32[]{:S(2)}) copy-start(s32[4,128]{1,0:T(4,128)S(1)} %get-tuple-element.372) | copy-start | bytes 6148
  113.4 121.8 %copy-start.16 = (f32[4,128,6]{2,1,0:T(8,128)}, f32[4,128,6]{2,1,0:T(8,128)S(1)}, u32[]{:S(2)}) copy-start(f32[4,128,6]{2,1,0:T(8,128)S(1)} %reduce_window_sum.32) | copy-start | bytes 36868
  114.0 4.6 collective-permute-start.1
  117.9 158.3 %all-gather.29.cloned.1.call-start = ((), (), s32[]{:S(2)}) async-start(), calls=%async_computation.34 | async-start | bytes 3538944 | tf_op jit(solution)/shard_map/all_gather | solution.py:35
  123.5 4.2 collective-permute-start
  127.0 133.6 %copy-start.23 = (f32[4,128,128]{2,1,0:T(8,128)}, f32[4,128,128]{2,1,0:T(8,128)S(1)}, u32[]{:S(2)}) copy-start(f32[4,128,128]{2,1,0:T(8,128)S(1)} %get-tuple-element.396) | copy-start | bytes 786436
  129.7 164.5 %copy-start.5 = (f32[4,128,384]{1,2,0:T(8,128)}, f32[4,128,384]{1,2,0:T(8,128)S(1)}, u32[]{:S(2)}) copy-start(f32[4,128,384]{1,2,0:T(8,128)S(1)} %copy.207) | copy-start | bytes 2359300
  132.6 199.8 %reduce-scatter.14.cloned.1.call-start = ((), (), s32[]{:S(2)}) async-start(), calls=%async_computation.16 | async-start | bytes 1310720 | tf_op jit(solution)/shard_map/reduce_scatter | solution.py:236
  134.1 101.2 %copy-start.106 = (f32[4,128]{1,0:T(4,128)S(1)}, f32[4,128]{1,0:T(4,128)}, u32[]{:S(2)}) copy-start(f32[4,128]{1,0:T(4,128)} %get-tuple-element.371) | copy-start | bytes 6148
  306.2 218.1 %copy-start.126 = (f32[4,128]{1,0:T(4,128)}, f32[4,128]{1,0:T(4,128)S(1)}, u32[]{:S(2)}) copy-start(f32[4,128]{1,0:T(4,128)S(1)} %rsqrt_bitcast_fusion) | copy-start | bytes 6148
  310.3 74.2 %all-gather.21.cloned.1.call-start = ((), (), s32[]{:S(2)}) async-start(), calls=%async_computation.18 | async-start | bytes 2359296 | tf_op jit(solution)/shard_map/all_gather | solution.py:208
  312.1 89.9 %all-gather.19.cloned.1.call-start = ((), (), s32[]{:S(2)}) async-start(), calls=%async_computation.17 | async-start | bytes 1310720 | tf_op jit(solution)/shard_map/all_gather | solution.py:233
  333.5 161.9 %copy-start.89 = (f32[4,32]{1,0:T(4,128)}, f32[4,32]{1,0:T(4,128)S(1)}, u32[]{:S(2)}) copy-start(f32[4,32]{1,0:T(4,128)S(1)} %fusion.171) | copy-start | bytes 1540
  335.3 85.1 %all-gather.25.cloned.1.call-start = ((), (), s32[]{:S(2)}) async-start(), calls=%async_computation.21 | async-start | bytes 1310720 | tf_op jit(solution)/shard_map/all_gather | solution.py:233
  336.1 126.1 %all-gather.23.cloned.1.call-start = ((), (), s32[]{:S(2)}) async-start(), calls=%async_computation.19 | async-start | bytes 1179648 | tf_op jit(solution)/shard_map/all_gather | solution.py:209
  336.8 156.8 %reduce-scatter.18.cloned.1.call-start = ((), (), s32[]{:S(2)}) async-start(), calls=%async_computation.22 | async-start | bytes 1310720 | tf_op jit(solution)/shard_map/reduce_scatter | solution.py:236
  469.7 44.5 %all-gather.27.cloned.1.call-start = ((), (), s32[]{:S(2)}) async-start(), calls=%async_computation.23 | async-start | bytes 1310720 | tf_op jit(solution)/shard_map/all_gather | solution.py:233
  497.4 97.1 %all-gather.31.cloned.1.call-start = ((), (), s32[]{:S(2)}) async-start(), calls=%async_computation.35 | async-start | bytes 3538944 | tf_op jit(solution)/shard_map/all_gather | solution.py:60
  532.8 131.8 %reduce-scatter.20.cloned.1.call-start = ((), (), s32[]{:S(2)}) async-start(), calls=%async_computation.24 | async-start | bytes 2359296 | tf_op jit(solution)/shard_map/reduce_scatter | solution.py:492
  545.3 258.5 %reduce-scatter.30.cloned.1.call-start = ((), (), s32[]{:S(2)}) async-start(), calls=%async_computation.29 | async-start | bytes 1179648 | tf_op jit(solution)/shard_map/reduce_scatter | solution.py:609
  620.6 5.5 collective-permute-start.3
  627.7 207.6 %reduce-scatter.36.cloned.1.call-start = ((), (), s32[]{:S(2)}) async-start(), calls=%async_computation.32 | async-start | bytes 4718592 | tf_op jit(solution)/shard_map/reduce_scatter | solution.py:606
  632.5 229.9 %reduce-scatter.22.cloned.1.call-start = ((), (), s32[]{:S(2)}) async-start(), calls=%async_computation.25 | async-start | bytes 1310720 | tf_op jit(solution)/shard_map/reduce_scatter | solution.py:236
  692.3 5.7 collective-permute-start.2
  702.2 202.3 %reduce-scatter.16.cloned.1.call-start = ((), (), s32[]{:S(2)}) async-start(), calls=%async_computation.20 | async-start | bytes 1310720 | tf_op jit(solution)/shard_map/reduce_scatter | solution.py:236
  704.0 219.7 %all-reduce.30.cloned.1.call-start = ((), (), s32[]{:S(2)}) async-start(), calls=%async_computation.36 | async-start | bytes 262144 | tf_op jit(solution)/shard_map/psum | solution.py:242
  805.4 196.7 %reduce-scatter.28.cloned.1.call-start = ((), (), s32[]{:S(2)}) async-start(), calls=%async_computation.28 | async-start | bytes 3538944 | tf_op jit(solution)/shard_map/reduce_scatter | solution.py:603
  809.2 264.7 %reduce-scatter.38.cloned.1.call-start = ((), (), s32[]{:S(2)}) async-start(), calls=%async_computation.33 | async-start | bytes 2359296 | tf_op jit(solution)/shard_map/reduce_scatter | solution.py:607
  813.6 326.0 %reduce-scatter.26.cloned.1.call-start = ((), (), s32[]{:S(2)}) async-start(), calls=%async_computation.27 | async-start | bytes 589824 | tf_op jit(solution)/shard_map/reduce_scatter | solution.py:602
  815.8 388.7 %reduce-scatter.24.cloned.1.call-start = ((), (), s32[]{:S(2)}) async-start(), calls=%async_computation.26 | async-start | bytes 589824 | tf_op jit(solution)/shard_map/reduce_scatter | solution.py:601
  817.1 456.4 %reduce-scatter.34.cloned.1.call-start = ((), (), s32[]{:S(2)}) async-start(), calls=%async_computation.31 | async-start | bytes 1769472 | tf_op jit(solution)/shard_map/reduce_scatter | solution.py:605
  820.3 84.2 %copy-start.15 = (bf16[4,32,1024]{2,1,0:T(8,128)(2,1)S(1)}, bf16[4,32,1024]{2,1,0:T(8,128)(2,1)}, u32[]{:S(2)}) copy-start(bf16[4,32,1024]{2,1,0:T(8,128)(2,1)} %reduce-scatter.14.cloned.1.call-done) | copy-start | bytes 786436
  820.3 84.2 %copy-start.31 = (bf16[4,32,1024]{2,1,0:T(8,128)(2,1)S(1)}, bf16[4,32,1024]{2,1,0:T(8,128)(2,1)}, u32[]{:S(2)}) copy-start(bf16[4,32,1024]{2,1,0:T(8,128)(2,1)} %reduce-scatter.18.cloned.1.call-done) | copy-start | bytes 786436
  820.3 84.2 %copy-start.33 = (bf16[4,32,1024]{2,1,0:T(8,128)(2,1)S(1)}, bf16[4,32,1024]{2,1,0:T(8,128)(2,1)}, u32[]{:S(2)}) copy-start(bf16[4,32,1024]{2,1,0:T(8,128)(2,1)} %param.28) | copy-start | bytes 786436
  820.4 84.2 %copy-start.82 = (f32[1024]{0:T(1024)S(1)}, f32[1024]{0:T(1024)}, u32[]{:S(2)}) copy-start(f32[1024]{0:T(1024)} %param.30) | copy-start | bytes 12292
  820.4 84.2 %copy-start.90 = (f32[4,32]{1,0:T(4,128)S(1)}, f32[4,32]{1,0:T(4,128)}, u32[]{:S(2)}) copy-start(f32[4,32]{1,0:T(4,128)} %copy-done.89) | copy-start | bytes 1540
  820.4 84.2 %copy-start.105 = (f32[4,32]{1,0:T(4,128)S(1)}, f32[4,32]{1,0:T(4,128)}, u32[]{:S(2)}) copy-start(f32[4,32]{1,0:T(4,128)} %copy-done.104) | copy-start | bytes 1540
  820.4 509.2 %reduce-scatter.32.cloned.1.call-start = ((), (), s32[]{:S(2)}) async-start(), calls=%async_computation.30 | async-start | bytes 36864 | tf_op jit(solution)/shard_map/reduce_scatter | solution.py:604
  (133 other events, 1538.6 us)
Sparse Core Ops, SparseCore 0:
  10.4 19.4 all-gather.12
  32.6 45.3 all-gather.16
  118.0 40.5 all-gather.14
  161.2 71.1 all-gather.28
  310.4 21.9 reduce-scatter.13
  335.2 49.2 all-gather.20
  386.7 15.2 all-gather.18
  403.6 16.7 all-gather.24
  422.6 39.5 all-gather.22
  469.9 23.7 reduce-scatter.17
  497.5 16.7 all-gather.26
  532.9 61.4 all-gather.30
  598.0 66.5 reduce-scatter.19
  667.8 63.6 reduce-scatter.29
  735.4 99.8 reduce-scatter.35
  837.7 24.7 reduce-scatter.21
  865.0 24.8 reduce-scatter.15
  892.1 31.5 all-reduce.29
  927.7 74.3 reduce-scatter.27
  1006.5 67.4 reduce-scatter.37
  1078.2 61.3 reduce-scatter.25
  1143.5 60.9 reduce-scatter.23
  1208.9 64.6 reduce-scatter.33
  1277.1 52.4 reduce-scatter.31
where the time goes:
time: 1350 us; the launch traced here: 1340 us
  waiting for transfers between devices  690 us (51%)
  blocking collectives  344 us (25%)
  matrix products  120 us (9%)
  other arithmetic  94.8 us (7%)
  local copies, waits for them, and re-layouts  59.8 us (4%)
  between operations  17.5 us (1%)
    unnamed x1, blocking collectives  85.6 us
    reduce_scatter x1, waiting for transfers between devices, body(): lax.psum_scatter(grad_mixer_in, 'dp', scatter_dimension=0, tiled=True)  75.3 us
    reduce_scatter x1, waiting for transfers between devices, body(): lax.psum_scatter(down_gradient, 'dp', scatter_dimension=1, tiled=True)  69.8 us
    reduce_scatter x1, waiting for transfers between devices, body(): lax.psum_scatter(grad_mixer_out, 'dp', scatter_dimension=1, tiled=True)  69.1 us
    reduce_scatter x4, waiting for transfers between devices, sum_rows(): lax.psum_scatter(partial_rows.astype(jnp.bfloat16), 'tensor', scatter_dim...  67.4 us
    reduce_scatter x1, waiting for transfers between devices, body(): lax.psum_scatter(grad_attn_out, 'dp', scatter_dimension=1, tiled=True)  65.7 us
    reduce_scatter x1, waiting for transfers between devices, body(): lax.psum_scatter(grad_query_w, 'dp', scatter_dimension=0, tiled=True)  64.9 us
    reduce_scatter x1, waiting for transfers between devices, body(): lax.psum_scatter(grad_step_w, 'dp', scatter_dimension=0, tiled=True)  56 us
  transfers between devices with their start and end apart: 28, of which 21 were waited for; matrix products, arithmetic and copies ran while one was open for 16% of the time, Pallas kernels for 0%

commit v1 on v0

--- a/solution.py
+++ b/solution.py
@@ -4,15 +4,797 @@
 import jax
 import jax.numpy as jnp
 from jax import lax
+from jax.experimental import pallas as pl
+from jax.experimental.pallas import tpu as pltpu
 from jax.sharding import PartitionSpec as P
 
 KVH = 2
-
-
 EPSILON = 1e-05
 ROTARY_BASE = 100000000000.0
 MASKED = -1e30
 MATMUL_EXACTNESS = lax.Precision.HIGHEST
+LANES = 128
+F32 = jnp.float32
+BF16 = jnp.bfloat16
+VMEM_BYTES = 60 * 2**20
+
+
+def dot_nn(a, b):
+    return lax.dot_general(a, b, (((1,), (0,)), ((), ())), preferred_element_type=F32)
+
+
+def dot_nt(a, b):
+    return lax.dot_general(a, b, (((1,), (1,)), ((), ())), preferred_element_type=F32)
+
+
+def dot_tn(a, b):
+    return lax.dot_general(a, b, (((0,), (0,)), ((), ())), preferred_element_type=F32)
+
+
+def remote(src, dst, send_sem, recv_sem, where):
+    return pltpu.make_async_remote_copy(
+        src_ref=src,
+        dst_ref=dst,
+        send_sem=send_sem,
+        recv_sem=recv_sem,
+        device_id=where,
+        device_id_type=pl.DeviceIdType.MESH,
+    )
+
+
+class Place:
+    def __init__(self, devices):
+        self.devices = devices
+        self.lines = devices // 2
+        self.dp = lax.axis_index("dp")
+        self.t = lax.axis_index("tensor")
+        self.z = lax.div(self.dp, 2)
+        self.p = lax.rem(self.dp, 2)
+        self.pair = self.dp + 1 - 2 * self.p
+        self.t_near = self.t + 1 - 2 * lax.rem(self.t, 2)
+        self.t_far = lax.rem(self.t + 2, 4)
+        self.t_both = lax.rem(self.t_near + 2, 4)
+        self.first = self.z == 0
+        self.last = self.z == self.lines - 1
+
+    def flips(self):
+        bit = 1
+        while bit < self.devices:
+            yield self.dp + bit - 2 * bit * lax.rem(lax.div(self.dp, bit), 2)
+            bit *= 2
+
+    def greet(self, line=False, tensor=False, flips=False):
+        barrier = pltpu.get_barrier_semaphore()
+        count = 0
+
+        def signal(**where):
+            pl.semaphore_signal(
+                barrier, inc=1, device_id=where, device_id_type=pl.DeviceIdType.MESH
+            )
+
+        if tensor:
+            signal(tensor=self.t_near)
+            signal(tensor=self.t_far)
+            count = count + 2
+        if line:
+            signal(dp=self.pair)
+            count = count + 1
+
+            @pl.when(jnp.logical_not(self.first))
+            def _():
+                signal(dp=self.dp - 2)
+
+            @pl.when(jnp.logical_not(self.last))
+            def _():
+                signal(dp=self.dp + 2)
+
+        if flips:
+            for other in self.flips():
+                signal(dp=other)
+                count = count + 1
+        if line:
+            count = count + 2
+            count = count - self.first.astype(jnp.int32) - self.last.astype(jnp.int32)
+        pl.semaphore_wait(barrier, count)
+
+
+class LineGather:
+    def __init__(self, place, view, recv, right, left, pair):
+        self.at, self.view = place, view
+        self.recv, self.right, self.left, self.side = recv, right, left, pair
+
+    def copy(self, block, sem, where):
+        ref = self.view(block)
+        return remote(ref, ref, sem, self.recv.at[block], where)
+
+    def send_right(self, zz):
+        return self.copy(zz * 2 + self.at.p, self.right.at[zz], {"dp": self.at.dp + 2})
+
+    def send_left(self, zz):
+        return self.copy(zz * 2 + self.at.p, self.left.at[zz], {"dp": self.at.dp - 2})
+
+    def send_pair(self, zz):
+        return self.copy(zz * 2 + self.at.p, self.side.at[zz], {"dp": self.at.pair})
+
+    def arrived(self, block):
+        self.copy(block, self.side.at[0], {"dp": self.at.pair}).wait_recv()
+
+    def start(self):
+        at = self.at
+        pl.when(jnp.logical_not(at.last))(lambda: self.send_right(at.z).start())
+        pl.when(jnp.logical_not(at.first))(lambda: self.send_left(at.z).start())
+        self.send_pair(at.z).start()
+
+    def step(self, s):
+        at = self.at
+        low, high = at.z - 1 - s, at.z + 1 + s
+
+        @pl.when(low >= 0)
+        def _():
+            self.arrived(low * 2 + at.p)
+            pl.when(jnp.logical_not(at.last))(lambda: self.send_right(low).start())
+            self.send_pair(low).start()
+
+        @pl.when(high < at.lines)
+        def _():
+            self.arrived(high * 2 + at.p)
+            pl.when(jnp.logical_not(at.first))(lambda: self.send_left(high).start())
+            self.send_pair(high).start()
+
+    def finish(self):
+        at = self.at
+
+        @pl.loop(0, at.lines)
+        def _(zz):
+            self.arrived(zz * 2 + 1 - at.p)
+
+    def drain(self):
+        at = self.at
+
+        @pl.loop(0, at.lines)
+        def _(zz):
+            self.send_pair(zz).wait_send()
+
+            @pl.when(jnp.logical_and(zz <= at.z, jnp.logical_not(at.last)))
+            def _():
+                self.send_right(zz).wait_send()
+
+            @pl.when(jnp.logical_and(zz >= at.z, jnp.logical_not(at.first)))
+            def _():
+                self.send_left(zz).wait_send()
+
+
+class LineScatter:
+    def __init__(self, place, part, got, right, left, sems):
+        self.at, self.part = place, part
+        self.got, self.right, self.left = got, right, left
+        (
+            self.pair_send,
+            self.pair_recv,
+            self.right_send,
+            self.right_recv,
+            self.left_send,
+            self.left_recv,
+        ) = sems
+
+    def pair_copy(self, zz):
+        src = self.part(zz * 2 + 1 - self.at.p)
+        return remote(
+            src, self.got(zz), self.pair_send.at[zz], self.pair_recv.at[zz], {"dp": self.at.pair}
+        )
+
+    def right_copy(self, zz):
+        src = self.part(zz * 2 + self.at.p)
+        return remote(
+            src,
+            self.right(zz),
+            self.right_send.at[zz],
+            self.right_recv.at[zz],
+            {"dp": self.at.dp + 2},
+        )
+
+    def left_copy(self, zz):
+        src = self.part(zz * 2 + self.at.p)
+        return remote(
+            src, self.left(zz), self.left_send.at[zz], self.left_recv.at[zz], {"dp": self.at.dp - 2}
+        )
+
+    def start(self):
+        at = self.at
+
+        @pl.loop(0, at.lines)
+        def _(i):
+            self.pair_copy(at.lines - 1 - i).start()
+
+    def add_into(self, ref, *others):
+        total = ref[...].astype(F32)
+        for other in others:
+            total = total + other[...].astype(F32)
+        ref[...] = total.astype(BF16)
+
+    def step(self, i):
+        at = self.at
+        high, low = at.lines - 1 - i, i
+
+        @pl.when(high > at.z)
+        def _():
+            self.pair_copy(high).wait_recv()
+            ref = self.part(high * 2 + at.p)
+
+            @pl.when(at.first)
+            def _():
+                self.add_into(ref, self.got(high))
+
+            @pl.when(jnp.logical_not(at.first))
+            def _():
+                self.right_copy(high).wait_recv()
+                self.add_into(ref, self.got(high), self.right(high))
+
+            self.right_copy(high).start()
+
+        @pl.when(low < at.z)
+        def _():
+            self.pair_copy(low).wait_recv()
+            ref = self.part(low * 2 + at.p)
+
+            @pl.when(at.last)
+            def _():
+                self.add_into(ref, self.got(low))
+
+            @pl.when(jnp.logical_not(at.last))
+            def _():
+                self.left_copy(low).wait_recv()
+                self.add_into(ref, self.got(low), self.left(low))
+
+            self.left_copy(low).start()
+
+    def finish(self, out):
+        at = self.at
+        self.pair_copy(at.z).wait_recv()
+        out[...] = self.part(at.dp)[...].astype(F32) + self.got(at.z)[...].astype(F32)
+
+        @pl.when(jnp.logical_not(at.first))
+        def _():
+            self.right_copy(at.z).wait_recv()
+            out[...] += self.right(at.z)[...].astype(F32)
+
+        @pl.when(jnp.logical_not(at.last))
+        def _():
+            self.left_copy(at.z).wait_recv()
+            out[...] += self.left(at.z)[...].astype(F32)
+
+    def drain(self):
+        at = self.at
+
+        @pl.loop(0, at.lines)
+        def _(zz):
+            self.pair_copy(zz).wait_send()
+            pl.when(zz > at.z)(lambda: self.right_copy(zz).wait_send())
+            pl.when(zz < at.z)(lambda: self.left_copy(zz).wait_send())
+
+
+class RowGather:
+    def __init__(self, place, view, send, recv):
+        self.at, self.view, self.send, self.recv = place, view, send, recv
+
+    def copy(self, rank, chunk, sem, near):
+        ref = self.view(rank, chunk)
+        where = {"tensor": self.at.t_near if near else self.at.t_far}
+        return remote(ref, ref, self.send.at[chunk, sem], self.recv.at[chunk, rank], where)
+
+    def start(self, chunk):
+        self.copy(self.at.t, chunk, 0, False).start()
+        self.copy(self.at.t, chunk, 1, True).start()
+
+    def forward(self, chunk):
+        self.copy(self.at.t_far, chunk, 2, False).wait_recv()
+        self.copy(self.at.t_far, chunk, 2, True).start()
+
+    def finish(self, chunk):
+        self.copy(self.at.t_near, chunk, 1, True).wait_recv()
+        self.copy(self.at.t_both, chunk, 2, True).wait_recv()
+
+    def drain(self, chunk):
+        self.copy(self.at.t, chunk, 0, False).wait_send()
+        self.copy(self.at.t, chunk, 1, True).wait_send()
+        self.copy(self.at.t_far, chunk, 2, True).wait_send()
+
+
+class RowScatter:
+    def __init__(self, place, view, near_buf, far_buf, send, recv):
+        self.at, self.view = place, view
+        self.near_buf, self.far_buf = near_buf, far_buf
+        self.send, self.recv = send, recv
+
+    def near_copy(self, chunk, which):
+        rank = self.at.t_both if which else self.at.t_near
+        return remote(
+            self.view(rank, chunk),
+            self.near_buf(which, chunk),
+            self.send.at[chunk, which],
+            self.recv.at[chunk, which],
+            {"tensor": self.at.t_near},
+        )
+
+    def far_copy(self, chunk):
+        return remote(
+            self.view(self.at.t_far, chunk),
+            self.far_buf(chunk),
+            self.send.at[chunk, 2],
+            self.recv.at[chunk, 2],
+            {"tensor": self.at.t_far},
+        )
+
+    def start(self, chunk):
+        self.near_copy(chunk, 1).start()
+        self.near_copy(chunk, 0).start()
+
+    def middle(self, chunk):
+        self.near_copy(chunk, 1).wait_recv()
+        ref = self.view(self.at.t_far, chunk)
+        ref[...] = (ref[...].astype(F32) + self.near_buf(1, chunk)[...].astype(F32)).astype(BF16)
+        self.far_copy(chunk).start()
+
+    def finish(self, chunk):
+        self.near_copy(chunk, 0).wait_recv()
+        total = self.view(self.at.t, chunk)[...].astype(F32) + self.near_buf(0, chunk)[
+            ...
+        ].astype(F32)
+        self.far_copy(chunk).wait_recv()
+        return total + self.far_buf(chunk)[...].astype(F32)
+
+    def drain(self, chunk):
+        self.near_copy(chunk, 0).wait_send()
+        self.near_copy(chunk, 1).wait_send()
+        self.far_copy(chunk).wait_send()
+
+
+def line_gather_sems(devices):
+    dma = pltpu.SemaphoreType.DMA
+    return [dma((devices,)), dma((devices // 2,)), dma((devices // 2,)), dma((devices // 2,))]
+
+
+def line_scatter_sems(devices):
+    return [pltpu.SemaphoreType.DMA((devices // 2,)) for _ in range(6)]
+
+
+def rms_rows(values, gain):
+    return values * lax.rsqrt(jnp.mean(values * values, -1, keepdims=True) + EPSILON) * gain
+
+
+def rms_rows_grad(values, gain, grad):
+    scale = lax.rsqrt(jnp.mean(values * values, -1, keepdims=True) + EPSILON)
+    term = grad * gain
+    inner = jnp.mean(values * term, -1, keepdims=True)
+    return scale * (term - values * (scale * scale * inner)), grad * values * scale
+
+
+def enter_kernel(devices, pieces, in_width, *refs):
+    (x_ref, og_in, gain_ref, w_in, w_all, nx, og, proj, row_send, row_recv), sems = (
+        refs[:10],
+        refs[10:],
+    )
+    at = Place(devices)
+    seqs, sub, width = x_ref.shape
+    depth = w_in.shape[0]
+    at.greet(line=True, tensor=True)
+    w_all[pl.ds(pl.multiple_of(at.dp * depth, depth), depth), :] = w_in[...]
+    gathers = []
+    for i, (first, size) in enumerate(pieces):
+
+        def view(block, first=first, size=size):
+            return w_all.at[
+                pl.ds(pl.multiple_of(block * depth, depth), depth), pl.ds(first, size)
+            ]
+
+        gathers.append(LineGather(at, view, *sems[4 * i : 4 * i + 4]))
+    gathers[0].start()
+    gain = gain_ref[...]
+    mine = pl.ds(pl.multiple_of(at.t * sub, sub), sub)
+    for s in range(seqs):
+        nx[s, mine, :] = rms_rows(x_ref[s].astype(F32), gain).astype(BF16)
+        og[s, mine, :] = og_in[s]
+    half = seqs // 2
+
+    def rows_of(buf):
+        def view(rank, chunk):
+            return buf.at[pl.ds(chunk * half, half), pl.ds(pl.multiple_of(rank * sub, sub), sub), :]
+
+        return view
+
+    row_nx = RowGather(at, rows_of(nx), row_send.at[0], row_recv.at[0])
+    row_og = RowGather(at, rows_of(og), row_send.at[1], row_recv.at[1])
+    for chunk in range(2):
+        row_nx.start(chunk)
+    for chunk in range(2):
+        row_nx.forward(chunk)
+    for chunk in range(2):
+        row_nx.finish(chunk)
+    for i, gather in enumerate(gathers):
+        if i + 1 < len(gathers):
+            gathers[i + 1].start()
+
+        @pl.loop(0, at.lines - 1)
+        def _(s):
+            gather.step(s)
+
+        gather.finish()
+        if i == 0:
+            for chunk in range(2):
+                row_og.start(chunk)
+        if i == 1:
+            rows = nx[...].reshape(seqs * nx.shape[1], width)
+            tile = LANES
+
+            @pl.loop(0, in_width // tile)
+            def _(j):
+                cols = pl.ds(pl.multiple_of(j * tile, tile), tile)
+                proj[:, cols] = dot_nn(rows, w_all[:, cols])
+
+            for chunk in range(2):
+                row_og.forward(chunk)
+            for chunk in range(2):
+                row_og.finish(chunk)
+    for gather in gathers:
+        gather.drain()
+    for row in (row_nx, row_og):
+        for chunk in range(2):
+            row.drain(chunk)
+
+
+def enter(devices, tensor, pieces, in_width, x, out_grad, gain, w_in):
+    seqs, sub, width = x.shape
+    depth, columns = w_in.shape
+    span = sub * tensor
+    shape = jax.ShapeDtypeStruct
+    vmem = pl.BlockSpec(memory_space=pltpu.VMEM)
+    dma = pltpu.SemaphoreType.DMA
+    return pl.pallas_call(
+        partial(enter_kernel, devices, pieces, in_width),
+        out_shape=(
+            shape((width, columns), BF16),
+            shape((seqs, span, width), BF16),
+            shape((seqs, span, width), BF16),
+            shape((seqs * span, in_width), F32),
+        ),
+        in_specs=[vmem] * 4,
+        out_specs=(vmem,) * 4,
+        scratch_shapes=[dma((2, 2, 3)), dma((2, 2, 4))] + line_gather_sems(devices) * len(pieces),
+        compiler_params=pltpu.CompilerParams(
+            collective_id=0, has_side_effects=True, vmem_limit_bytes=VMEM_BYTES
+        ),
+        name="enter",
+    )(x, out_grad, gain, w_in)
+
+
+def ffn_kernel(devices, layout, *refs):
+    (
+        x_ref, a_ref, og_ref, ogl_ref, gain_ref, w_ref,
+        out_ref, gh_ref, gb, nf, act, dgu, gain_grad,
+        part, part2, near1, far1, near2, far2, near3, far3, hid,
+        send, recv,
+    ) = refs
+    at = Place(devices)
+    seqs, sub, width = x_ref.shape
+    span = sub * 4
+    half = seqs // 2
+    rows = half * span
+    out_w, gu_w, dn_w = (pl.ds(*layout[k]) for k in ("out", "gu", "down"))
+    ff = layout["down"][1]
+    at.greet(tensor=True)
+
+    def rows_of(buf):
+        def view(rank, chunk):
+            return buf.at[pl.ds(chunk * half, half), pl.ds(pl.multiple_of(rank * sub, sub), sub), :]
+
+        return view
+
+    def parts_of(buf):
+        return lambda which, chunk: buf.at[which, pl.ds(chunk * half, half)]
+
+    def part_of(buf):
+        return lambda chunk: buf.at[pl.ds(chunk * half, half)]
+
+    branch = RowScatter(at, rows_of(part), parts_of(near1), part_of(far1), send.at[0], recv.at[0])
+    ffn = RowScatter(at, rows_of(part2), parts_of(near2), part_of(far2), send.at[1], recv.at[1])
+    back = RowScatter(at, rows_of(part), parts_of(near3), part_of(far3), send.at[2], recv.at[2])
+    row_nf = RowGather(at, rows_of(nf), send.at[3], recv.at[3])
+    row_gb = RowGather(at, rows_of(gb), send.at[4], recv.at[4])
+    mine = pl.ds(pl.multiple_of(at.t * sub, sub), sub)
+    gain = gain_ref[...]
+
+    def seq_rows(chunk):
+        return pl.ds(chunk * half, half)
+
+    def tok_rows(chunk):
+        return pl.ds(chunk * rows, rows)
+
+    for c in range(2):
+        value = dot_nt(a_ref[tok_rows(c), :], w_ref[:, out_w])
+        part[seq_rows(c)] = value.astype(BF16).reshape(half, span, width)
+        branch.start(c)
+    for c in range(2):
+        branch.middle(c)
+    for c in range(2):
+        hidden = x_ref[seq_rows(c)].astype(F32) + branch.finish(c)
+        hid[seq_rows(c)] = hidden
+        nf[seq_rows(c), mine, :] = rms_rows(hidden, gain).astype(BF16)
+        row_nf.start(c)
+    for c in range(2):
+        row_nf.forward(c)
+    for c in range(2):
+        row_nf.finish(c)
+        branch.drain(c)
+        flat = nf[seq_rows(c)].reshape(rows, width)
+        flat_og = og_ref[seq_rows(c)].reshape(rows, width)
+        gate_up = dot_nn(flat, w_ref[:, gu_w])
+        gate, up = gate_up[:, :ff], gate_up[:, ff:]
+        sigmoid = jax.nn.sigmoid(gate)
+        grad_act = dot_nn(flat_og, w_ref[:, dn_w])
+        act[tok_rows(c), :] = (gate * sigmoid * up).astype(BF16)
+        dgu[tok_rows(c), :ff] = (
+            grad_act * up * sigmoid * (1.0 + gate * (1.0 - sigmoid))
+        ).astype(BF16)
+        dgu[tok_rows(c), ff:] = (grad_act * gate * sigmoid).astype(BF16)
+        value = dot_nt(dgu[tok_rows(c), :], w_ref[:, gu_w])
+        part[seq_rows(c)] = value.astype(BF16).reshape(half, span, width)
+        back.start(c)
+    for c in range(2):
+        back.middle(c)
+        value = dot_nt(act[tok_rows(c), :], w_ref[:, dn_w])
+        part2[seq_rows(c)] = value.astype(BF16).reshape(half, span, width)
+    total = jnp.zeros((1, width), F32)
+    for c in range(2):
+        grad_hidden, terms = rms_rows_grad(hid[seq_rows(c)], gain, back.finish(c))
+        total = total + jnp.sum(terms.reshape(half * sub, width), 0, keepdims=True)
+        grad_hidden = grad_hidden + ogl_ref[seq_rows(c)].astype(F32)
+        gh_ref[seq_rows(c)] = grad_hidden
+        gb[seq_rows(c), mine, :] = grad_hidden.astype(BF16)
+        row_gb.start(c)
+        ffn.start(c)
+    gain_grad[...] = total
+    for c in range(2):
+        row_gb.forward(c)
+        ffn.middle(c)
+    for c in range(2):
+        out_ref[seq_rows(c)] = (hid[seq_rows(c)] + ffn.finish(c)).astype(BF16)
+        row_gb.finish(c)
+    for c in range(2):
+        row_nf.drain(c)
+        row_gb.drain(c)
+        back.drain(c)
+        ffn.drain(c)
+
+
+def feed_forward(devices, tensor, layout, x, a, og, out_grad, gain, w_all):
+    seqs, sub, width = x.shape
+    span = sub * tensor
+    tokens = seqs * span
+    ff = layout["down"][1]
+    shape = jax.ShapeDtypeStruct
+    vmem = pl.BlockSpec(memory_space=pltpu.VMEM)
+    dma = pltpu.SemaphoreType.DMA
+    whole, own = (seqs, span, width), (seqs, sub, width)
+    return pl.pallas_call(
+        partial(ffn_kernel, devices, layout),
+        out_shape=(
+            shape(own, BF16),
+            shape(own, F32),
+            shape(whole, BF16),
+            shape(whole, BF16),
+            shape((tokens, ff), BF16),
+            shape((tokens, 2 * ff), BF16),
+            shape((1, width), F32),
+        ),
+        in_specs=[vmem] * 6,
+        out_specs=(vmem,) * 7,
+        scratch_shapes=[
+            pltpu.VMEM(whole, BF16),
+            pltpu.VMEM(whole, BF16),
+        ]
+        + [pltpu.VMEM((2,) + own, BF16), pltpu.VMEM(own, BF16)] * 3
+        + [
+            pltpu.VMEM(own, F32),
+            dma((5, 2, 3)),
+            dma((5, 2, 4)),
+        ],
+        compiler_params=pltpu.CompilerParams(
+            collective_id=1, has_side_effects=True, vmem_limit_bytes=VMEM_BYTES
+        ),
+        name="feed_forward",
+    )(x, a, og, out_grad, gain, w_all)
+
+
+def leave_kernel(devices, layout, pieces, *refs):
+    (
+        x_ref, gh_ref, gain_ref, w_ref, nx_ref, dp_ref, gb_ref, a_ref, nf_ref, dgu_ref, og_ref,
+        act_ref, small_ref,
+        rg_ref, dw_ref, sums, kvs,
+        part, near, far, grads, got, right, left, small_near, small_far, small_dp, kv_near, kv_far,
+        send, recv, small_send, small_recv, dp_send, dp_recv, kv_send, kv_recv, *sems,
+    ) = refs
+    at = Place(devices)
+    seqs, sub, width = x_ref.shape
+    span = sub * 4
+    half = seqs // 2
+    rows = half * span
+    depth = width // devices
+    in_w = layout["in"]
+    at.greet(line=True, tensor=True, flips=True)
+
+    def rows_of(buf):
+        def view(rank, chunk):
+            return buf.at[pl.ds(chunk * half, half), pl.ds(pl.multiple_of(rank * sub, sub), sub), :]
+
+        return view
+
+    back = RowScatter(
+        at,
+        rows_of(part),
+        lambda which, chunk: near.at[which, pl.ds(chunk * half, half)],
+        lambda chunk: far.at[pl.ds(chunk * half, half)],
+        send,
+        recv,
+    )
+    for c in range(2):
+        value = dot_nt(dp_ref[pl.ds(c * rows, rows), :], w_ref[:, pl.ds(*in_w)])
+        part[pl.ds(c * half, half)] = value.astype(BF16).reshape(half, span, width)
+        back.start(c)
+    scatters = []
+    for i, (first, size) in enumerate(pieces):
+
+        def block(buf, k, first=first, size=size):
+            return buf.at[pl.ds(pl.multiple_of(k * depth, depth), depth), pl.ds(first, size)]
+
+        scatters.append(
+            LineScatter(
+                at,
+                partial(block, grads),
+                partial(block, got),
+                partial(block, right),
+                partial(block, left),
+                sems[6 * i : 6 * i + 6],
+            )
+        )
+
+    flat_nx = nx_ref[...].reshape(2 * rows, width)
+
+    def product(lhs, rhs_ref, first):
+        size = rhs_ref.shape[-1]
+
+        @pl.loop(0, size // LANES)
+        def _(j):
+            cols = pl.ds(pl.multiple_of(j * LANES, LANES), LANES)
+            dst = pl.ds(pl.multiple_of(first + j * LANES, LANES), LANES)
+            grads[:, dst] = dot_tn(lhs, rhs_ref[:, cols]).astype(BF16)
+
+    product(flat_nx, dp_ref, in_w[0])
+    scatters[0].start()
+    for c in range(2):
+        back.middle(c)
+    product(gb_ref[...].reshape(2 * rows, width), a_ref, layout["out"][0])
+    scatters[1].start()
+    product(nf_ref[...].reshape(2 * rows, width), dgu_ref, layout["gu"][0])
+    scatters[2].start()
+    product(og_ref[...].reshape(2 * rows, width), act_ref, layout["down"][0])
+    scatters[3].start()
+    total = jnp.zeros((1, width), F32)
+    gain = gain_ref[...]
+    for c in range(2):
+        seq = pl.ds(c * half, half)
+        grad, terms = rms_rows_grad(x_ref[seq].astype(F32), gain, back.finish(c))
+        rg_ref[seq] = gh_ref[seq] + grad
+        total = total + jnp.sum(terms.reshape(half * sub, width), 0, keepdims=True)
+    sums[...] = small_ref[...]
+    sums[0:1, :] = total
+    for i, (buf, where) in enumerate(
+        ((small_near, {"tensor": at.t_near}), (small_far, {"tensor": at.t_far}))
+    ):
+        buf[0] = sums[0:8, :]
+        copy = remote(buf.at[0], buf.at[1], small_send.at[i], small_recv.at[i], where)
+        copy.start()
+        copy.wait()
+        sums[0:8, :] += buf[1]
+    for i, other in enumerate(at.flips()):
+        small_dp[i, 0] = sums[...]
+        copy = remote(
+            small_dp.at[i, 0], small_dp.at[i, 1], dp_send.at[i], dp_recv.at[i], {"dp": other}
+        )
+        copy.start()
+        copy.wait()
+        sums[...] += small_dp[i, 1]
+    for i, (first, size) in enumerate(pieces):
+
+        @pl.loop(0, at.lines - 1)
+        def _(s):
+            scatters[i].step(s)
+
+        scatters[i].finish(dw_ref.at[:, pl.ds(first, size)])
+        if i == 0:
+            state = layout["state"]
+            kvw = layout["kv"][1]
+            kv_near[0, :, pl.ds(0, kvw)] = dw_ref[:, pl.ds(*layout["kv"])]
+            kv_near[0, :, pl.ds(kvw, state[1])] = dw_ref[:, pl.ds(*state)]
+            copy = remote(
+                kv_near.at[0], kv_near.at[1], kv_send.at[0], kv_recv.at[0], {"tensor": at.t_near}
+            )
+            copy.start()
+            copy.wait()
+            kv_far[0] = kv_near[0] + kv_near[1]
+            copy = remote(
+                kv_far.at[0], kv_far.at[1], kv_send.at[1], kv_recv.at[1], {"tensor": at.t_far}
+            )
+            copy.start()
+            copy.wait()
+            kvs[:, pl.ds(0, kvw)] = kv_far[0, :, pl.ds(0, kvw)]
+            kvs[:, pl.ds(kvw, kvw)] = kv_far[1, :, pl.ds(0, kvw)]
+
+            @pl.when(at.t >= 2)
+            def _():
+                kvs[:, pl.ds(0, kvw)] = kv_far[1, :, pl.ds(0, kvw)]
+                kvs[:, pl.ds(kvw, kvw)] = kv_far[0, :, pl.ds(0, kvw)]
+
+            kvs[:, pl.ds(2 * kvw, state[1])] = (
+                kv_far[0, :, pl.ds(kvw, state[1])] + kv_far[1, :, pl.ds(kvw, state[1])]
+            )
+    for scatter in scatters:
+        scatter.drain()
+    for c in range(2):
+        back.drain(c)
+
+
+def leave(
+    devices, tensor, layout, pieces, x, gh, gain, w_all, nx, d_in, gb, a, nf, dgu, og, act, small
+):
+    seqs, sub, width = x.shape
+    span = sub * tensor
+    depth = width // devices
+    columns = w_all.shape[1]
+    kvw, state = layout["kv"][1], layout["state"][1]
+    shape = jax.ShapeDtypeStruct
+    vmem = pl.BlockSpec(memory_space=pltpu.VMEM)
+    dma = pltpu.SemaphoreType.DMA
+    own = (seqs, sub, width)
+    rounds = devices.bit_length() - 1
+    block = (devices // 2 * depth, columns)
+    return pl.pallas_call(
+        partial(leave_kernel, devices, layout, pieces),
+        out_shape=(
+            shape(own, F32),
+            shape((depth, columns), F32),
+            shape(small.shape, F32),
+            shape((depth, 2 * kvw + state), F32),
+        ),
+        in_specs=[vmem] * 13,
+        out_specs=(vmem,) * 4,
+        scratch_shapes=[
+            pltpu.VMEM((seqs, span, width), BF16),
+            pltpu.VMEM((2,) + own, BF16),
+            pltpu.VMEM(own, BF16),
+            pltpu.VMEM((width, columns), BF16),
+            pltpu.VMEM(block, BF16),
+            pltpu.VMEM(block, BF16),
+            pltpu.VMEM(block, BF16),
+            pltpu.VMEM((2, 8, width), F32),
+            pltpu.VMEM((2, 8, width), F32),
+            pltpu.VMEM((rounds, 2) + small.shape, F32),
+            pltpu.VMEM((2, depth, kvw + state), F32),
+            pltpu.VMEM((2, depth, kvw + state), F32),
+            dma((2, 3)),
+            dma((2, 4)),
+            dma((2,)),
+            dma((2,)),
+            dma((rounds,)),
+            dma((rounds,)),
+            dma((2,)),
+            dma((2,)),
+        ]
+        + line_scatter_sems(devices) * len(pieces),
+        compiler_params=pltpu.CompilerParams(
+            collective_id=2, has_side_effects=True, vmem_limit_bytes=VMEM_BYTES
+        ),
+        name="leave",
+    )(x, gh, gain, w_all, nx, d_in, gb, a, nf, dgu, og, act, small)
 
 
 def as_sent(array):
@@ -90,10 +872,6 @@
     return jnp.concatenate(
         [first_half * cosine - second_half * sine, second_half * cosine + first_half * sine], -1
     )
-
-
-def rms_norm(values, gain):
-    return values * lax.rsqrt(jnp.mean(values * values, -1, keepdims=True) + EPSILON) * gain
 
 
 def conv_apply(extended, weight, bias, seg_ext, seg_span):
@@ -197,30 +975,57 @@
     state_dim = state_input_weight.shape[1] // 2
     edge_rows = conv_mixer.shape[0] - 1
     scale = 1.0 / math.sqrt(head_dim)
-    gathered = (
-        lax.all_gather(query_weight, "dp", axis=0, tiled=True),
-        lax.all_gather(keyvalue_weight, "dp", axis=0, tiled=True),
-        lax.all_gather(attention_output_weight, "dp", axis=1, tiled=True),
-        lax.all_gather(mixer_input_weight, "dp", axis=0, tiled=True),
-        lax.all_gather(state_input_weight, "dp", axis=0, tiled=True),
-        lax.all_gather(step_weight, "dp", axis=0, tiled=True),
-        lax.all_gather(mixer_output_weight, "dp", axis=1, tiled=True),
-        lax.all_gather(gate_up_weight, "dp", axis=0, tiled=True),
-        lax.all_gather(down_weight, "dp", axis=1, tiled=True),
-    )
-    (
-        gathered_query_weight,
-        full_keyval,
-        gathered_attention_weight,
-        gathered_mixer_input_weight,
-        gathered_state_input_weight,
-        gathered_step_weight,
-        gathered_mixer_output_weight,
-        gathered_gate_up_weight,
-        gathered_down_weight,
-    ) = gathered
     keyval_index = tensor_rank * KVH // tensor_count
-    keyvalue_local = lax.dynamic_index_in_dim(full_keyval, keyval_index, 1, keepdims=False)
+    keyvalue_local = lax.dynamic_index_in_dim(keyvalue_weight, keyval_index, 1, keepdims=False)
+    ff = down_weight.shape[0]
+    depth = query_weight.shape[0]
+    layout = {}
+    columns = 0
+    for name, size in (
+        ("q", query_width),
+        ("kv", 2 * head_dim),
+        ("step", LANES),
+        ("x", mixer_width),
+        ("state", 2 * state_dim),
+        ("z", mixer_width),
+        ("out", query_width + mixer_width),
+        ("gu", 2 * ff),
+        ("down", ff),
+    ):
+        layout[name] = (columns, size)
+        columns += size
+    layout["in"] = (0, layout["out"][0])
+    w_packed = jnp.concatenate(
+        [
+            query_weight,
+            keyvalue_local,
+            jnp.pad(step_weight, ((0, 0), (0, LANES - mixer_local))),
+            mixer_input_weight[:, 1],
+            state_input_weight,
+            mixer_input_weight[:, 0],
+            jnp.concatenate([attention_output_weight, mixer_output_weight], 0).T,
+            gate_up_weight.reshape(depth, 2 * ff),
+            down_weight.T,
+        ],
+        1,
+    )
+    early = (0, layout["z"][0])
+    w_all, span_normed_input, span_gradient, projected = enter(
+        shard_count,
+        tensor_count,
+        (early, layout["z"], layout["out"], layout["gu"], layout["down"]),
+        layout["out"][0],
+        resid_in,
+        out_grad,
+        input_gain[None, :],
+        w_packed,
+    )
+
+    def columns_of(array, name):
+        first, size = layout[name]
+        return array[..., first : first + size]
+
+    projected = projected.reshape(sequences, span_rows, -1)
     first_row = shard_rank * span_rows
     query_pos = first_row + jnp.arange(span_rows, dtype=jnp.int32)
     positions = query_pos.astype(jnp.float32)
@@ -229,14 +1034,6 @@
     seg_ext = lax.dynamic_slice_in_dim(seg_padded, first_row, span_rows + edge_rows, 1)
     seg_prev = seg_ext[:, edge_rows - 1]
 
-    def gather_rows(shard_rows):
-        return lax.all_gather(shard_rows, "tensor", axis=1, tiled=True)
-
-    def sum_rows(partial_rows):
-        return lax.psum_scatter(
-            partial_rows.astype(jnp.bfloat16), "tensor", scatter_dimension=1, tiled=True
-        ).astype(jnp.float32)
-
     def tensor_total(partial_value):
         return jax.tree.map(
             lambda part: part.astype(jnp.float32), lax.psum(as_sent(partial_value), "tensor")
@@ -252,15 +1049,8 @@
         causal = (key_pos[None, :] <= query_pos[:, None])[None, None]
         return causal & (seg_span[:, None, :, None] == segment_ids[:, None, None, :])
 
-    x_float = resid_in.astype(jnp.float32)
-    normed_input = rms_norm(x_float, input_gain).astype(jnp.bfloat16)
-    span_normed_input = gather_rows(normed_input)
-    query_projected = jnp.einsum(
-        "mbn,nf->mbf", span_normed_input, gathered_query_weight, preferred_element_type=jnp.float32
-    )
-    keyvalue_projected = jnp.einsum(
-        "mbn,nf->mbf", span_normed_input, keyvalue_local, preferred_element_type=jnp.float32
-    )
+    query_projected = columns_of(projected, "q")
+    keyvalue_projected = columns_of(projected, "kv")
     queries = rotate(
         query_projected.reshape(sequences, span_rows, local_heads, head_dim), positions, 1.0
     ).astype(jnp.bfloat16)
@@ -306,29 +1096,10 @@
     attention_reduced = attention_rows.reshape(sequences, span_rows, query_width).astype(
         jnp.bfloat16
     )
-    attn_part = jnp.einsum(
-        "uqn,nh->uqh",
-        attention_reduced,
-        gathered_attention_weight,
-        preferred_element_type=jnp.float32,
-    )
-    mixed_rows = jnp.einsum(
-        "uxo,ofw->uxfw",
-        span_normed_input,
-        gathered_mixer_input_weight,
-        preferred_element_type=jnp.float32,
-    ).astype(jnp.bfloat16)
-    gate_z = mixed_rows[:, :, 0]
-    mixer_x = mixed_rows[:, :, 1]
-    state_projected = jnp.einsum(
-        "mbn,nf->mbf",
-        span_normed_input,
-        gathered_state_input_weight,
-        preferred_element_type=jnp.float32,
-    ).astype(jnp.bfloat16)
-    step_unactivated = jnp.einsum(
-        "qji,ig->qjg", span_normed_input, gathered_step_weight, preferred_element_type=jnp.float32
-    )
+    gate_z = columns_of(projected, "z").astype(jnp.bfloat16)
+    mixer_x = columns_of(projected, "x").astype(jnp.bfloat16)
+    state_projected = columns_of(projected, "state").astype(jnp.bfloat16)
+    step_unactivated = columns_of(projected, "step")[..., :mixer_local]
     edge_x, edge_state = from_behind(
         (mixer_x[:, span_rows - edge_rows :], state_projected[:, span_rows - edge_rows :]), "dp", 1
     )
@@ -369,81 +1140,26 @@
     square_total = tensor_total(jnp.sum(gated * gated, -1, keepdims=True))
     norm_scale = lax.rsqrt(square_total / mixer_total + EPSILON)
     mixer_normed_input = (gated * norm_scale * mixer_gain).astype(jnp.bfloat16)
-    mixer_part = jnp.einsum(
-        "uqn,nh->uqh",
-        mixer_normed_input,
-        gathered_mixer_output_weight,
-        preferred_element_type=jnp.float32,
-    )
-    branch_output = sum_rows(attn_part + mixer_part)
-    hidden_rows = x_float + branch_output
-    normed_feedforward = rms_norm(hidden_rows, ffn_gain).astype(jnp.bfloat16)
-    span_feedforward = gather_rows(normed_feedforward)
-    gate_up_rows = jnp.einsum(
-        "pjn,nrt->pjrt",
-        span_feedforward,
-        gathered_gate_up_weight,
-        preferred_element_type=jnp.float32,
-    )
-    gate_value = gate_up_rows[:, :, 0]
-    up_value = gate_up_rows[:, :, 1]
-    sigmoid_gate = jax.nn.sigmoid(gate_value)
-    swiglu_activated = (gate_value * sigmoid_gate * up_value).astype(jnp.bfloat16)
-    ffn_out = sum_rows(
-        jnp.einsum(
-            "axt,tz->axz",
-            swiglu_activated,
-            gathered_down_weight,
-            preferred_element_type=jnp.float32,
-        )
-    )
-    block_out = (hidden_rows + ffn_out).astype(jnp.bfloat16)
-    grad_out = out_grad.astype(jnp.float32)
-    span_gradient = gather_rows(out_grad)
-    activation_gradient = jnp.einsum(
-        "ikm,nm->ikn", span_gradient, gathered_down_weight, preferred_element_type=jnp.float32
-    )
-    down_gradient = jnp.einsum(
-        "ukz,ukt->zt", swiglu_activated, span_gradient, preferred_element_type=jnp.float32
-    )
-    grad_gate = (
-        activation_gradient * up_value * sigmoid_gate * (1.0 + gate_value * (1.0 - sigmoid_gate))
-    )
-    grad_up = activation_gradient * gate_value * sigmoid_gate
-    gate_up_gradient = jnp.stack([grad_gate, grad_up], 2).astype(jnp.bfloat16)
-    grad_gate_up_w = jnp.einsum(
-        "wbm,wbpe->mpe", span_feedforward, gate_up_gradient, preferred_element_type=jnp.float32
-    )
-    grad_normed_ffn = sum_rows(
-        jnp.einsum(
-            "xirp,zrp->xiz",
-            gate_up_gradient,
-            gathered_gate_up_weight,
-            preferred_element_type=jnp.float32,
-        )
-    )
-    _, ffn_pull = jax.vjp(rms_norm, hidden_rows, ffn_gain)
-    grad_hidden_norm, grad_ffn_gain = ffn_pull(grad_normed_ffn)
-    grad_hidden = grad_out + grad_hidden_norm
-    span_branch_output = gather_rows(grad_hidden.astype(jnp.bfloat16))
-    grad_attention = jnp.einsum(
-        "irh,yh->iry",
-        span_branch_output,
-        gathered_attention_weight,
-        preferred_element_type=jnp.float32,
-    )
-    grad_attn_out = jnp.einsum(
-        "nyu,nyb->ub", attention_reduced, span_branch_output, preferred_element_type=jnp.float32
-    )
-    grad_mixer_norm = jnp.einsum(
-        "irh,yh->iry",
-        span_branch_output,
-        gathered_mixer_output_weight,
-        preferred_element_type=jnp.float32,
-    )
-    grad_mixer_out = jnp.einsum(
-        "nyu,nyb->ub", mixer_normed_input, span_branch_output, preferred_element_type=jnp.float32
-    )
+    tokens = sequences * span_rows
+    branch_low = jnp.concatenate([attention_reduced, mixer_normed_input], -1).reshape(tokens, -1)
+    block_out, grad_hidden, grad_branch, span_feedforward, activated, grad_gate_up, ffn_gain_part = (
+        feed_forward(
+            shard_count,
+            tensor_count,
+            layout,
+            resid_in,
+            branch_low,
+            span_gradient,
+            out_grad,
+            ffn_gain[None, :],
+            w_all,
+        )
+    )
+    grad_low = jnp.einsum(
+        "irh,hy->iry", grad_branch, columns_of(w_all, "out"), preferred_element_type=jnp.float32
+    )
+    grad_attention = grad_low[..., :query_width]
+    grad_mixer_norm = grad_low[..., query_width:]
     grad_attn_low = grad_attention.reshape(sequences, span_rows, local_heads, head_dim).astype(
         jnp.bfloat16
     )
@@ -542,124 +1258,82 @@
     grad_state_pre = grad_ext_state[:, edge_rows:] + jnp.pad(back_state, tail_pad)
     mixed_gradient = jnp.stack([grad_gate_z, grad_mixer_x], 2).astype(jnp.bfloat16)
     state_reduced_gradient = grad_state_pre.astype(jnp.bfloat16)
-    grad_rows_part = jnp.einsum(
-        "fvp,jp->fvj",
-        query_projected_gradient,
-        gathered_query_weight,
-        preferred_element_type=jnp.float32,
-    )
-    grad_rows_part = grad_rows_part + jnp.einsum(
-        "fvp,jp->fvj", keyvalue_reduced_gradient, keyvalue_local, preferred_element_type=jnp.float32
-    )
-    grad_rows_part = grad_rows_part + jnp.einsum(
-        "ofgk,ugk->ofu",
-        mixed_gradient,
-        gathered_mixer_input_weight,
-        preferred_element_type=jnp.float32,
-    )
-    grad_rows_part = grad_rows_part + jnp.einsum(
-        "fvp,jp->fvj",
-        state_reduced_gradient,
-        gathered_state_input_weight,
-        preferred_element_type=jnp.float32,
-    )
-    grad_rows_part = grad_rows_part + jnp.einsum(
-        "bmo,eo->bme",
-        step_reduced_gradient,
-        gathered_step_weight,
-        preferred_element_type=jnp.float32,
-    )
-    grad_normed = sum_rows(grad_rows_part)
-    _, input_pull = jax.vjp(rms_norm, x_float, input_gain)
-    grad_x_norm, grad_input_gain = input_pull(grad_normed)
-    resid_grad = grad_hidden + grad_x_norm
-    grad_query_w = jnp.einsum(
-        "frh,frp->hp",
+    grad_in = jnp.concatenate(
+        [
+            query_projected_gradient,
+            keyvalue_reduced_gradient,
+            jnp.pad(step_reduced_gradient, ((0, 0), (0, 0), (0, LANES - mixer_local))),
+            grad_mixer_x.astype(jnp.bfloat16),
+            state_reduced_gradient,
+            grad_gate_z.astype(jnp.bfloat16),
+        ],
+        -1,
+    ).reshape(tokens, -1)
+
+    def row(array):
+        return jnp.pad(array, ((0, 0), (0, model_width - array.shape[1])))
+
+    def lanes(array):
+        return jnp.pad(array[None, :], ((0, 0), (0, LANES - array.shape[0])))
+
+    small = jnp.concatenate(
+        [
+            jnp.zeros((1, model_width), jnp.float32),
+            ffn_gain_part,
+            row(grad_state_w),
+            row(grad_state_b[None, :]),
+            jnp.zeros((1, model_width), jnp.float32),
+            row(grad_conv_w),
+            row(grad_conv_b[None, :]),
+            row(grad_mixer_gain[None, :]),
+            row(jnp.concatenate([lanes(grad_step_bias), lanes(grad_decay_log), lanes(grad_skip)], 1)),
+            jnp.zeros((1, model_width), jnp.float32),
+        ],
+        0,
+    )
+    resid_grad, weight_grads, sums, replicated = leave(
+        shard_count,
+        tensor_count,
+        layout,
+        (layout["in"], layout["out"], layout["gu"], layout["down"]),
+        resid_in,
+        grad_hidden,
+        input_gain[None, :],
+        w_all,
         span_normed_input,
-        query_projected_gradient,
-        preferred_element_type=jnp.float32,
-    )
-    grad_keyval_own = jnp.einsum(
-        "frh,frp->hp",
-        span_normed_input,
-        keyvalue_reduced_gradient,
-        preferred_element_type=jnp.float32,
-    )
-    grad_mixer_in = jnp.einsum(
-        "iqf,iqyj->fyj", span_normed_input, mixed_gradient, preferred_element_type=jnp.float32
-    )
-    grad_state_in = jnp.einsum(
-        "frh,frp->hp", span_normed_input, state_reduced_gradient, preferred_element_type=jnp.float32
-    )
-    grad_step_w = jnp.einsum(
-        "njq,njb->qb", span_normed_input, step_reduced_gradient, preferred_element_type=jnp.float32
-    )
-    keyval_full = lax.dynamic_update_index_in_dim(
-        jnp.zeros(full_keyval.shape, jnp.float32), grad_keyval_own, keyval_index, 1
-    )
-    shard_grads = (
-        lax.psum_scatter(grad_query_w, "dp", scatter_dimension=0, tiled=True),
-        lax.psum_scatter(grad_attn_out, "dp", scatter_dimension=1, tiled=True),
-        lax.psum_scatter(grad_mixer_in, "dp", scatter_dimension=0, tiled=True),
-        lax.psum_scatter(grad_step_w, "dp", scatter_dimension=0, tiled=True),
-        lax.psum_scatter(grad_mixer_out, "dp", scatter_dimension=1, tiled=True),
-        lax.psum_scatter(grad_gate_up_w, "dp", scatter_dimension=0, tiled=True),
-        lax.psum_scatter(down_gradient, "dp", scatter_dimension=1, tiled=True),
-        lax.psum_scatter(keyval_full, "dp", scatter_dimension=0, tiled=True),
-        lax.psum_scatter(grad_state_in, "dp", scatter_dimension=0, tiled=True),
-    )
-    keyval_rows, state_rows = tensor_total((shard_grads[7], shard_grads[8]))
-
-    def placed(local_value, axis_number):
-        full_shape = list(local_value.shape)
-        full_shape[axis_number] = full_shape[axis_number] * tensor_count
-        start_index = tensor_rank * local_value.shape[axis_number]
-        return lax.dynamic_update_slice_in_dim(
-            jnp.zeros(full_shape, jnp.float32), local_value, start_index, axis_number
-        )
-
-    def take_slot(full_value, axis_number, piece_size):
-        return lax.dynamic_slice_in_dim(
-            full_value, tensor_rank * piece_size, piece_size, axis_number
-        )
-
-    summed = lax.psum(
-        (
-            grad_input_gain,
-            grad_ffn_gain,
-            placed(grad_conv_w, 1),
-            placed(grad_conv_b, 0),
-            placed(grad_step_bias, 0),
-            placed(grad_decay_log, 0),
-            placed(grad_skip, 0),
-            placed(grad_mixer_gain, 0),
-            grad_state_w,
-            grad_state_b,
-        ),
-        ("dp", "tensor"),
-    )
+        grad_in,
+        grad_branch,
+        branch_low,
+        span_feedforward,
+        grad_gate_up,
+        span_gradient,
+        activated,
+        small,
+    )
+    out_grads = columns_of(weight_grads, "out").T
+    kv_width = 2 * head_dim
     return (
         block_out,
         resid_grad,
-        summed[0],
-        summed[1],
-        shard_grads[0],
-        keyval_rows,
-        shard_grads[1],
-        shard_grads[2],
-        state_rows,
-        shard_grads[3],
-        take_slot(summed[2], 1, mixer_width),
-        take_slot(summed[3], 0, mixer_width),
-        summed[8],
-        summed[9],
-        take_slot(summed[4], 0, mixer_local),
-        take_slot(summed[5], 0, mixer_local),
-        take_slot(summed[6], 0, mixer_local),
-        take_slot(summed[7], 0, mixer_width),
-        shard_grads[4],
-        shard_grads[5],
-        shard_grads[6],
+        sums[0],
+        sums[1],
+        columns_of(weight_grads, "q"),
+        replicated[:, : 2 * kv_width].reshape(depth, 2, kv_width),
+        out_grads[:query_width],
+        jnp.stack([columns_of(weight_grads, "z"), columns_of(weight_grads, "x")], 1),
+        replicated[:, 2 * kv_width :],
+        columns_of(weight_grads, "step")[:, :mixer_local],
+        sums[8:12, :mixer_width],
+        sums[12, :mixer_width],
+        sums[2:6, : 2 * state_dim],
+        sums[6, : 2 * state_dim],
+        sums[14, :mixer_local],
+        sums[14, LANES : LANES + mixer_local],
+        sums[14, 2 * LANES : 2 * LANES + mixer_local],
+        sums[13, :mixer_width],
+        out_grads[query_width:],
+        columns_of(weight_grads, "gu").reshape(depth, 2, ff),
+        columns_of(weight_grads, "down").T,
     )
 
 

time: 1350 us -> 758 us (0.56)
  waiting for transfers between devices: 690 us -> 122 us
  Pallas kernels: 0 us -> 351 us
  blocking collectives: 344 us -> 35.1 us
  matrix products: 120 us -> 60 us
    reduce_scatter x12 -> x0, waiting for transfers between devices: 482 us -> none  [the longest x1 75.3 us: body(): lax.psum_scatter(grad_mixer_in, 'dp', scatter_dimension=0, tiled=True)]
    pallas_call x0 -> x3, Pallas kernels: none -> 351 us  [the longest x1 198 us: leave(): pl.pallas_call(partial(leave_kernel, devices, layout, pieces), out_shape=...]
    all_gather x6 -> x0, blocking collectives: 187 us -> none  [the longest x1 35 us: body(): lax.all_gather(mixer_output_weight, 'dp', axis=1, tiled=True)]
    all_gather x7 -> x0, waiting for transfers between devices: 137 us -> none  [the longest x4 48.1 us: gather_rows(): return lax.all_gather(shard_rows, 'tensor', axis=1, tiled=True)]
    unnamed x1 -> x0, blocking collectives: 85.6 us -> none
    dot_general x27 -> x1, matrix products: 60.2 us -> 2.25 us  [body(): jnp.einsum('irh,hy->iry', grad_branch, columns_of(w_all, 'out'), preferre...]
    psum x1 -> x0, blocking collectives: 40.9 us -> none  [body(): lax.psum((grad_input_gain, grad_ffn_gain, placed(grad_conv_w, 1), placed(...]
    all_gather x1, waiting for transfers between devices: 0.01 us -> 34.2 us  [prefix(): lax.all_gather(part.astype(kind), axis)]
  transfers between devices with their start and end apart: 28 -> 8, of which waited for: 21 -> 6; matrix products, arithmetic and copies ran while one was open for 16% -> 12% of each run, Pallas kernels for 0% -> 0%
where the time goes in v1:
time: 758 us; the launch traced here: 748 us
  Pallas kernels  351 us (46%)
  waiting for transfers between devices  122 us (16%)
  other arithmetic  84.7 us (11%)
  local copies, waits for them, and re-layouts  72.5 us (10%)
  matrix products  60 us (8%)
  blocking collectives  35.1 us (5%)
  between operations  16 us (2%)
    pallas_call x1, Pallas kernels, leave(): pl.pallas_call(partial(leave_kernel, devices, layout, pieces), out_shape=...  198 us
    pallas_call x1, Pallas kernels, enter(): pl.pallas_call(partial(enter_kernel, devices, pieces, in_width), out_shap...  108 us
    all_gather x1, waiting for transfers between devices, carried_in(): lax.all_gather(a.astype(kind), axis)  58.9 us
    pallas_call x1, Pallas kernels, feed_forward(): pl.pallas_call(partial(ffn_kernel, devices, layout), out_shape=(shape(own...  45 us
    all_gather x1, waiting for transfers between devices, prefix(): lax.all_gather(part.astype(kind), axis)  34.2 us
    all_gather x1, blocking collectives, prefix(): lax.all_gather(part.astype(kind), axis)  22.6 us
    unnamed x253, local copies, waits for them, and re-layouts  20.8 us
    reduce_scatter x1, waiting for transfers between devices, body(): lax.psum_scatter(grad_keys_all, 'dp', scatter_dimension=1, tiled=True)  15.4 us
  transfers between devices with their start and end apart: 8, of which 6 were waited for; matrix products, arithmetic and copies ran while one was open for 12% of the time, Pallas kernels for 0%

profile of v1, /device:TPU:0, one launch (start us, length us, event | category | flops | bytes accessed | tf_op | source)
XLA Modules:
  0.0 748.4 jit_solution(3067039187065730801)
XLA Ops:
  14.6 107.9 %enter.1 = (bf16[1024,3456]{1,0:T(8,128)(2,1)}, bf16[4,128,1024]{2,1,0:T(8,128)(2,1)}, bf16[4,128,1024]{2,1,0:T(8,128)(2,1)}, f32[512,1408]{1,0:T(8,128)}) custom-call(bf16[4,32,1024]{2,1,0:T(8,128)(2,1)} %refs_0_.5, bf16[4,32,1024]{2,1,0:T(8,128)(2,1)} %refs_3_.1, f32[1,1024]{1,0:T(1,128)} %bitcast.288, bf16[128,3456]{1,0:T(8,128)(2,1)} %copy-done.33), custom_call_target="tpu_custom_call" | custom-call | tf_op jit(solution)/shard_map/enter/pallas_call | solution.py:452
  122.5 3.4 copy.195
  126.8 2.0 convert.57
  131.1 3.2 collective-permute-start.1
  139.4 2.3 collective-permute-done.1
  147.0 1.8 fusion.70
  148.9 2.1 convolution_convert_fusion.1
  152.8 1.8 copy.197
  156.8 22.6 %all_gather.23 = bf16[8,4,6]{2,1,0:T(4,128)(2,1)} all-gather(bf16[1,4,6]{2,1,0:T(4,128)(2,1)S(1)} %fusion.109), channel_id=1, replica_groups=mesh['dp'=8,'tensor'=4] {'dp'}, dimensions={0}, use_global_device_ids=true | all-gather | bytes 432 | tf_op jit(solution)/shard_map/all_gather | solution.py:817
  182.7 2.5 compare_and_fusion
  185.3 1.8 copy.201
  187.1 5.5 fusion.64
  192.6 2.2 fusion.3
  198.5 34.2 %all-gather.8.cloned.1.call-done = bf16[32,6,64,128]{3,2,1,0:T(8,128)(2,1)} async-done(((bf16[4,6,64,128]{3,2,1,0:T(8,128)(2,1)}), bf16[32,6,64,128]{3,2,1,0:T(8,128)(2,1)}) %all-gather.8.cloned.1.call-update) | async-done | bytes 3145744 | tf_op jit(solution)/shard_map/all_gather | solution.py:817
  232.7 14.8 %while.29 = (s32[]{:T(128)}, f32[4,6,64,128]{3,2,1,0:T(8,128)S(1)}, s32[]{:T(128)}, bf16[8,4,6]{2,1,0:T(4,128)(2,1)}, bf16[8,4,6,64,128]{4,3,2,1,0:T(8,128)(2,1)}, /*index=5*/s32[]{:T(128)}, s32[]{:T(128)}) while((s32[]{:T(128)}, f32[4,6,64,128]{3,2,1,0:T(8,128)S(1)}, s32[]{:T(128)}, bf16[8,4,6]{2,1,0:T(4,128)(2,1)}, ...), condition=%wide.region_4.5_spmd.clone, body=%wide.region_3.4_spmd.clone.sunk | while | flops 983068 | bytes 1966433 | solution.py:834
  247.6 4.2 convolution_bitcast_fusion.3
  251.8 1.9 fusion.26
  254.7 6.1 psum.14
  262.7 2.1 copy.209
  264.8 45.0 %feed_forward.1 = (bf16[4,32,1024]{2,1,0:T(8,128)(2,1)}, f32[4,32,1024]{2,1,0:T(8,128)}, bf16[4,128,1024]{2,1,0:T(8,128)(2,1)}, bf16[4,128,1024]{2,1,0:T(8,128)(...) custom-call(bf16[4,32,1024]{2,1,0:T(8,128)(2,1)} %refs_0_.5, ...), custom_call_target="tpu_custom_call" | custom-call | tf_op jit(solution)/shard_map/feed_forward/pallas_call | solution.py:578
  309.8 2.2 fusion.34
  316.4 3.5 fusion.21
  325.0 2.1 slice.392
  327.1 2.4 copy.265
  329.5 1.9 multiply_reduce_fusion.3
  331.4 6.3 psum.15
  337.8 3.5 multiply_reduce_fusion.2
  341.3 2.1 convolution_convert_fusion
  351.3 5.4 reduce_window_sum.34
  357.4 5.0 fusion.80
  362.4 3.1 copy.218
  365.5 2.2 fusion.30
  368.6 2.5 convolution_bitcast_fusion.6
  371.1 3.9 convolution_bitcast_fusion.5
  376.6 15.4 %reduce-scatter.2.cloned.1.call-done = f32[4,128,128]{1,2,0:T(8,128)} async-done(((f32[4,1024,128]{1,2,0:T(8,128)}), f32[4,128,128]{1,2,0:T(8,128)}) %reduce-scatter.2.cloned.1.call-update) | async-done | bytes 262160 | tf_op jit(solution)/shard_map/reduce_scatter | solution.py:1208
  395.2 58.9 %all-gather.10.cloned.1.call-done = bf16[32,6,64,128]{3,2,1,0:T(8,128)(2,1)} async-done(((bf16[4,6,64,128]{3,2,1,0:T(8,128)(2,1)}), bf16[32,6,64,128]{3,2,1,0:T(8,128)(2,1)}) %all-gather.10.cloned.1.call-update) | async-done | bytes 3145744 | tf_op jit(solution)/shard_map/all_gather | solution.py:842
  454.3 13.2 %while.28 = (s32[]{:T(128)}, f32[4,6,64,128]{3,2,1,0:T(8,128)S(1)}, s32[]{:T(128)}, bf16[8,4,6]{2,1,0:T(4,128)(2,1)}, bf16[8,4,6,64,128]{4,3,2,1,0:T(8,128)(2,1)...) while((s32[]{:T(128)}, f32[4,6,64,128]{3,2,1,0:T(8,128)S(1)}, s32[]{:T(128)}, ...), condition=%wide.region_12.13_spmd, body=%wide.region_11.12_spmd.sunk | while | flops 589854 | bytes 1966475 | solution.py:859
  467.6 4.0 convolution_bitcast_fusion.2
  471.7 3.8 fusion.77
  475.7 5.8 multiply_reduce_fusion
  483.7 5.1 fusion.17
  489.1 4.6 reduce_window_sum.33
  502.9 2.0 concatenate.62.refs_12_
  504.9 9.5 %collective-permute-done.2 = bf16[4,3,384]{1,2,0:T(8,128)(2,1)} collective-permute-done((bf16[4,3,384]{1,2,0:T(8,128)(2,1)S(1)}, bf16[4,3,384]{1,2,0:T(8,128)(2,1)}, u32[]{:S(2)}, u32[]{:S(2)}) %collective-permute-start.2) | collective-permute-done | bytes 9248 | tf_op jit(solution)/shard_map/ppermute | solution.py:811
  514.4 2.2 fusion.88
  516.6 1.9 fusion.96
  519.4 2.5 copy.230
  522.0 197.9 %leave.1 = (f32[4,32,1024]{2,1,0:T(8,128)}, f32[128,3456]{1,0:T(8,128)}, f32[16,1024]{1,0:T(8,128)}, f32[128,512]{1,0:T(8,128)}) custom-call(bf16[4,32,1024]{2,1,0:T(8,128)(2,1)} %refs_0_.5, f32[4,32,1024]{2,1,0:T(8,128)} %get-tuple-element.219.refs_1_, f32[1,1024]{1,0:T(1,128)} %bitcast.289, bf16[1024,3456]{1,0:T(8,128)(2,1)} %get-tuple-element.217.refs_5_.refs_3_, ...), custom_call_target="tpu_custom_call" | custom-call | tf_op jit(solution)/shard_map/leave/pallas_call | solution.py:760
  (423 shorter events, 119.6 us)
Async XLA Ops:
  7.2 6.2 copy-start
  7.2 6.2 copy-start.74
  7.2 6.4 copy-start.68
  7.2 185.3 %all-gather.6.cloned.1.call-start = ((), (), s32[]{:S(2)}) async-start(), calls=%async_computation.1 | async-start | bytes 1179648 | tf_op jit(solution)/shard_map/all_gather | solution.py:1044
  128.8 10.6 %copy-start.11 = (bf16[4,128,1408]{1,2,0:T(8,128)(2,1)}, bf16[4,128,1408]{1,2,0:T(8,128)(2,1)S(1)}, u32[]{:S(2)}) copy-start(bf16[4,128,1408]{1,2,0:T(8,128)(2,1)S(1)} %convert.57) | copy-start | bytes 4325380
  128.8 6.9 copy-start.113
  128.8 6.9 copy-start.41
  128.8 8.0 %copy-start.106 = (f32[6]{0:T(128)S(1)}, f32[6]{0:T(128)}, u32[]{:S(2)}) copy-start(f32[6]{0:T(128)} %param.41) | copy-start | bytes 76
  128.8 8.9 %copy-start.102 = (f32[4,256]{1,0:T(4,128)S(1)}, f32[4,256]{1,0:T(4,128)}, u32[]{:S(2)}) copy-start(f32[4,256]{1,0:T(4,128)} %param.39) | copy-start | bytes 12292
  130.1 7.7 %copy-start.39 = (f32[128,32]{0,1:T(8,128)}, f32[128,32]{0,1:T(8,128)S(1)}, u32[]{:S(2)}) copy-start(f32[128,32]{0,1:T(8,128)S(1)} %get-tuple-element.445) | copy-start | bytes 49156
  130.1 7.7 %copy-start.53 = (f32[128,32]{0,1:T(8,128)}, f32[128,32]{0,1:T(8,128)S(1)}, u32[]{:S(2)}) copy-start(f32[128,32]{0,1:T(8,128)S(1)} %get-tuple-element.444) | copy-start | bytes 49156
  130.2 9.1 %copy-start.99 = (f32[4,384]{1,0:T(4,128)S(1)}, f32[4,384]{1,0:T(4,128)}, u32[]{:S(2)}) copy-start(f32[4,384]{1,0:T(4,128)} %param.37) | copy-start | bytes 18436
  130.9 101.8 %all-gather.8.cloned.1.call-start = ((), (), s32[]{:S(2)}) async-start(), calls=%async_computation.3 | async-start | bytes 3538944 | tf_op jit(solution)/shard_map/all_gather | solution.py:817
  131.1 10.6 %collective-permute-start.1 = (bf16[4,3,256]{1,2,0:T(8,128)(2,1)S(1)}, bf16[4,3,256]{1,2,0:T(8,128)(2,1)}, u32[]{:S(2)}, u32[]{:S(2)}) collective-permute-start(bf16[4,3,256]{1,2,0:T(8,128)(2,1)S(1)} %slice.375), channel_id=1, source_target_pairs={{0,4},{4,8},{8,12},{12,16},{16,20},{20,24},{24,28},{1,5},{5,9},{9,... | collective-permute-start | bytes 18440 | tf_op jit(solution)/shard_map/ppermute | solution.py:811
  134.4 12.2 %collective-permute-start = (bf16[4,3,384]{1,2,0:T(8,128)(2,1)S(1)}, bf16[4,3,384]{1,2,0:T(8,128)(2,1)S(1)}, u32[]{:S(2)}, u32[]{:S(2)}) collective-permute-start(bf16[4,3,384]{1,2,0:T(8,128)(2,1)S(1)} %slice.369), channel_id=1, source_target_pairs={{0,4},{4,8},{8,12},{12,16},{16,20},{20,24},{24,28},{1,5},{5,9},{9,... | collective-permute-start | bytes 27656 | tf_op jit(solution)/shard_map/ppermute | solution.py:811
  137.8 9.2 %copy-start.55 = (f32[4,128]{1,0:T(4,128)}, f32[4,128]{1,0:T(4,128)S(1)}, u32[]{:S(2)}) copy-start(f32[4,128]{1,0:T(4,128)S(1)} %get-tuple-element.432) | copy-start | bytes 6148
  137.8 9.2 %copy-start.57 = (f32[4,128]{1,0:T(4,128)}, f32[4,128]{1,0:T(4,128)S(1)}, u32[]{:S(2)}) copy-start(f32[4,128]{1,0:T(4,128)S(1)} %get-tuple-element.433) | copy-start | bytes 6148
  137.8 9.2 %copy-start.59 = (f32[4,128]{1,0:T(4,128)}, f32[4,128]{1,0:T(4,128)S(1)}, u32[]{:S(2)}) copy-start(f32[4,128]{1,0:T(4,128)S(1)} %get-tuple-element.434) | copy-start | bytes 6148
  137.8 9.1 %copy-start.61 = (f32[4,128]{1,0:T(4,128)}, f32[4,128]{1,0:T(4,128)S(1)}, u32[]{:S(2)}) copy-start(f32[4,128]{1,0:T(4,128)S(1)} %get-tuple-element.435) | copy-start | bytes 6148
  139.3 9.6 %copy-start.43 = (f32[4,128,6]{1,2,0:T(8,128)}, f32[4,128,6]{1,2,0:T(8,128)S(1)}, u32[]{:S(2)}) copy-start(f32[4,128,6]{1,2,0:T(8,128)S(1)} %select_multiply_fusion.1) | copy-start | bytes 36868
  139.3 7.6 %copy-start.76 = (f32[384]{0:T(512)}, f32[384]{0:T(512)S(1)}, u32[]{:S(2)}) copy-start(f32[384]{0:T(512)S(1)} %get-tuple-element.355) | copy-start | bytes 4612
  139.3 7.6 %copy-start.78 = (f32[384]{0:T(512)}, f32[384]{0:T(512)S(1)}, u32[]{:S(2)}) copy-start(f32[384]{0:T(512)S(1)} %get-tuple-element.356) | copy-start | bytes 4612
  139.3 7.6 %copy-start.80 = (f32[384]{0:T(512)}, f32[384]{0:T(512)S(1)}, u32[]{:S(2)}) copy-start(f32[384]{0:T(512)S(1)} %get-tuple-element.357) | copy-start | bytes 4612
  139.4 7.6 %copy-start.82 = (f32[384]{0:T(512)}, f32[384]{0:T(512)S(1)}, u32[]{:S(2)}) copy-start(f32[384]{0:T(512)S(1)} %get-tuple-element.358) | copy-start | bytes 4612
  148.8 102.9 %copy-start.4 = (f32[4,128,384]{1,2,0:T(8,128)}, f32[4,128,384]{1,2,0:T(8,128)S(1)}, u32[]{:S(2)}) copy-start(f32[4,128,384]{1,2,0:T(8,128)S(1)} %get-tuple-element.393) | copy-start | bytes 2359300
  148.9 7.6 %copy-start.42 = (s32[4,1024]{1,0:T(4,128)S(1)}, s32[4,1024]{1,0:T(4,128)}, u32[]{:S(2)}) copy-start(s32[4,1024]{1,0:T(4,128)} %param.27) | copy-start | bytes 49156
  148.9 7.6 %copy-start.64 = (s32[4,128]{1,0:T(4,128)S(1)}, s32[4,128]{1,0:T(4,128)}, u32[]{:S(2)}) copy-start(s32[4,128]{1,0:T(4,128)} %copy-done.63) | copy-start | bytes 6148
  148.9 7.8 %copy-start.98 = (f32[4,6]{1,0:T(4,128)S(1)}, f32[4,6]{1,0:T(4,128)}, u32[]{:S(2)}) copy-start(f32[4,6]{1,0:T(4,128)} %get-tuple-element.354) | copy-start | bytes 292
  148.9 30.5 %copy-start.112 = (s32[128]{0:T(128)S(1)}, s32[128]{0:T(128)}, u32[]{:S(2)}) copy-start(s32[128]{0:T(128)} %get-tuple-element.450) | copy-start | bytes 1540
  151.0 30.1 %copy-start.40 = (f32[128,32]{0,1:T(8,128)S(1)}, f32[128,32]{0,1:T(8,128)}, u32[]{:S(2)}) copy-start(f32[128,32]{0,1:T(8,128)} %copy-done.39) | copy-start | bytes 49156
  151.0 30.1 %copy-start.54 = (f32[128,32]{0,1:T(8,128)S(1)}, f32[128,32]{0,1:T(8,128)}, u32[]{:S(2)}) copy-start(f32[128,32]{0,1:T(8,128)} %copy-done.53) | copy-start | bytes 49156
  151.0 241.0 %reduce-scatter.2.cloned.1.call-start = ((), (), s32[]{:S(2)}) async-start(), calls=%async_computation.2 | async-start | bytes 2359296 | tf_op jit(solution)/shard_map/reduce_scatter | solution.py:1208
  156.7 22.8 %copy-start.100 = (f32[4]{0:T(128)}, f32[4]{0:T(128)S(1)}, u32[]{:S(2)}) copy-start(f32[4]{0:T(128)S(1)} %convert_reduce_fusion) | copy-start | bytes 52
  253.8 7.0 copy-start.75
  254.7 74.8 %copy-start.10 = (f32[4,128,384]{1,2,0:T(8,128)}, f32[4,128,384]{1,2,0:T(8,128)S(1)}, u32[]{:S(2)}) copy-start(f32[4,128,384]{1,2,0:T(8,128)S(1)} %get-tuple-element.388) | copy-start | bytes 2359300
  325.0 129.2 %all-gather.10.cloned.1.call-start = ((), (), s32[]{:S(2)}) async-start(), calls=%async_computation.4 | async-start | bytes 3538944 | tf_op jit(solution)/shard_map/all_gather | solution.py:842
  341.3 27.3 %copy-start.2 = (f32[4,128,384]{1,2,0:T(8,128)}, f32[4,128,384]{1,2,0:T(8,128)S(1)}, u32[]{:S(2)}) copy-start(f32[4,128,384]{1,2,0:T(8,128)S(1)} %get-tuple-element.382) | copy-start | bytes 2359300
  475.7 5.8 copy-start.16
  475.7 5.8 copy-start.56
  475.7 5.8 copy-start.58
  475.7 5.8 copy-start.60
  483.7 10.2 %copy-start.7 = (f32[4,131,256]{1,2,0:T(8,128)S(1)}, f32[4,131,256]{1,2,0:T(8,128)}, u32[]{:S(2)}) copy-start(f32[4,131,256]{1,2,0:T(8,128)} %copy-done.6) | copy-start | bytes 1609732
  483.7 10.2 %copy-start.30 = (f32[4,128,256]{1,2,0:T(8,128)S(1)}, f32[4,128,256]{1,2,0:T(8,128)}, u32[]{:S(2)}) copy-start(f32[4,128,256]{1,2,0:T(8,128)} %get-tuple-element.396) | copy-start | bytes 1572868
  483.7 10.1 %copy-start.32 = (f32[4,128,128]{1,2,0:T(8,128)S(1)}, f32[4,128,128]{1,2,0:T(8,128)}, u32[]{:S(2)}) copy-start(f32[4,128,128]{1,2,0:T(8,128)} %convolution_bitcast_fusion.6) | copy-start | bytes 786436
  483.7 10.1 %copy-start.45 = (f32[4,128,128]{1,2,0:T(8,128)S(1)}, f32[4,128,128]{1,2,0:T(8,128)}, u32[]{:S(2)}) copy-start(f32[4,128,128]{1,2,0:T(8,128)} %convolution_bitcast_fusion.5) | copy-start | bytes 786436
  496.6 20.0 %collective-permute-start.3 = (bf16[4,3,256]{1,2,0:T(8,128)(2,1)}, bf16[4,3,256]{1,2,0:T(8,128)(2,1)}, u32[]{:S(2)}, u32[]{:S(2)}) collective-permute-start(bf16[4,3,256]{1,2,0:T(8,128)(2,1)} %slice.492), channel_id=1, source_target_pairs={{4,0},{8,4},{12,8},{16,12},{20,16},{24,20},{28,24},{5,1},{9,5},{13... | collective-permute-start | bytes 18440 | tf_op jit(solution)/shard_map/ppermute | solution.py:811
  499.7 14.7 %collective-permute-start.2 = (bf16[4,3,384]{1,2,0:T(8,128)(2,1)S(1)}, bf16[4,3,384]{1,2,0:T(8,128)(2,1)}, u32[]{:S(2)}, u32[]{:S(2)}) collective-permute-start(bf16[4,3,384]{1,2,0:T(8,128)(2,1)S(1)} %slice.491), channel_id=1, source_target_pairs={{4,0},{8,4},{12,8},{16,12},{20,16},{24,20},{28,24},{5,1},{9,5},{13... | collective-permute-start | bytes 27656 | tf_op jit(solution)/shard_map/ppermute | solution.py:811
  501.1 17.5 %copy-start.31 = (bf16[4,128,384]{1,2,0:T(8,128)(2,1)S(1)}, bf16[4,128,384]{1,2,0:T(8,128)(2,1)}, u32[]{:S(2)}) copy-start(bf16[4,128,384]{1,2,0:T(8,128)(2,1)} %get-tuple-element.397) | copy-start | bytes 1179652
  (76 other events, 248.1 us)
Sparse Core Ops, SparseCore 0:
  131.0 39.0 all-gather.5
  172.8 59.8 all-gather.7
  325.1 66.9 reduce-scatter.1
  394.7 59.4 all-gather.9

commit v2 on v1

v2 whole, which is shorter than its diff:
```python
from functools import partial
import math

import jax
import jax.numpy as jnp
import numpy as np
from jax import lax
from jax.experimental import pallas as pl
from jax.experimental.pallas import tpu as pltpu
from jax.sharding import PartitionSpec as P

KVH = 2
EPSILON = 1e-05
ROTARY_BASE = 100000000000.0
MASKED = -1e30
MATMUL_EXACTNESS = lax.Precision.HIGHEST
LANES = 128
F32 = jnp.float32
BF16 = jnp.bfloat16
VMEM_BYTES = 62 * 2**20


def dot_nn(a, b):
    return lax.dot_general(a, b, (((1,), (0,)), ((), ())), preferred_element_type=F32)


def dot_nt(a, b):
    return lax.dot_general(a, b, (((1,), (1,)), ((), ())), preferred_element_type=F32)


def dot_tn(a, b):
    return lax.dot_general(a, b, (((0,), (0,)), ((), ())), preferred_element_type=F32)


def remote(src, dst, send_sem, recv_sem, where):
    return pltpu.make_async_remote_copy(
        src_ref=src,
        dst_ref=dst,
        send_sem=send_sem,
        recv_sem=recv_sem,
        device_id=where,
        device_id_type=pl.DeviceIdType.MESH,
    )


class Place:
    def __init__(self, devices):
        self.devices = devices
        self.lines = devices // 2
        self.dp = lax.axis_index("dp")
        self.t = lax.axis_index("tensor")
        self.z = lax.div(self.dp, 2)
        self.p = lax.rem(self.dp, 2)
        self.pair = self.dp + 1 - 2 * self.p
        self.t_near = self.t + 1 - 2 * lax.rem(self.t, 2)
        self.t_far = lax.rem(self.t + 2, 4)
        self.t_both = lax.rem(self.t_near + 2, 4)
        self.first = self.z == 0
        self.last = self.z == self.lines - 1

    def flips(self):
        bit = 1
        while bit < self.devices:
            yield self.dp + bit - 2 * bit * lax.rem(lax.div(self.dp, bit), 2)
            bit *= 2

    def greet(self, line=False, tensor=False, flips=False):
        barrier = pltpu.get_barrier_semaphore()
        count = 0

        def signal(**where):
            pl.semaphore_signal(
                barrier, inc=1, device_id=where, device_id_type=pl.DeviceIdType.MESH
            )

        if tensor:
            signal(tensor=self.t_near)
            signal(tensor=self.t_far)
            count = count + 2
        if line:
            signal(dp=self.pair)
            count = count + 1

            @pl.when(jnp.logical_not(self.first))
            def _():
                signal(dp=self.dp - 2)

            @pl.when(jnp.logical_not(self.last))
            def _():
                signal(dp=self.dp + 2)

        if flips:
            for other in self.flips():
                signal(dp=other)
                count = count + 1
        if line:
            count = count + 2
            count = count - self.first.astype(jnp.int32) - self.last.astype(jnp.int32)
        pl.semaphore_wait(barrier, count)


class LineGather:
    def __init__(self, place, view, recv, right, left, pair):
        self.at, self.view = place, view
        self.recv, self.right, self.left, self.side = recv, right, left, pair

    def copy(self, block, sem, where):
        ref = self.view(block)
        return remote(ref, ref, sem, self.recv.at[block], where)

    def send_right(self, zz):
        return self.copy(zz * 2 + self.at.p, self.right.at[zz], {"dp": self.at.dp + 2})

    def send_left(self, zz):
        return self.copy(zz * 2 + self.at.p, self.left.at[zz], {"dp": self.at.dp - 2})

    def send_pair(self, zz):
        return self.copy(zz * 2 + self.at.p, self.side.at[zz], {"dp": self.at.pair})

    def arrived(self, block):
        self.copy(block, self.side.at[0], {"dp": self.at.pair}).wait_recv()

    def start(self):
        at = self.at
        pl.when(jnp.logical_not(at.last))(lambda: self.send_right(at.z).start())
        pl.when(jnp.logical_not(at.first))(lambda: self.send_left(at.z).start())
        self.send_pair(at.z).start()

    def step(self, s):
        at = self.at
        low, high = at.z - 1 - s, at.z + 1 + s

        @pl.when(low >= 0)
        def _():
            self.arrived(low * 2 + at.p)
            pl.when(jnp.logical_not(at.last))(lambda: self.send_right(low).start())
            self.send_pair(low).start()

        @pl.when(high < at.lines)
        def _():
            self.arrived(high * 2 + at.p)
            pl.when(jnp.logical_not(at.first))(lambda: self.send_left(high).start())
            self.send_pair(high).start()

    def finish(self):
        at = self.at

        @pl.loop(0, at.lines)
        def _(zz):
            self.arrived(zz * 2 + 1 - at.p)

    def drain(self):
        at = self.at

        @pl.loop(0, at.lines)
        def _(zz):
            self.send_pair(zz).wait_send()

            @pl.when(jnp.logical_and(zz <= at.z, jnp.logical_not(at.last)))
            def _():
                self.send_right(zz).wait_send()

            @pl.when(jnp.logical_and(zz >= at.z, jnp.logical_not(at.first)))
            def _():
                self.send_left(zz).wait_send()


class LineScatter:
    def __init__(self, place, part, got, right, left, sems, causal=False):
        self.at, self.part = place, part
        self.got, self.right, self.left = got, right, left
        self.causal = causal
        (
            self.pair_send,
            self.pair_recv,
            self.right_send,
            self.right_recv,
            self.left_send,
            self.left_recv,
        ) = sems

    def pair_copy(self, zz):
        src = self.part(zz * 2 + 1 - self.at.p)
        return remote(
            src, self.got(zz), self.pair_send.at[zz], self.pair_recv.at[zz], {"dp": self.at.pair}
        )

    def right_copy(self, zz):
        src = self.part(zz * 2 + self.at.p)
        return remote(
            src,
            self.right(zz),
            self.right_send.at[zz],
            self.right_recv.at[zz],
            {"dp": self.at.dp + 2},
        )

    def left_copy(self, zz):
        src = self.part(zz * 2 + self.at.p)
        return remote(
            src, self.left(zz), self.left_send.at[zz], self.left_recv.at[zz], {"dp": self.at.dp - 2}
        )

    def start(self):
        at = self.at

        @pl.loop(0, at.z + 1 if self.causal else at.lines)
        def _(i):
            self.pair_copy(i if self.causal else at.lines - 1 - i).start()

    def add_into(self, ref, *others):
        total = ref[...].astype(F32)
        for other in others:
            total = total + other[...].astype(F32)
        ref[...] = total.astype(BF16)

    def step(self, i):
        at = self.at
        high, low = at.lines - 1 - i, i
        if self.causal:
            self.step_low(low)
            return

        @pl.when(at.z < at.lines // 2)
        def _():
            self.step_high(high)
            self.step_low(low)

        @pl.when(at.z >= at.lines // 2)
        def _():
            self.step_low(low)
            self.step_high(high)

    def step_high(self, high):
        at = self.at

        @pl.when(high > at.z)
        def _():
            self.pair_copy(high).wait_recv()
            ref = self.part(high * 2 + at.p)

            @pl.when(at.first)
            def _():
                self.add_into(ref, self.got(high))

            @pl.when(jnp.logical_not(at.first))
            def _():
                self.right_copy(high).wait_recv()
                self.add_into(ref, self.got(high), self.right(high))

            self.right_copy(high).start()

    def step_low(self, low):
        at = self.at

        @pl.when(low < at.z)
        def _():
            self.pair_copy(low).wait_recv()
            ref = self.part(low * 2 + at.p)

            @pl.when(at.last)
            def _():
                self.add_into(ref, self.got(low))

            @pl.when(jnp.logical_not(at.last))
            def _():
                self.left_copy(low).wait_recv()
                self.add_into(ref, self.got(low), self.left(low))

            self.left_copy(low).start()

    def finish(self, out):
        at = self.at
        self.pair_copy(at.z).wait_recv()
        out[...] = self.part(at.dp)[...].astype(F32) + self.got(at.z)[...].astype(F32)

        if not self.causal:

            @pl.when(jnp.logical_not(at.first))
            def _():
                self.right_copy(at.z).wait_recv()
                out[...] += self.right(at.z)[...].astype(F32)

        @pl.when(jnp.logical_not(at.last))
        def _():
            self.left_copy(at.z).wait_recv()
            out[...] += self.left(at.z)[...].astype(F32)

    def drain(self):
        at = self.at

        @pl.loop(0, at.z + 1 if self.causal else at.lines)
        def _(zz):
            self.pair_copy(zz).wait_send()
            if not self.causal:
                pl.when(zz > at.z)(lambda: self.right_copy(zz).wait_send())
            pl.when(zz < at.z)(lambda: self.left_copy(zz).wait_send())

    def run_causal(self, out):
        @pl.loop(0, self.at.lines - 1)
        def _(s):
            self.step(s)

        self.finish(out)


class RowGather:
    def __init__(self, place, view, send, recv):
        self.at, self.view, self.send, self.recv = place, view, send, recv

    def copy(self, rank, chunk, sem, near):
        ref = self.view(rank, chunk)
        where = {"tensor": self.at.t_near if near else self.at.t_far}
        return remote(ref, ref, self.send.at[chunk, sem], self.recv.at[chunk, rank], where)

    def start(self, chunk):
        self.copy(self.at.t, chunk, 0, False).start()
        self.copy(self.at.t, chunk, 1, True).start()

    def forward(self, chunk):
        self.copy(self.at.t_far, chunk, 2, False).wait_recv()
        self.copy(self.at.t_far, chunk, 2, True).start()

    def finish(self, chunk):
        self.copy(self.at.t_near, chunk, 1, True).wait_recv()
        self.copy(self.at.t_both, chunk, 2, True).wait_recv()

    def drain(self, chunk):
        self.copy(self.at.t, chunk, 0, False).wait_send()
        self.copy(self.at.t, chunk, 1, True).wait_send()
        self.copy(self.at.t_far, chunk, 2, True).wait_send()


class RowScatter:
    def __init__(self, place, view, near_buf, far_buf, send, recv):
        self.at, self.view = place, view
        self.near_buf, self.far_buf = near_buf, far_buf
        self.send, self.recv = send, recv

    def near_copy(self, chunk, which):
        rank = self.at.t_both if which else self.at.t_near
        return remote(
            self.view(rank, chunk),
            self.near_buf(which, chunk),
            self.send.at[chunk, which],
            self.recv.at[chunk, which],
            {"tensor": self.at.t_near},
        )

    def far_copy(self, chunk):
        return remote(
            self.view(self.at.t_far, chunk),
            self.far_buf(chunk),
            self.send.at[chunk, 2],
            self.recv.at[chunk, 2],
            {"tensor": self.at.t_far},
        )

    def start(self, chunk):
        self.near_copy(chunk, 1).start()
        self.near_copy(chunk, 0).start()

    def middle(self, chunk):
        self.near_copy(chunk, 1).wait_recv()
        ref = self.view(self.at.t_far, chunk)
        ref[...] = (ref[...].astype(F32) + self.near_buf(1, chunk)[...].astype(F32)).astype(BF16)
        self.far_copy(chunk).start()

    def finish(self, chunk):
        self.near_copy(chunk, 0).wait_recv()
        total = self.view(self.at.t, chunk)[...].astype(F32) + self.near_buf(0, chunk)[
            ...
        ].astype(F32)
        self.far_copy(chunk).wait_recv()
        return total + self.far_buf(chunk)[...].astype(F32)

    def drain(self, chunk):
        self.near_copy(chunk, 0).wait_send()
        self.near_copy(chunk, 1).wait_send()
        self.far_copy(chunk).wait_send()


def line_gather_sems(devices):
    dma = pltpu.SemaphoreType.DMA
    return [dma((devices,)), dma((devices // 2,)), dma((devices // 2,)), dma((devices // 2,))]


def line_scatter_sems(devices):
    return [pltpu.SemaphoreType.DMA((devices // 2,)) for _ in range(6)]


def rms_rows(values, gain):
    return values * lax.rsqrt(jnp.mean(values * values, -1, keepdims=True) + EPSILON) * gain


def rms_rows_grad(values, gain, grad):
    scale = lax.rsqrt(jnp.mean(values * values, -1, keepdims=True) + EPSILON)
    term = grad * gain
    inner = jnp.mean(values * term, -1, keepdims=True)
    return scale * (term - values * (scale * scale * inner)), grad * values * scale


def ffn_kernel(devices, layout, *refs):
    (
        x_ref, a_ref, og_ref, ogl_ref, gain_ref, w_ref,
        out_ref, gh_ref, gb, nf, act, dgu, gain_grad,
        part, part2, near1, far1, near2, far2, near3, far3, hid,
        send, recv,
    ) = refs
    at = Place(devices)
    seqs, sub, width = x_ref.shape
    span = sub * 4
    half = seqs // 2
    rows = half * span
    out_w, gu_w, dn_w = (pl.ds(*layout[k]) for k in ("out", "gu", "down"))
    ff = layout["down"][1]
    at.greet(tensor=True)

    def rows_of(buf):
        def view(rank, chunk):
            return buf.at[pl.ds(chunk * half, half), pl.ds(pl.multiple_of(rank * sub, sub), sub), :]

        return view

    def parts_of(buf):
        return lambda which, chunk: buf.at[which, pl.ds(chunk * half, half)]

    def part_of(buf):
        return lambda chunk: buf.at[pl.ds(chunk * half, half)]

    branch = RowScatter(at, rows_of(part), parts_of(near1), part_of(far1), send.at[0], recv.at[0])
    ffn = RowScatter(at, rows_of(part2), parts_of(near2), part_of(far2), send.at[1], recv.at[1])
    back = RowScatter(at, rows_of(part), parts_of(near3), part_of(far3), send.at[2], recv.at[2])
    row_nf = RowGather(at, rows_of(nf), send.at[3], recv.at[3])
    row_gb = RowGather(at, rows_of(gb), send.at[4], recv.at[4])
    mine = pl.ds(pl.multiple_of(at.t * sub, sub), sub)
    gain = gain_ref[...]

    def seq_rows(chunk):
        return pl.ds(chunk * half, half)

    def tok_rows(chunk):
        return pl.ds(chunk * rows, rows)

    for c in range(2):
        value = dot_nt(a_ref[tok_rows(c), :], w_ref[:, out_w])
        part[seq_rows(c)] = value.astype(BF16).reshape(half, span, width)
        branch.start(c)
    for c in range(2):
        branch.middle(c)
    for c in range(2):
        hidden = x_ref[seq_rows(c)].astype(F32) + branch.finish(c)
        hid[seq_rows(c)] = hidden
        nf[seq_rows(c), mine, :] = rms_rows(hidden, gain).astype(BF16)
        row_nf.start(c)
    for c in range(2):
        row_nf.forward(c)
    for c in range(2):
        row_nf.finish(c)
        branch.drain(c)
        flat = nf[seq_rows(c)].reshape(rows, width)
        flat_og = og_ref[seq_rows(c)].reshape(rows, width)
        gate_up = dot_nn(flat, w_ref[:, gu_w])
        gate, up = gate_up[:, :ff], gate_up[:, ff:]
        sigmoid = jax.nn.sigmoid(gate)
        grad_act = dot_nn(flat_og, w_ref[:, dn_w])
        act[tok_rows(c), :] = (gate * sigmoid * up).astype(BF16)
        dgu[tok_rows(c), :ff] = (
            grad_act * up * sigmoid * (1.0 + gate * (1.0 - sigmoid))
        ).astype(BF16)
        dgu[tok_rows(c), ff:] = (grad_act * gate * sigmoid).astype(BF16)
        value = dot_nt(dgu[tok_rows(c), :], w_ref[:, gu_w])
        part[seq_rows(c)] = value.astype(BF16).reshape(half, span, width)
        back.start(c)
    for c in range(2):
        back.middle(c)
        value = dot_nt(act[tok_rows(c), :], w_ref[:, dn_w])
        part2[seq_rows(c)] = value.astype(BF16).reshape(half, span, width)
    total = jnp.zeros((1, width), F32)
    for c in range(2):
        grad_hidden, terms = rms_rows_grad(hid[seq_rows(c)], gain, back.finish(c))
        total = total + jnp.sum(terms.reshape(half * sub, width), 0, keepdims=True)
        grad_hidden = grad_hidden + ogl_ref[seq_rows(c)].astype(F32)
        gh_ref[seq_rows(c)] = grad_hidden
        gb[seq_rows(c), mine, :] = grad_hidden.astype(BF16)
        row_gb.start(c)
        ffn.start(c)
    gain_grad[...] = total
    for c in range(2):
        row_gb.forward(c)
        ffn.middle(c)
    for c in range(2):
        out_ref[seq_rows(c)] = (hid[seq_rows(c)] + ffn.finish(c)).astype(BF16)
        row_gb.finish(c)
    for c in range(2):
        row_nf.drain(c)
        row_gb.drain(c)
        back.drain(c)
        ffn.drain(c)


def feed_forward(devices, tensor, layout, x, a, og, out_grad, gain, w_all):
    seqs, sub, width = x.shape
    span = sub * tensor
    tokens = seqs * span
    ff = layout["down"][1]
    shape = jax.ShapeDtypeStruct
    vmem = pl.BlockSpec(memory_space=pltpu.VMEM)
    dma = pltpu.SemaphoreType.DMA
    whole, own = (seqs, span, width), (seqs, sub, width)
    return pl.pallas_call(
        partial(ffn_kernel, devices, layout),
        out_shape=(
            shape(own, BF16),
            shape(own, F32),
            shape(whole, BF16),
            shape(whole, BF16),
            shape((tokens, ff), BF16),
            shape((tokens, 2 * ff), BF16),
            shape((1, width), F32),
        ),
        in_specs=[vmem] * 6,
        out_specs=(vmem,) * 7,
        scratch_shapes=[
            pltpu.VMEM(whole, BF16),
            pltpu.VMEM(whole, BF16),
        ]
        + [pltpu.VMEM((2,) + own, BF16), pltpu.VMEM(own, BF16)] * 3
        + [
            pltpu.VMEM(own, F32),
            dma((5, 2, 3)),
            dma((5, 2, 4)),
        ],
        compiler_params=pltpu.CompilerParams(
            collective_id=1, has_side_effects=True, vmem_limit_bytes=VMEM_BYTES
        ),
        name="feed_forward",
    )(x, a, og, out_grad, gain, w_all)


def to_row(column):
    size = column.shape[0]
    eye = iota((size, size), 0) == iota((size, size), 1)
    return jnp.sum(jnp.where(eye, column, 0.0), 0, keepdims=True)


def to_column(row):
    size = row.shape[1]
    eye = iota((size, size), 0) == iota((size, size), 1)
    return jnp.sum(jnp.where(eye, row, 0.0), 1, keepdims=True)


def iota(shape, dim):
    return lax.broadcasted_iota(jnp.int32, shape, dim)


def spread(columns, heads, head_dim):
    rows = columns.shape[0]
    lane = iota((rows, LANES), 1)
    blocks = []
    for first in range(0, heads, LANES // head_dim):
        block = jnp.broadcast_to(columns[:, first : first + 1], (rows, LANES))
        for k in range(1, LANES // head_dim):
            block = jnp.where(lane >= k * head_dim, columns[:, first + k : first + k + 1], block)
        blocks.append(block)
    return jnp.concatenate(blocks, 1)


def head_sums(values, heads, head_dim):
    rows = values.shape[0]
    lane = iota((rows, LANES), 1)
    out = jnp.zeros((rows, LANES), F32)
    per = LANES // head_dim
    for h in range(heads):
        block = values[:, h // per * LANES : (h // per + 1) * LANES]
        inside = jnp.logical_and(lane >= h % per * head_dim, lane < (h % per + 1) * head_dim)
        total = jnp.sum(jnp.where(inside, block, 0.0), 1, keepdims=True)
        out = jnp.where(lane == h, total, out)
    return out


def pick_halves(blocks, head_dim):
    lane = iota(blocks[0].shape, 1)
    per = LANES // head_dim
    out = []
    for first in range(0, len(blocks), per):
        block = blocks[first]
        for k in range(1, per):
            block = jnp.where(lane >= k * head_dim, blocks[first + k], block)
        out.append(block)
    return jnp.concatenate(out, 1)


def softplus(value):
    return jnp.maximum(value, 0.0) + jnp.log1p(jnp.exp(-jnp.abs(value)))


def running_sum(values, backward=False):
    rows = values.shape[0]
    row = iota(values.shape, 0)
    step = 1
    while step < rows:
        if backward:
            moved = jnp.where(row < rows - step, pltpu.roll(values, rows - step, 0), 0.0)
        else:
            moved = jnp.where(row >= step, pltpu.roll(values, step, 0), 0.0)
        values = values + moved
        step *= 2
    return values


def turn(values, cosine, sine, half):
    lane = iota(values.shape, 1)
    first = lax.rem(lane, 2 * half) < half
    swapped = jnp.where(
        first, pltpu.roll(values, LANES - half, 1), pltpu.roll(values, half, 1)
    )
    return values * cosine + swapped * sine


def decay_parts(step_pre, decay_log, bias):
    step = softplus(step_pre + bias)
    rate = -jnp.exp(decay_log)
    return step, rate, running_sum(step * rate)


def same_document(aux, row):
    span = aux.shape[0]
    same = aux[:, 5:6] == row
    causal = iota((span, span), 0) >= iota((span, span), 1)
    return jnp.where(jnp.logical_and(same, causal), 0.0, MASKED)


class Neighbours:
    def __init__(self, at):
        self.at = at

    def greet(self, flips=False):
        at = self.at
        barrier = pltpu.get_barrier_semaphore()
        end = at.devices - 1

        def signal(**where):
            pl.semaphore_signal(
                barrier, inc=1, device_id=where, device_id_type=pl.DeviceIdType.MESH
            )

        for other in (at.t_near, at.t_far, at.t_both):
            signal(tensor=other)
        signal(dp=at.pair)
        count = 4
        for step in (1, 2):
            low, high = at.dp >= step, at.dp + step <= end
            pl.when(low)(partial(signal, dp=at.dp - step))
            pl.when(high)(partial(signal, dp=at.dp + step))
            count = count + low.astype(jnp.int32) + high.astype(jnp.int32)
        if flips:
            for other in at.flips():
                signal(dp=other)
                count = count + 1
        pl.semaphore_wait(barrier, count)


class TensorTotal:
    def __init__(self, at, own, got, send, recv):
        self.at, self.own, self.got, self.send, self.recv = at, own, got, send, recv

    def copies(self):
        others = (self.at.t_near, self.at.t_far, self.at.t_both)
        return [
            remote(
                self.own, self.got.at[i], self.send.at[i], self.recv.at[i], {"tensor": other}
            )
            for i, other in enumerate(others)
        ]

    def start(self):
        for copy in self.copies():
            copy.start()

    def finish(self):
        for copy in self.copies():
            copy.wait()
        return self.own[...] + self.got[0] + self.got[1] + self.got[2]


class StatePass:
    def __init__(self, at, local, pair_in, chain_in, chain_out, share, result, sems, backward):
        self.at, self.local, self.pair_in = at, local, pair_in
        self.chain_in, self.chain_out, self.share, self.result = chain_in, chain_out, share, result
        self.backward = backward
        self.pair_send, self.pair_recv, self.chain_send, self.chain_recv = sems[:4]
        self.share_send, self.share_recv = sems[4:]
        self.half = local.shape[0] // 2
        self.size = result.shape[1]
        self.head = at.last if backward else at.first
        self.tail = at.first if backward else at.last
        self.onward = at.dp - 2 if backward else at.dp + 2

    def pair_copy(self):
        src = self.local.at[pl.ds((1 - self.at.p) * self.half, self.half)]
        return remote(
            src, self.pair_in, self.pair_send.at[0], self.pair_recv.at[0], {"dp": self.at.pair}
        )

    def chain_copy(self, i):
        return remote(
            self.chain_out.at[i],
            self.chain_in.at[i],
            self.chain_send.at[i],
            self.chain_recv.at[i],
            {"dp": self.onward},
        )

    def share_copy(self, i):
        return remote(
            self.share.at[i],
            self.result.at[self.at.p * self.half + i],
            self.share_send.at[i],
            self.share_recv.at[i],
            {"dp": self.at.pair},
        )

    def start(self):
        self.pair_copy().start()

    def run(self):
        at, size = self.at, self.size
        sooner = at.p == (1 if self.backward else 0)
        self.pair_copy().wait_recv()
        for i in range(self.half):
            mine = self.local[at.p * self.half + i].astype(F32)
            other = self.pair_in[i].astype(F32)
            one = jnp.where(sooner, mine, other)
            two = jnp.where(sooner, other, mine)
            state1, keep1 = one[:size], one[size : size + 1]
            state2, keep2 = two[:size], two[size : size + 1]

            @pl.when(self.head)
            def _():
                self.chain_in[i] = jnp.zeros(self.chain_in.shape[1:], BF16)

            @pl.when(jnp.logical_not(self.head))
            def _():
                self.chain_copy(i).wait_recv()

            before = self.chain_in[i].astype(F32)
            middle = keep1 * before + state1

            @pl.when(jnp.logical_not(self.tail))
            def _():
                self.chain_out[i] = (keep2 * middle + state2).astype(BF16)
                self.chain_copy(i).start()

            self.result[at.p * self.half + i] = jnp.where(sooner, before, middle).astype(BF16)
            self.share[i] = jnp.where(sooner, middle, before).astype(BF16)
            self.share_copy(i).start()

    def finish(self):
        at = self.at
        for i in range(self.half):
            remote(
                self.share.at[i],
                self.result.at[(1 - at.p) * self.half + i],
                self.share_send.at[i],
                self.share_recv.at[i],
                {"dp": at.pair},
            ).wait_recv()
            self.share_copy(i).wait_send()
            pl.when(jnp.logical_not(self.tail))(lambda: self.chain_copy(i).wait_send())
        self.pair_copy().wait_send()


def state_pass_scratch(half, size, width):
    dma = pltpu.SemaphoreType.DMA
    return [
        pltpu.VMEM((half, size + 16, width), BF16),
        pltpu.VMEM((half, size, width), BF16),
        pltpu.VMEM((half, size, width), BF16),
        pltpu.VMEM((half, size, width), BF16),
        dma((1,)),
        dma((1,)),
        dma((half,)),
        dma((half,)),
        dma((half,)),
        dma((half,)),
    ]


def mixer_kernel(cfg, *refs):
    (
        x_ref, og_in, gain_ref, w_in, ao_in, mo_in, dn_in, aux_ref, seg_ref, all_ref, rope_ref, taps_ref,
        tap_bias, step_bias, decay_log, skip_ref, mgain_ref,
        w_all, nx, og, low, kv, q2, probs, att, ext, pre, step_buf, entering, carry, y_buf, z_buf,
        squares,
        local, xs_buf, row_send, row_recv, kv_sems, halo_sems, sq_own, sq_got, sq_send, sq_recv,
        *rest,
    ) = refs
    devices, layout, pieces, heads = (cfg[k] for k in ("devices", "layout", "pieces", "heads"))
    at = Place(devices)
    seqs, sub, width = x_ref.shape
    span = sub * 4
    tokens = seqs * span
    depth = w_in.shape[0]
    xw = layout["x"][1]
    head_dim = xw // heads
    sw = layout["state"][1]
    size = sw // 2
    mixed = xw + sw
    qw = layout["q"][1]
    at_dim = qw // 2
    pass_refs, sems = rest[:10], rest[10:]
    own_rows = pl.ds(pl.multiple_of(at.dp * depth, depth), depth)
    Neighbours(at).greet()
    first_w = w_in.shape[1] - layout["gu"][1]
    w_all[own_rows, pl.ds(0, first_w)] = w_in[:, :first_w]
    w_all[own_rows, pl.ds(*layout["gu"])] = w_in[:, first_w:]
    gathers = []
    for i, (first, count) in enumerate(pieces):

        def view(block, first=first, count=count):
            return w_all.at[
                pl.ds(pl.multiple_of(block * depth, depth), depth), pl.ds(first, count)
            ]

        gathers.append(LineGather(at, view, *sems[4 * i : 4 * i + 4]))

    def steps(i, *which):
        for s in which:
            if s < at.lines - 1:
                gathers[i].step(s)
        if which[-1] == 2:
            pl.loop(3, max(at.lines - 1, 3))(lambda s: gathers[i].step(s))
            gathers[i].finish()

    gathers[0].start()
    gain = gain_ref[...]
    mine = pl.ds(pl.multiple_of(at.t * sub, sub), sub)
    for s in range(seqs):
        nx[s, mine, :] = rms_rows(x_ref[s].astype(F32), gain).astype(BF16)
        og[s, mine, :] = og_in[s]
    half = seqs // 2

    def rows_of(buf):
        def view(rank, chunk):
            return buf.at[pl.ds(chunk * half, half), pl.ds(pl.multiple_of(rank * sub, sub), sub), :]

        return view

    row_nx = RowGather(at, rows_of(nx), row_send.at[0], row_recv.at[0])
    row_og = RowGather(at, rows_of(og), row_send.at[1], row_recv.at[1])
    for chunk in range(2):
        row_nx.start(chunk)
    gathers[1].start()
    out_at, dn_at = layout["out"][0], layout["down"][0]
    w_all[own_rows, pl.ds(out_at, qw)] = ao_in[...].T
    w_all[own_rows, pl.ds(out_at + qw, xw)] = mo_in[...].T
    w_all[own_rows, pl.ds(*layout["down"])] = dn_in[...].T
    for chunk in range(2):
        row_nx.forward(chunk)
    for chunk in range(2):
        row_nx.finish(chunk)
    steps(0, 0, 1, 2)
    rows = nx[...].reshape(tokens, width)

    def project(name):
        first, count = layout[name]
        return dot_nn(rows, w_all[:, pl.ds(first, count)])

    value = project("x").astype(BF16).astype(F32)
    ext[:, pl.ds(8, span), pl.ds(0, xw)] = value.reshape(seqs, span, xw)
    value = project("state").astype(BF16).astype(F32)
    ext[:, pl.ds(8, span), pl.ds(xw, sw)] = value.reshape(seqs, span, sw)
    before, after = at.dp > 0, at.dp < devices - 1

    def halo():
        return remote(
            ext.at[:, pl.ds(span, 8), :],
            ext.at[:, pl.ds(0, 8), :],
            halo_sems.at[0],
            halo_sems.at[1],
            {"dp": at.dp + 1},
        )

    pl.when(after)(lambda: halo().start())
    step_buf[...] = project("step").reshape(seqs, span, LANES)
    steps(1, 0)
    for chunk in range(2):
        row_og.start(chunk)
    pl.when(before)(lambda: halo().wait_recv())

    @pl.when(jnp.logical_not(before))
    def _():
        ext[:, pl.ds(0, 8), :] = jnp.zeros((seqs, 8, mixed), F32)

    def scan_parts(s):
        return decay_parts(step_buf[s], decay_log[...], step_bias[...])

    @pl.loop(0, seqs)
    def _(s):
        aux = aux_ref[s]
        total = tap_bias[...] + taps_ref[3:4, :] * ext[s, pl.ds(8, span), :]
        for back in (1, 2, 3):
            moved = ext[s, pl.ds(8 - back, span), :] * aux[:, back - 1 : back]
            total = total + taps_ref[3 - back : 4 - back, :] * moved
        pre[s] = total
        active = total * jax.nn.sigmoid(total)
        step, _, running = scan_parts(s)
        scaled = active[:, :xw] * spread(step, heads, head_dim)
        xs_buf[s] = scaled.astype(BF16)
        end = running[span - 1 : span, :]
        tail = spread(jnp.exp(end - running) * aux[:, 4:5], heads, head_dim)
        state_in = active[:, xw : xw + size].astype(BF16)
        local[s, :size, :] = dot_tn(state_in, (scaled * tail).astype(BF16)).astype(BF16)
        keep = jnp.broadcast_to(jnp.exp(end) * aux[span - 1 : span, 3:4], (16, LANES))
        keep = spread(keep, heads, head_dim).astype(BF16)
        local[s, size : size + 16, :] = keep
        carry[s] = keep

    passing = StatePass(
        at, local, pass_refs[0], pass_refs[1], pass_refs[2], pass_refs[3], entering,
        pass_refs[4:], False,
    )
    passing.start()
    gathers[2].start()
    steps(1, 1, 2)
    lane = iota((span, LANES), 1)
    cosine, sine = rope_ref[:, :LANES], rope_ref[:, LANES:]
    queries = project("q").reshape(seqs, span, qw)
    pairs = project("kv").reshape(seqs, span, qw)
    key_cosine = jnp.where(lane < at_dim, cosine, 1.0)
    key_sine = jnp.where(lane < at_dim, sine, 0.0)
    scale = 1.0 / math.sqrt(at_dim)
    for s in range(seqs):
        kv[at.dp, s] = turn(pairs[s], key_cosine, key_sine, at_dim // 2).astype(BF16)
    kv_gather = LineGather(
        at, lambda block: kv.at[block], *(kv_sems.at[i] for i in range(3)), kv_sems.at[3]
    )
    kv_gather.start()
    for s in range(seqs):
        turned = turn(queries[s], cosine, sine, at_dim // 2) * scale
        q2[s, :span, :] = jnp.where(lane < at_dim, turned, 0.0).astype(BF16)
        turned = pltpu.roll(turned, at_dim, 1)
        q2[s, span:, :] = jnp.where(lane < at_dim, turned, 0.0).astype(BF16)
    z_buf[...] = project("z").astype(BF16).reshape(seqs, span, xw)
    passing.run()
    for s in range(2):
        if s < at.lines - 1:
            kv_gather.step(s)

    @pl.loop(0, seqs)
    def _(s):
        aux = aux_ref[s]
        active = pre[s] * jax.nn.sigmoid(pre[s])
        _, _, running = scan_parts(s)
        running_rows = running.T
        allowed = same_document(aux, seg_ref[s])
        state_in = active[:, xw : xw + size].astype(BF16)
        state_out = active[:, xw + size :].astype(BF16)
        joined = dot_nt(state_out, state_in)
        blocks = []
        for h in range(heads):
            gap = running[:, h : h + 1] - running_rows[h : h + 1, :]
            weight = (joined * jnp.exp(gap + allowed)).astype(BF16)
            cols = pl.ds(h * head_dim // LANES * LANES, LANES)
            blocks.append(dot_nn(weight, xs_buf[s, :, cols]))
        y_buf[s] = pick_halves(blocks, head_dim) + skip_ref[...] * active[:, :xw]

    pl.loop(2, max(at.lines - 1, 2))(lambda s: kv_gather.step(s))
    kv_gather.finish()
    steps(2, 0, 1, 2)
    gathers[3].start()
    for chunk in range(2):
        row_og.forward(chunk)
    count = devices * span
    key_at = iota((span, count), 1)
    query_at = iota((span, count), 0) + at.dp * span

    @pl.loop(0, seqs)
    def _(s):
        keys = kv[:, s].reshape(count, qw)
        allowed = jnp.logical_and(aux_ref[s][:, 5:6] == all_ref[s], key_at <= query_at)
        bias = jnp.where(allowed, 0.0, MASKED)
        outs = []
        for h in range(2):
            part = pl.ds(h * span, span)
            scores = dot_nt(q2[s, part, :], keys) + bias
            power = jnp.exp(scores - jnp.max(scores, 1, keepdims=True))
            weight = power * (1.0 / jnp.sum(power, 1, keepdims=True))
            weight = weight.astype(BF16)
            probs[s, part, :] = weight
            outs.append(dot_nn(weight, keys))
        att[s] = jnp.where(lane < at_dim, pltpu.roll(outs[0], at_dim, 1), outs[1])

    low[:, pl.ds(0, qw)] = att[...].reshape(tokens, qw).astype(BF16)
    passing.finish()
    sq_own[...] = jnp.zeros(sq_own.shape, F32)
    for s in range(seqs):
        aux = aux_ref[s]
        state_out = (pre[s, :, pl.ds(xw + size, size)])
        state_out = (state_out * jax.nn.sigmoid(state_out)).astype(BF16)
        _, _, running = scan_parts(s)
        factor = spread(jnp.exp(running) * aux[:, 3:4], heads, head_dim)
        y = y_buf[s] + dot_nn(state_out, entering[s]) * factor
        y_buf[s] = y
        gate = z_buf[s].astype(F32)
        gated = y * gate * jax.nn.sigmoid(gate)
        sq_own[s : s + 1, :] = to_row(jnp.sum(gated * gated, 1, keepdims=True))
    total = TensorTotal(at, sq_own, sq_got, sq_send, sq_recv)
    total.start()
    steps(3, 0, 1)
    gathers[4].start()
    squares[...] = total.finish()
    for s in range(seqs):
        gate = z_buf[s].astype(F32)
        gated = y_buf[s] * gate * jax.nn.sigmoid(gate)
        norm = lax.rsqrt(to_column(squares[s : s + 1, :]) / (4 * xw) + EPSILON)
        low[pl.ds(s * span, span), pl.ds(qw, xw)] = (gated * norm * mgain_ref[...]).astype(BF16)
    for chunk in range(2):
        row_og.finish(chunk)
    steps(3, 2)
    steps(4, 0, 1, 2)
    for gather in [*gathers, kv_gather]:
        gather.drain()
    for row in (row_nx, row_og):
        for chunk in range(2):
            row.drain(chunk)
    pl.when(after)(lambda: halo().wait_send())


def mixer(cfg, x, *args):
    devices, layout, pieces, heads = (cfg[k] for k in ("devices", "layout", "pieces", "heads"))
    seqs, sub, width = x.shape
    span = sub * 4
    tokens = seqs * span
    columns = layout["down"][0] + layout["down"][1]
    xw, sw, qw = (layout[k][1] for k in ("x", "state", "q"))
    size = sw // 2
    count = devices * span
    shape = jax.ShapeDtypeStruct
    vmem = pl.BlockSpec(memory_space=pltpu.VMEM)
    dma = pltpu.SemaphoreType.DMA
    outs = (
        shape((width, columns), BF16),
        shape((seqs, span, width), BF16),
        shape((seqs, span, width), BF16),
        shape((tokens, qw + xw), BF16),
        shape((devices, seqs, span, qw), BF16),
        shape((seqs, 2 * span, qw), BF16),
        shape((seqs, 2 * span, count), BF16),
        shape((seqs, span, qw), F32),
        shape((seqs, span + 8, xw + sw), F32),
        shape((seqs, span, xw + sw), F32),
        shape((seqs, span, LANES), F32),
        shape((seqs, size, xw), BF16),
        shape((seqs, 16, xw), BF16),
        shape((seqs, span, xw), F32),
        shape((seqs, span, xw), BF16),
        shape((8, span), F32),
    )
    return pl.pallas_call(
        partial(mixer_kernel, cfg),
        out_shape=outs,
        in_specs=[vmem] * (1 + len(args)),
        out_specs=(vmem,) * len(outs),
        scratch_shapes=[
            pltpu.VMEM((seqs, size + 16, xw), BF16),
            pltpu.VMEM((seqs, span, xw), BF16),
            dma((2, 2, 3)),
            dma((2, 2, 4)),
            dma((4, devices)),
            dma((2,)),
            pltpu.VMEM((8, span), F32),
            pltpu.VMEM((3, 8, span), F32),
            dma((3,)),
            dma((3,)),
        ]
        + state_pass_scratch(seqs // 2, size, xw)
        + line_gather_sems(devices) * len(pieces),
        compiler_params=pltpu.CompilerParams(
            collective_id=0, has_side_effects=True, vmem_limit_bytes=VMEM_BYTES
        ),
        name="mixer",
    )(x, *args)


def back_kernel(cfg, *refs):
    (
        x_ref, gh_ref, gain_ref, w_any, nx_ref, og_ref, gb_ref, low_ref, nf_any, dgu_any, act_ref,
        kv_any, q2_ref, probs_any, att_ref, ext_ref, pre_ref, step_ref, entering, carry, y_ref,
        z_ref, squares, aux_ref, seg_ref, rope_ref, taps_ref, step_bias, decay_log, skip_ref,
        mgain_ref, fgain_ref,
        rg_ref, dw_ref, sums, kvs,
        w_ref, d_in, dlow, dy, dbc, dcum, ext_grad, halo_got, local2, after_state, keys_buf,
        prob_buf, dkv, dkv_got, dkv_line, dkv_own,
        part, near, far, grads, got, line, small_near, small_far, small_dp, kv_near, kv_far,
        sq_own, sq_got,
        w_sem, early_sems, load_sems, halo_sems, sq_send, sq_recv, send, recv, small_send, small_recv,
        dp_send, dp_recv, kv_send, kv_recv,
        *rest,
    ) = refs
    devices, layout, pieces, heads = (cfg[k] for k in ("devices", "layout", "scatters", "heads"))
    at = Place(devices)
    seqs, sub, width = x_ref.shape
    span = sub * 4
    tokens = seqs * span
    half = seqs // 2
    rows = half * span
    depth = width // devices
    xw, sw, qw = (layout[k][1] for k in ("x", "state", "q"))
    size = sw // 2
    head_dim = xw // heads
    at_dim = qw // 2
    mixed = xw + sw
    count = devices * span
    in_w = layout["in"][1]
    pass_refs, kv_sems, sems = rest[:10], rest[10:16], rest[16:]
    load = pltpu.make_async_copy(w_any.at[:, pl.ds(0, w_ref.shape[1])], w_ref, w_sem)
    load.start()
    early = (
        pltpu.make_async_copy(nf_any, part, early_sems.at[0]),
        pltpu.make_async_copy(dgu_any, d_in.at[:, pl.ds(0, dgu_any.shape[1])], early_sems.at[1]),
    )
    for copy in early:
        copy.start()

    slots = keys_buf.shape[0]

    def loads(s):
        slot = s % slots
        return (
            pltpu.make_async_copy(kv_any.at[:, s], keys_buf.at[slot], load_sems.at[0, slot]),
            pltpu.make_async_copy(probs_any.at[s], prob_buf.at[slot], load_sems.at[1, slot]),
        )

    for copy in loads(0):
        copy.start()
    Neighbours(at).greet(flips=True)

    def rows_of(buf):
        def view(rank, chunk):
            return buf.at[pl.ds(chunk * half, half), pl.ds(pl.multiple_of(rank * sub, sub), sub), :]

        return view

    scatters = []
    for i, (first, columns) in enumerate(pieces):

        def block(buf, k, first=first, columns=columns):
            return buf.at[pl.ds(pl.multiple_of(k * depth, depth), depth), pl.ds(first, columns)]

        scatters.append(
            LineScatter(
                at,
                partial(block, grads),
                partial(block, got),
                lambda zz, block=block: block(line, zz + 1),
                partial(block, line),
                sems[6 * i : 6 * i + 6],
            )
        )

    def steps(i):
        @pl.loop(0, at.lines - 1)
        def _(s):
            scatters[i].step(s)

    def finish(i):
        first, columns = pieces[i]
        scatters[i].finish(dw_ref.at[:, pl.ds(first, columns)])

    def product(lhs, rhs_ref, first, columns, into):
        tile = 2 * LANES if columns % (2 * LANES) == 0 else LANES

        @pl.loop(0, columns // tile)
        def _(j):
            src = pl.ds(pl.multiple_of(first + j * tile, LANES), tile)
            dst = pl.ds(pl.multiple_of(into + j * tile, LANES), tile)
            grads[:, dst] = dot_tn(lhs, rhs_ref[:, src]).astype(BF16)

    def weights(name_or_piece, lhs_ref, rhs_ref, first):
        into, columns = name_or_piece
        product(lhs_ref[...].reshape(tokens, width), rhs_ref, first, columns, into)

    dn, gu, out = layout["down"], layout["gu"], layout["out"]
    weights(dn, og_ref, act_ref, 0)
    scatters[0].start()
    load.wait()
    dlow[...] = dot_nn(
        gb_ref[...].reshape(tokens, width), w_ref[:, pl.ds(*layout["out"])]
    )
    mixer_gain = jnp.zeros((1, xw), F32)
    sq_own[...] = jnp.zeros(sq_own.shape, F32)
    for s in range(seqs):
        gate = z_ref[s].astype(F32)
        gated = y_ref[s] * gate * jax.nn.sigmoid(gate)
        norm = lax.rsqrt(to_column(squares[s : s + 1, :]) / (4 * xw) + EPSILON)
        grad = dlow[pl.ds(s * span, span), pl.ds(qw, xw)]
        mixer_gain = mixer_gain + jnp.sum(grad * gated * norm, 0, keepdims=True)
        inner = jnp.sum(gated * grad * mgain_ref[...], 1, keepdims=True)
        sq_own[s : s + 1, :] = to_row(inner)
    total = TensorTotal(at, sq_own, sq_got, sq_send, sq_recv)
    total.start()
    for copy in early:
        copy.wait()
    weights(gu, part, d_in, 0)
    inner_rows = total.finish()
    for s in range(seqs):
        gate = z_ref[s].astype(F32)
        sigmoid = jax.nn.sigmoid(gate)
        gated = y_ref[s] * gate * sigmoid
        norm = lax.rsqrt(to_column(squares[s : s + 1, :]) / (4 * xw) + EPSILON)
        inner = to_column(inner_rows[s : s + 1, :])
        term = dlow[pl.ds(s * span, span), pl.ds(qw, xw)] * mgain_ref[...]
        grad = norm * (term - gated * (norm * norm * inner / (4 * xw)))
        dy[s] = grad * gate * sigmoid
        grad = grad * y_ref[s] * sigmoid * (1.0 + gate * (1.0 - sigmoid))
        d_in[pl.ds(s * span, span), pl.ds(*layout["z"])] = grad.astype(BF16)

    def parts(s):
        active = pre_ref[s] * jax.nn.sigmoid(pre_ref[s])
        step, rate, running = decay_parts(step_ref[s], decay_log[...], step_bias[...])
        state_in = active[:, xw : xw + size].astype(BF16)
        state_out = active[:, xw + size :].astype(BF16)
        return active[:, :xw], state_in, state_out, step, rate, running

    @pl.loop(0, seqs)
    def _(s):
        _, _, state_out, _, _, running = parts(s)
        factor = spread(jnp.exp(running) * aux_ref[s][:, 3:4], heads, head_dim)
        low = (dy[s] * factor).astype(BF16)
        local2[s, :size, :] = dot_tn(state_out, low).astype(BF16)
        local2[s, size:, :] = carry[s]

    passing = StatePass(
        at, local2, pass_refs[0], pass_refs[1], pass_refs[2], pass_refs[3], after_state,
        pass_refs[4:], True,
    )
    passing.start()
    scatters[1].start()
    weights(out, gb_ref, low_ref, 0)

    @pl.loop(0, seqs)
    def _(s):
        x, state_in, state_out, step, _, running = parts(s)
        running_rows = running.T
        allowed = same_document(aux_ref[s], seg_ref[s])
        xs = (x * spread(step, heads, head_dim)).astype(BF16)
        joined = dot_nt(state_out, state_in)
        lane = iota((span, LANES), 1)
        d_joined = jnp.zeros((span, span), F32)
        d_running = jnp.zeros((span, LANES), F32)
        blocks = []
        for h in range(heads):
            cols = slice(h * head_dim // LANES * LANES, h * head_dim // LANES * LANES + LANES)
            begin = h * head_dim % LANES
            inside = jnp.logical_and(lane >= begin, lane < begin + head_dim)
            grad = dy[s, :, pl.ds(cols.start, LANES)]
            decay = jnp.exp(running[:, h : h + 1] - running_rows[h : h + 1, :] + allowed)
            weight = joined * decay
            d_weight = dot_nt(jnp.where(inside, grad, 0.0).astype(BF16), xs[:, cols])
            d_joined = d_joined + d_weight * decay
            product_ = (d_weight * weight).astype(BF16)
            one = (lane == h).astype(BF16)
            d_running = d_running + dot_nn(product_, one) - dot_tn(product_, one)
            blocks.append(dot_tn(weight.astype(BF16), grad.astype(BF16)))
        dlow[pl.ds(pl.multiple_of(s * span, span), span), pl.ds(qw, xw)] = pick_halves(blocks, head_dim)
        d_joined = d_joined.astype(BF16)
        factor = spread(jnp.exp(running) * aux_ref[s][:, 3:4], heads, head_dim)
        crossed = dot_nn(state_out, entering[s]) * factor
        dcum[s] = d_running + head_sums(dy[s] * crossed, heads, head_dim)
        low = (dy[s] * factor).astype(BF16)
        dbc[s, :, :size] = dot_tn(d_joined, state_out)
        dbc[s, :, size:] = dot_nn(d_joined, state_in) + dot_nt(low, entering[s])

    steps(0)
    passing.run()
    scatters[2].start()
    lane = iota((span, LANES), 1)
    upper = lane >= at_dim
    cosine, sine = rope_ref[:, :LANES], rope_ref[:, LANES:]
    scale = 1.0 / math.sqrt(at_dim)
    for s in range(seqs):
        slot = s % slots
        for copy in loads(s):
            copy.wait()
        if slots > 1 and s + 1 < seqs:
            for copy in loads(s + 1):
                copy.start()
        keys = keys_buf[slot].reshape(count, qw)
        grad = dlow[pl.ds(s * span, span), pl.ds(0, qw)].astype(BF16).astype(F32)
        inner = grad * att_ref[s]
        d_keys = jnp.zeros((count, qw), F32)
        d_query = []
        for h in range(2):
            mine = upper if h else jnp.logical_not(upper)
            delta = jnp.sum(jnp.where(mine, inner, 0.0), 1, keepdims=True)
            moved = grad if h else pltpu.roll(grad, at_dim, 1)
            moved = jnp.where(upper, moved, 0.0).astype(BF16)
            weight = prob_buf[slot, pl.ds(h * span, span), :]
            d_weight = dot_nt(moved, keys)
            d_score = (weight.astype(F32) * (d_weight - delta)).astype(BF16)
            query = q2_ref[s, pl.ds(h * span, span), :]
            d_keys = d_keys + dot_tn(d_score, query) + dot_tn(weight, moved)
            d_query.append(dot_nn(d_score, keys))
        dkv[:, s] = d_keys.astype(BF16).reshape(devices, span, qw)
        if slots == 1 and s + 1 < seqs:
            for copy in loads(s + 1):
                copy.start()
        d_query = jnp.where(upper, pltpu.roll(d_query[1], at_dim, 1), d_query[0]) * scale
        d_in[pl.ds(s * span, span), pl.ds(*layout["q"])] = turn(
            d_query, cosine, -sine, at_dim // 2
        ).astype(BF16)
    kv_scatter = LineScatter(
        at,
        lambda k: dkv.at[k],
        lambda zz: dkv_got.at[zz],
        None,
        lambda zz: dkv_line.at[zz],
        kv_sems,
        causal=True,
    )
    kv_scatter.start()
    passing.finish()
    tap_grads = [jnp.zeros((1, mixed), F32) for _ in range(4)]
    bias_grad = jnp.zeros((1, mixed), F32)
    step_grad = jnp.zeros((1, LANES), F32)
    decay_grad = jnp.zeros((1, LANES), F32)
    skip_grad = jnp.zeros((1, xw), F32)
    ext_grad[:, pl.ds(0, 8), :] = jnp.zeros((seqs, 8, mixed), F32)
    for s in range(seqs):
        aux = aux_ref[s]
        x, state_in, state_out, step, rate, running = parts(s)
        step_wide = spread(step, heads, head_dim)
        xs = x * step_wide
        end = running[span - 1 : span, :]
        tail = spread(jnp.exp(end - running) * aux[:, 4:5], heads, head_dim)
        later = after_state[s]
        found = dot_nn(state_in, later)
        weighted = xs * tail
        d_xs = dlow[pl.ds(s * span, span), pl.ds(qw, xw)] + found * tail
        d_in_state = dbc[s, :, :size] + dot_nt(weighted.astype(BF16), later)
        moved = head_sums(found * weighted, heads, head_dim)
        carried = jnp.sum(later.astype(F32) * entering[s].astype(F32), 0, keepdims=True)
        carried = head_sums(carried, heads, head_dim) * jnp.exp(end) * aux[span - 1 : span, 3:4]
        final = jnp.sum(moved, 0, keepdims=True) + carried
        d_running = dcum[s] - moved
        d_running = d_running + jnp.where(iota((span, LANES), 0) == span - 1, final, 0.0)
        d_decay = running_sum(d_running, backward=True)
        d_step = head_sums(d_xs * x, heads, head_dim) + d_decay * rate
        d_step = d_step * jax.nn.sigmoid(step_ref[s] + step_bias[...])
        d_in[pl.ds(s * span, span), pl.ds(*layout["step"])] = d_step.astype(BF16)
        step_grad = step_grad + jnp.sum(d_step, 0, keepdims=True)
        decay_grad = decay_grad + jnp.sum(d_decay * step, 0, keepdims=True) * rate
        skip_grad = skip_grad + jnp.sum(dy[s] * x, 0, keepdims=True)
        d_x = d_xs * step_wide + skip_ref[...] * dy[s]
        value = pre_ref[s]
        sigmoid = jax.nn.sigmoid(value)
        slope = sigmoid * (1.0 + value * (1.0 - sigmoid))
        outer = jnp.concatenate([d_x, d_in_state, dbc[s, :, size:]], 1) * slope
        bias_grad = bias_grad + jnp.sum(outer, 0, keepdims=True)
        ext_grad[s, pl.ds(8, span), :] = taps_ref[3:4, :] * outer
        tap_grads[3] = tap_grads[3] + jnp.sum(
            outer * ext_ref[s, pl.ds(8, span), :], 0, keepdims=True
        )
        for back in (1, 2, 3):
            valid = outer * aux[:, back - 1 : back]
            tap_grads[3 - back] = tap_grads[3 - back] + jnp.sum(
                valid * ext_ref[s, pl.ds(8 - back, span), :], 0, keepdims=True
            )
            ext_grad[s, pl.ds(8 - back, span), :] += taps_ref[3 - back : 4 - back, :] * valid
    before, after = at.dp > 0, at.dp < devices - 1

    def halo():
        return remote(
            ext_grad.at[:, pl.ds(0, 8), :],
            halo_got,
            halo_sems.at[0],
            halo_sems.at[1],
            {"dp": at.dp - 1},
        )

    pl.when(before)(lambda: halo().start())
    sums[...] = jnp.zeros(sums.shape, F32)
    sums[1:2, :] = fgain_ref[...]
    for k in range(4):
        sums[2 + k : 3 + k, pl.ds(0, sw)] = tap_grads[k][:, xw:]
        sums[8 + k : 9 + k, pl.ds(0, xw)] = tap_grads[k][:, :xw]
    sums[6:7, pl.ds(0, sw)] = bias_grad[:, xw:]
    sums[12:13, pl.ds(0, xw)] = bias_grad[:, :xw]
    sums[13:14, pl.ds(0, xw)] = mixer_gain
    sums[14:15, pl.ds(0, LANES)] = step_grad
    sums[14:15, pl.ds(LANES, LANES)] = decay_grad
    sums[14:15, pl.ds(2 * LANES, LANES)] = head_sums(
        jnp.broadcast_to(skip_grad, (8, xw)), heads, head_dim
    )[:1]
    steps(1)
    finish(0)
    kv_scatter.run_causal(dkv_own)
    for s in range(seqs):
        key_cosine = jnp.where(upper, 1.0, cosine)
        key_sine = jnp.where(upper, 0.0, -sine)
        d_in[pl.ds(s * span, span), pl.ds(*layout["kv"])] = turn(
            dkv_own[s], key_cosine, key_sine, at_dim // 2
        ).astype(BF16)
    q_piece, x_piece = pieces[3], pieces[4]
    weights(q_piece, nx_ref, d_in, q_piece[0])
    scatters[3].start()
    pl.when(after)(lambda: halo().wait_recv())
    ends = pl.ds(span, 8)

    @pl.when(after)
    def _():
        ext_grad[:, ends, :] += halo_got[...]

    value = ext_grad[:, pl.ds(8, span), :].reshape(tokens, mixed).astype(BF16)
    d_in[:, pl.ds(layout["x"][0], mixed)] = value
    back = RowScatter(
        at,
        rows_of(part),
        lambda which, chunk: near.at[which, pl.ds(chunk * half, half)],
        lambda chunk: far.at[pl.ds(chunk * half, half)],
        send,
        recv,
    )
    for c in range(2):
        value = dot_nt(d_in[pl.ds(c * rows, rows), :], w_ref[:, pl.ds(0, in_w)])
        part[pl.ds(c * half, half)] = value.astype(BF16).reshape(half, span, width)
        back.start(c)
    weights(x_piece, nx_ref, d_in, x_piece[0])
    scatters[4].start()
    steps(2)
    finish(1)
    for c in range(2):
        back.middle(c)
    steps(3)
    finish(2)
    total = jnp.zeros((1, width), F32)
    gain = gain_ref[...]
    for c in range(2):
        seq = pl.ds(c * half, half)
        grad, terms = rms_rows_grad(x_ref[seq].astype(F32), gain, back.finish(c))
        rg_ref[seq] = gh_ref[seq] + grad
        total = total + jnp.sum(terms.reshape(half * sub, width), 0, keepdims=True)
    sums[0:1, :] = total
    for i, (buf, where) in enumerate(
        ((small_near, {"tensor": at.t_near}), (small_far, {"tensor": at.t_far}))
    ):
        copy = remote(sums.at[pl.ds(0, 8)], buf, small_send.at[i], small_recv.at[i], where)
        copy.start()
        copy.wait()
        sums[0:8, :] += buf[...]
    for i, other in enumerate(at.flips()):
        copy = remote(sums, small_dp.at[i], dp_send.at[i], dp_recv.at[i], {"dp": other})
        copy.start()
        copy.wait()
        sums[...] += small_dp[i]
    steps(4)
    finish(3)
    finish(4)
    kvw = layout["kv"][1]
    kv_near[0, :, pl.ds(0, kvw)] = dw_ref[:, pl.ds(*layout["kv"])]
    kv_near[0, :, pl.ds(kvw, sw)] = dw_ref[:, pl.ds(*layout["state"])]
    copy = remote(kv_near.at[0], kv_near.at[1], kv_send.at[0], kv_recv.at[0], {"tensor": at.t_near})
    copy.start()
    copy.wait()
    kv_far[0] = kv_near[0] + kv_near[1]
    copy = remote(kv_far.at[0], kv_far.at[1], kv_send.at[1], kv_recv.at[1], {"tensor": at.t_far})
    copy.start()
    copy.wait()
    kvs[:, pl.ds(0, kvw)] = kv_far[0, :, pl.ds(0, kvw)]
    kvs[:, pl.ds(kvw, kvw)] = kv_far[1, :, pl.ds(0, kvw)]

    @pl.when(at.t >= 2)
    def _():
        kvs[:, pl.ds(0, kvw)] = kv_far[1, :, pl.ds(0, kvw)]
        kvs[:, pl.ds(kvw, kvw)] = kv_far[0, :, pl.ds(0, kvw)]

    kvs[:, pl.ds(2 * kvw, sw)] = kv_far[0, :, pl.ds(kvw, sw)] + kv_far[1, :, pl.ds(kvw, sw)]
    for scatter in [*scatters, kv_scatter]:
        scatter.drain()
    for c in range(2):
        back.drain(c)
    pl.when(before)(lambda: halo().wait_send())


def backward(cfg, x, *args):
    devices, layout, pieces, heads = (cfg[k] for k in ("devices", "layout", "scatters", "heads"))
    seqs, sub, width = x.shape
    span = sub * 4
    tokens = seqs * span
    half = seqs // 2
    depth = width // devices
    lines = devices // 2
    columns = layout["down"][0] + layout["down"][1]
    xw, sw, qw, kvw = (layout[k][1] for k in ("x", "state", "q", "kv"))
    size = sw // 2
    mixed = xw + sw
    in_w = layout["in"][1]
    own = (seqs, sub, width)
    rounds = devices.bit_length() - 1
    slots = 2 if devices * span <= 2048 else 1
    shape = jax.ShapeDtypeStruct
    vmem = pl.BlockSpec(memory_space=pltpu.VMEM)
    hbm = pl.BlockSpec(memory_space=pl.ANY)
    dma = pltpu.SemaphoreType.DMA
    in_specs = [vmem] * (1 + len(args))
    for i in (3, 8, 9, 11, 13):
        in_specs[i] = hbm
    return pl.pallas_call(
        partial(back_kernel, cfg),
        out_shape=(
            shape(own, F32),
            shape((depth, columns), F32),
            shape((16, width), F32),
            shape((depth, 2 * kvw + sw), F32),
        ),
        in_specs=in_specs,
        out_specs=(vmem,) * 4,
        scratch_shapes=[
            pltpu.VMEM((width, in_w + qw + xw), BF16),
            pltpu.VMEM((tokens, in_w), BF16),
            pltpu.VMEM((tokens, qw + xw), F32),
            pltpu.VMEM((seqs, span, xw), F32),
            pltpu.VMEM((seqs, span, sw), F32),
            pltpu.VMEM((seqs, span, LANES), F32),
            pltpu.VMEM((seqs, span + 8, mixed), F32),
            pltpu.VMEM((seqs, 8, mixed), F32),
            pltpu.VMEM((seqs, size + 16, xw), BF16),
            pltpu.VMEM((seqs, size, xw), BF16),
            pltpu.VMEM((slots, devices, span, qw), BF16),
            pltpu.VMEM((slots, 2 * span, devices * span), BF16),
            pltpu.VMEM((devices, seqs, span, qw), BF16),
            pltpu.VMEM((lines, seqs, span, qw), BF16),
            pltpu.VMEM((lines, seqs, span, qw), BF16),
            pltpu.VMEM((seqs, span, qw), F32),
            pltpu.VMEM((seqs, span, width), BF16),
            pltpu.VMEM((2,) + own, BF16),
            pltpu.VMEM(own, BF16),
            pltpu.VMEM((width, columns), BF16),
            pltpu.VMEM((lines * depth, columns), BF16),
            pltpu.VMEM(((lines + 1) * depth, columns), BF16),
            pltpu.VMEM((8, width), F32),
            pltpu.VMEM((8, width), F32),
            pltpu.VMEM((rounds, 16, width), F32),
            pltpu.VMEM((2, depth, kvw + sw), F32),
            pltpu.VMEM((2, depth, kvw + sw), F32),
            pltpu.VMEM((8, span), F32),
            pltpu.VMEM((3, 8, span), F32),
            dma,
            dma((2,)),
            dma((2, 2)),
            dma((2,)),
            dma((3,)),
            dma((3,)),
            dma((2, 3)),
            dma((2, 4)),
            dma((2,)),
            dma((2,)),
            dma((rounds,)),
            dma((rounds,)),
            dma((2,)),
            dma((2,)),
        ]
        + state_pass_scratch(half, size, xw)
        + line_scatter_sems(devices) * (1 + len(pieces)),
        compiler_params=pltpu.CompilerParams(
            collective_id=2, has_side_effects=True, vmem_limit_bytes=VMEM_BYTES
        ),
        name="backward",
    )(x, *args)


def rope_table(length, head_dim):
    half = head_dim // 2
    frequency = np.exp(-math.log(ROTARY_BASE) * 2.0 * np.arange(half) / head_dim)
    angle = np.arange(length)[:, None] * frequency[None, :]
    cosine, sine = np.cos(angle), np.sin(angle)
    copies = LANES // head_dim
    table = [cosine, cosine] * copies + [-sine, sine] * copies
    return np.concatenate(table, 1).astype(np.float32)


def body(
    resid_in,
    segment_ids,
    out_grad,
    input_gain,
    ffn_gain,
    query_weight,
    keyvalue_weight,
    attention_output_weight,
    mixer_input_weight,
    state_input_weight,
    step_weight,
    conv_mixer,
    conv_mixer_bias,
    conv_state,
    conv_state_bias,
    step_bias,
    decay_log,
    skip_gain,
    mixer_gain,
    mixer_output_weight,
    gate_up_weight,
    down_weight,
):
    tensor_count = lax.axis_size("tensor")
    shard_count = lax.axis_size("dp")
    tensor_rank = lax.axis_index("tensor")
    shard_rank = lax.axis_index("dp")
    sequences, sub_rows, model_width = resid_in.shape
    span_rows = sub_rows * tensor_count
    head_dim = keyvalue_weight.shape[2] // 2
    query_width = query_weight.shape[1]
    local_heads = query_width // head_dim
    mixer_local = step_weight.shape[1]
    mixer_width = conv_mixer.shape[1]
    mixer_total = mixer_width * tensor_count
    mixer_dim = mixer_width // mixer_local
    state_dim = state_input_weight.shape[1] // 2
    edge_rows = conv_mixer.shape[0] - 1
    scale = 1.0 / math.sqrt(head_dim)
    keyval_index = tensor_rank * KVH // tensor_count
    keyvalue_local = lax.dynamic_index_in_dim(keyvalue_weight, keyval_index, 1, keepdims=False)
    ff = down_weight.shape[0]
    depth = query_weight.shape[0]
    layout = {}
    columns = 0
    for name, size in (
        ("step", LANES),
        ("x", mixer_width),
        ("state", 2 * state_dim),
        ("q", query_width),
        ("kv", 2 * head_dim),
        ("z", mixer_width),
        ("out", query_width + mixer_width),
        ("gu", 2 * ff),
        ("down", ff),
    ):
        layout[name] = (columns, size)
        columns += size
    layout["in"] = (0, layout["out"][0])
    def columns_of(array, name):
        first, size = layout[name]
        return array[..., first : first + size]

    w_packed = jnp.concatenate(
        [
            jnp.pad(step_weight, ((0, 0), (0, LANES - mixer_local))),
            mixer_input_weight[:, 1],
            state_input_weight,
            query_weight,
            keyvalue_local,
            mixer_input_weight[:, 0],
            gate_up_weight.reshape(depth, 2 * ff),
        ],
        1,
    )
    first_row = shard_rank * span_rows
    seg_span = lax.dynamic_slice_in_dim(segment_ids, first_row, span_rows, 1)
    seg_padded = jnp.pad(segment_ids, ((0, 0), (edge_rows, 0)), constant_values=-1)
    seg_ext = lax.dynamic_slice_in_dim(seg_padded, first_row, span_rows + edge_rows, 1)
    same = [seg_ext[:, edge_rows - d : edge_rows - d + span_rows] == seg_span for d in (1, 2, 3)]
    aux = jnp.stack(
        [
            *same,
            seg_span == seg_ext[:, edge_rows - 1 : edge_rows],
            seg_span == seg_span[:, -1:],
            seg_span,
        ],
        -1,
    ).astype(jnp.float32)
    rope = lax.dynamic_slice_in_dim(
        jnp.asarray(rope_table(segment_ids.shape[1], head_dim)), first_row, span_rows, 0
    )

    def lanes(array):
        return jnp.pad(array[None, :], ((0, 0), (0, LANES - array.shape[0])))

    config = {
        "devices": shard_count,
        "layout": layout,
        "heads": mixer_local,
        "pieces": (
            (layout["step"][0], layout["q"][0] - layout["step"][0]),
            (layout["q"][0], layout["out"][0] - layout["q"][0]),
            layout["out"],
            layout["gu"],
            layout["down"],
        ),
        "scatters": (
            layout["down"],
            layout["gu"],
            layout["out"],
            (layout["q"][0], layout["out"][0] - layout["q"][0]),
            (layout["step"][0], layout["q"][0] - layout["step"][0]),
        ),
    }
    (
        w_all, span_normed_input, span_gradient, branch_low, keys, queries, probs, attention, ext,
        pre, step_pre, entering, state_decay, mixer_y, gate_z, squares,
    ) = mixer(
        config,
        resid_in,
        out_grad,
        input_gain[None, :],
        w_packed,
        attention_output_weight,
        mixer_output_weight,
        down_weight,
        aux,
        seg_span.astype(jnp.float32)[:, None, :],
        segment_ids.astype(jnp.float32)[:, None, :],
        rope,
        jnp.concatenate([conv_mixer, conv_state], 1),
        jnp.concatenate([conv_mixer_bias, conv_state_bias])[None, :],
        lanes(step_bias),
        lanes(decay_log),
        jnp.repeat(skip_gain, mixer_dim)[None, :],
        mixer_gain[None, :],
    )
    block_out, grad_hidden, grad_branch, span_feedforward, activated, grad_gate_up, ffn_gain_part = (
        feed_forward(
            shard_count,
            tensor_count,
            layout,
            resid_in,
            branch_low,
            span_gradient,
            out_grad,
            ffn_gain[None, :],
            w_all,
        )
    )
    resid_grad, weight_grads, sums, replicated = backward(
        config,
        resid_in,
        grad_hidden,
        input_gain[None, :],
        w_all,
        span_normed_input,
        span_gradient,
        grad_branch,
        branch_low,
        span_feedforward,
        grad_gate_up,
        activated,
        keys,
        queries,
        probs,
        attention,
        ext,
        pre,
        step_pre,
        entering,
        state_decay,
        mixer_y,
        gate_z,
        squares,
        aux,
        seg_span.astype(jnp.float32)[:, None, :],
        rope,
        jnp.concatenate([conv_mixer, conv_state], 1),
        lanes(step_bias),
        lanes(decay_log),
        jnp.repeat(skip_gain, mixer_dim)[None, :],
        mixer_gain[None, :],
        ffn_gain_part,
    )
    out_grads = columns_of(weight_grads, "out").T
    kv_width = 2 * head_dim
    return (
        block_out,
        resid_grad,
        sums[0],
        sums[1],
        columns_of(weight_grads, "q"),
        replicated[:, : 2 * kv_width].reshape(depth, 2, kv_width),
        out_grads[:query_width],
        jnp.stack([columns_of(weight_grads, "z"), columns_of(weight_grads, "x")], 1),
        replicated[:, 2 * kv_width :],
        columns_of(weight_grads, "step")[:, :mixer_local],
        sums[8:12, :mixer_width],
        sums[12, :mixer_width],
        sums[2:6, : 2 * state_dim],
        sums[6, : 2 * state_dim],
        sums[14, :mixer_local],
        sums[14, LANES : LANES + mixer_local],
        sums[14, 2 * LANES : 2 * LANES + mixer_local],
        sums[13, :mixer_width],
        out_grads[query_width:],
        columns_of(weight_grads, "gu").reshape(depth, 2, ff),
        columns_of(weight_grads, "down").T,
    )


def solution(mesh):
    placed = (
        P(None, ("dp", "tensor"), None),
        P(),
        P(None, ("dp", "tensor"), None),
        P(),
        P(),
        P("dp", "tensor"),
        P("dp", None, None),
        P("tensor", "dp"),
        P("dp", None, "tensor"),
        P("dp", None),
        P("dp", "tensor"),
        P(None, "tensor"),
        P("tensor"),
        P(),
        P(),
        P("tensor"),
        P("tensor"),
        P("tensor"),
        P("tensor"),
        P("tensor", "dp"),
        P("dp", None, "tensor"),
        P("tensor", "dp"),
    )
    return jax.shard_map(
        body,
        mesh=mesh,
        in_specs=placed,
        out_specs=(
            P(None, ("dp", "tensor"), None),
            P(None, ("dp", "tensor"), None),
            P(),
            P(),
            P("dp", "tensor"),
            P("dp", None, None),
            P("tensor", "dp"),
            P("dp", None, "tensor"),
            P("dp", None),
            P("dp", "tensor"),
            P(None, "tensor"),
            P("tensor"),
            P(),
            P(),
            P("tensor"),
            P("tensor"),
            P("tensor"),
            P("tensor"),
            P("tensor", "dp"),
            P("dp", None, "tensor"),
            P("tensor", "dp"),
        ),
        check_vma=False,
    )
```

time: 758 us -> 367 us (0.48); the launches traced: 748 us -> 367 us
  waiting for transfers between devices: 122 us -> 0 us
  other arithmetic: 84.7 us -> 1.08 us
  matrix products: 60 us -> 0 us
  local copies, waits for them, and re-layouts: 72.5 us -> 30.3 us
  blocking collectives: 35.1 us -> 0 us
  Pallas kernels: 351 us -> 334 us
  between operations: 16 us -> 0.95 us
    all_gather x3 -> x0, waiting for transfers between devices: 93.2 us -> none  [the longest x1 58.9 us: carried_in(): lax.all_gather(a.astype(kind), axis)]
    dot_general x19 -> x0, matrix products: 60 us -> none  [the longest x3 14.5 us: state_inner(): jnp.einsum('sthn,sjhn->stjh', output_heads, input_heads, precision=MATMUL...]
    all_gather x1 -> x0, blocking collectives: 22.6 us -> none  [prefix(): lax.all_gather(part.astype(kind), axis)]
    reduce_scatter x1 -> x0, waiting for transfers between devices: 15.4 us -> none  [body(): lax.psum_scatter(grad_keys_all, 'dp', scatter_dimension=1, tiled=True)]
    pallas_call x2, Pallas kernels: 306 us -> 290 us  [the longest x1 154 us: backward(): pl.pallas_call(partial(back_kernel, cfg), out_shape=(shape(own, F32), sha...]
    reduce_sum x13 -> x0, other arithmetic: 15.1 us -> none  [the longest x2 4.14 us: body(): grad_skip = jnp.sum(grad_y_heads * x_heads, (0, 1, 3))]
    another operation x9 -> x0, other arithmetic: 14 us -> none  [the longest x1 5.38 us: state_cross(): cumulative = jnp.cumsum(step_size * decay_rate, axis=1)]
    ppermute x4 -> x0, waiting for transfers between devices: 13.1 us -> none  [from_behind(): return lax.ppermute(array, axis, pairs)]
  transfers between devices with their start and end apart: 8 -> 0, of which waited for: 6 -> 0; matrix products, arithmetic and copies ran while one was open for 12% -> 0% of each run, Pallas kernels for 0% -> 0%
where the time goes in v2:
time: 367 us
  Pallas kernels  334 us (91%)
  local copies, waits for them, and re-layouts  30.3 us (8%)
    pallas_call x1, Pallas kernels, backward(): pl.pallas_call(partial(back_kernel, cfg), out_shape=(shape(own, F32), sha...  154 us
    pallas_call x1, Pallas kernels, mixer(): pl.pallas_call(partial(mixer_kernel, cfg), out_shape=outs, in_specs=[vmem...  137 us
    pallas_call x1, Pallas kernels, feed_forward(): pl.pallas_call(partial(ffn_kernel, devices, layout), out_shape=(shape(own...  43.8 us
    unnamed x48, local copies, waits for them, and re-layouts  8.26 us

profile of v2, /device:TPU:0, one launch (start us, length us, event | category | flops | bytes accessed | tf_op | source)
XLA Modules:
  0.0 366.6 jit_solution(8817704239215600856)
XLA Ops:
  0.7 0.0 copy-start
  0.7 0.9 copy.54
  1.6 0.0 copy-start.9
  1.6 0.0 copy-start.10
  1.6 0.0 copy-start.15
  1.6 0.0 copy-start.13
  1.7 1.4 fusion.8
  3.1 0.8 constant_dynamic-update-slice_fusion.3
  3.9 0.8 constant_dynamic-update-slice_fusion.2
  4.7 0.1 constant_dynamic-slice_fusion.2
  4.9 0.6 fusion.6
  5.6 0.1 constant_dynamic-update-slice_fusion.10
  5.7 0.1 constant_dynamic-update-slice_fusion.9
  5.7 0.1 constant_dynamic-update-slice_fusion.8
  5.8 0.2 fusion.5
  6.0 0.1 constant_dynamic-update-slice_fusion.7
  6.1 0.2 slice_reduce_fusion
  6.3 0.1 constant_dynamic-update-slice_fusion.6
  6.4 0.9 copy.58.refs_7_.refs_23_
  7.2 0.6 broadcast_in_dim.35.refs_9_
  7.9 1.6 constant_dynamic-slice_fusion.refs_10_.refs_25_
  9.5 0.6 broadcast_in_dim.36.refs_12_
  10.1 0.5 pad.19.refs_13_.refs_27_
  10.6 0.5 pad.20.refs_14_.refs_28_
  11.1 0.1 broadcast_in_dim.39
  11.2 0.6 broadcast_in_dim_reshape.4.refs_15_.refs_29_
  11.8 0.6 broadcast_in_dim.40.refs_16_.refs_30_
  12.4 136.6 %mixer.1 = (bf16[1024,3456]{1,0:T(8,128)(2,1)}, bf16[4,128,1024]{2,1,0:T(8,128)(2,1)}, bf16[4,128,1024]{2,1,0:T(8,128)(2,1)}, bf16[512,512]{1,0:T(8,128)(2,1)}, ...) custom-call(bf16[4,32,1024]{2,1,0:T(8,128)(2,1)} %refs_0_.5, ...), custom_call_target="tpu_custom_call" | custom-call | tf_op jit(solution)/shard_map/mixer/pallas_call | solution.py:1061
  149.0 43.8 %feed_forward.1 = (bf16[4,32,1024]{2,1,0:T(8,128)(2,1)}, f32[4,32,1024]{2,1,0:T(8,128)}, bf16[4,128,1024]{2,1,0:T(8,128)(2,1)}, bf16[4,128,1024]{2,1,0:T(8,128)(...) custom-call(bf16[4,32,1024]{2,1,0:T(8,128)(2,1)} %refs_0_.5, ...), custom_call_target="tpu_custom_call" | custom-call | tf_op jit(solution)/shard_map/feed_forward/pallas_call | solution.py:511
  192.8 153.8 %backward.1 = (f32[4,32,1024]{2,1,0:T(8,128)}, f32[128,3456]{1,0:T(8,128)}, f32[16,1024]{1,0:T(8,128)}, f32[128,512]{1,0:T(8,128)}) custom-call(bf16[4,32,1024]{2,1,0:T(8,128)(2,1)} %refs_0_.5, f32[4,32,1024]{2,1,0:T(8,128)} %get-tuple-element.52.refs_1_, f32[1,1024]{1,0:T(1,128)} %bitcast.53, bf16[1024,3456]{1,0:T(8,128)(2,1)} %get-tuple-element.50.refs_5_.refs_3_, ...), custom_call_target="tpu_custom_call" | custom-call | tf_op jit(solution)/shard_map/backward/pallas_call | solution.py:1510
  346.7 1.5 fusion.9
  348.2 1.5 slice.95
  349.6 1.6 fusion.7
  351.3 0.7 reshape.52
  352.0 1.1 slice_bitcast_fusion
  353.1 0.7 copy.60
  353.9 1.1 copy.61
  354.9 0.7 copy.62
  355.6 1.3 slice.103
  356.9 1.4 slice_reduce_fusion.1
  358.3 1.3 slice.105
  359.6 1.3 slice.106
  360.9 1.2 slice_bitcast_fusion.4
  362.1 0.8 copy.63
  363.0 1.2 reshape.53
  364.2 0.8 copy.64
  365.1 0.7 copy.92
  365.8 0.8 copy.93
  (45 shorter events, 0.4 us)
Async XLA Ops:
  0.7 4.1 %copy-start = (bf16[128,2,128]{2,1,0:T(2,128)(2,1)S(1)}, bf16[128,2,128]{2,1,0:T(2,128)(2,1)}, u32[]{:S(2)}) copy-start(bf16[128,2,128]{2,1,0:T(2,128)(2,1)} %param.29) | copy-start | bytes 196612
  0.7 4.2 %copy-start.5 = (bf16[128,2,512]{2,1,0:T(2,128)(2,1)S(1)}, bf16[128,2,512]{2,1,0:T(2,128)(2,1)}, u32[]{:S(2)}) copy-start(bf16[128,2,512]{2,1,0:T(2,128)(2,1)} %param.43) | copy-start | bytes 786436
  0.7 4.3 %copy-start.4 = (s32[4,1024]{1,0:T(4,128)S(1)}, s32[4,1024]{1,0:T(4,128)}, u32[]{:S(2)}) copy-start(s32[4,1024]{1,0:T(4,128)} %param.24) | copy-start | bytes 49156
  1.6 7.9 %copy-start.8 = (f32[4,384]{1,0:T(4,128)S(1)}, f32[4,384]{1,0:T(4,128)}, u32[]{:S(2)}) copy-start(f32[4,384]{1,0:T(4,128)} %param.34) | copy-start | bytes 18436
  1.6 7.9 %copy-start.9 = (f32[4,256]{1,0:T(4,128)S(1)}, f32[4,256]{1,0:T(4,128)}, u32[]{:S(2)}) copy-start(f32[4,256]{1,0:T(4,128)} %param.36) | copy-start | bytes 12292
  1.6 7.9 %copy-start.10 = (f32[384]{0:T(512)S(1)}, f32[384]{0:T(512)}, u32[]{:S(2)}) copy-start(f32[384]{0:T(512)} %param.35) | copy-start | bytes 4612
  1.6 7.9 %copy-start.12 = (f32[256]{0:T(256)S(1)}, f32[256]{0:T(256)}, u32[]{:S(2)}) copy-start(f32[256]{0:T(256)} %param.37) | copy-start | bytes 3076
  1.6 8.5 %copy-start.14 = (f32[6]{0:T(128)S(1)}, f32[6]{0:T(128)}, u32[]{:S(2)}) copy-start(f32[6]{0:T(128)} %param.38) | copy-start | bytes 76
  1.6 9.0 %copy-start.15 = (f32[6]{0:T(128)S(1)}, f32[6]{0:T(128)}, u32[]{:S(2)}) copy-start(f32[6]{0:T(128)} %param.39) | copy-start | bytes 76
  1.6 9.5 %copy-start.13 = (f32[6]{0:T(128)S(1)}, f32[6]{0:T(128)}, u32[]{:S(2)}) copy-start(f32[6]{0:T(128)} %param.40) | copy-start | bytes 76
  1.6 10.2 %copy-start.11 = (f32[384]{0:T(512)S(1)}, f32[384]{0:T(512)}, u32[]{:S(2)}) copy-start(f32[384]{0:T(512)} %param.41) | copy-start | bytes 4612
  4.9 7.5 %copy-start.2 = (bf16[128,2432]{1,0:T(8,128)(2,1)}, bf16[128,2432]{1,0:T(8,128)(2,1)S(1)}, u32[]{:S(2)}) copy-start(bf16[128,2432]{1,0:T(8,128)(2,1)S(1)} %constant_dynamic-update-slice_fusion.refs_3_) | copy-start | bytes 1867780
  9.5 2.9 copy-start.7
  346.6 7.2 %copy-start.1 = (f32[128,3456]{1,0:T(8,128)S(1)}, f32[128,3456]{1,0:T(8,128)}, u32[]{:S(2)}) copy-start(f32[128,3456]{1,0:T(8,128)} %get-tuple-element.73) | copy-start | bytes 5308420
  354.9 10.1 %copy-start.6 = (bf16[4,32,1024]{2,1,0:T(8,128)(2,1)S(1)}, bf16[4,32,1024]{2,1,0:T(8,128)(2,1)}, u32[]{:S(2)}) copy-start(bf16[4,32,1024]{2,1,0:T(8,128)(2,1)} %get-tuple-element.155) | copy-start | bytes 786436
  362.1 3.6 copy-start.3
